TPU v7x, 32 devices: a whole 2x2x4 slice. The times are simulated.
32 devices in a mesh: img: 8 (over z, x), ha: 4 (over y, core).
Axes of the slice: x: 2, y: 2, z: 4, core: 2. Of those that a mesh axis runs over, the one named last changes fastest.
Arguments:
- inputs: bfloat16 [128, 28, 28, 1024], P('img', 'ha'), may hold values from -6 to 6
- image_count: int32 [8], P('img'), may hold values from 8 to 16, as said below
- pixel_mask: int32 [128, 28, 28], P('img', 'ha'), may hold values 0 or 1
- w_first: bfloat16 [1024, 256], replicated, may hold values from -0.1875 to 0.1875
- gain_first: float32 [256], replicated, may hold values from 0.25 to 1.75
- bias_first: float32 [256], replicated, may hold values from -1.5 to 1.5
- w_group: bfloat16 [2, 3, 3, 128, 256], replicated, may hold values from -0.1875 to 0.1875
- gain_group: float32 [512], replicated, may hold values from 0.25 to 1.75
- bias_group: float32 [512], replicated, may hold values from -1.5 to 1.5
- w_squeeze: bfloat16 [256, 128], replicated, may hold values from -0.75 to 0.75
- gain_squeeze: float32 [128], replicated, may hold values from 0.25 to 1.75
- bias_squeeze: float32 [128], replicated, may hold values from -1.5 to 1.5
- w_excite: bfloat16 [128, 512], replicated, may hold values from -1 to 1
- bias_excite: float32 [512], replicated, may hold values from -2.5 to 2.5
- w_last: bfloat16 [256, 1024], replicated, may hold values from -0.375 to 0.375
- gain_last: float32 [1024], replicated, may hold values from 0.25 to 1.75
- bias_last: float32 [1024], replicated, may hold values from -1.5 to 1.5
- cotangent: bfloat16 [128, 28, 28, 1024], P('img', 'ha'), may hold values from -6 to 6
Outputs:
- output: bfloat16 [128, 28, 28, 1024], P('img', 'ha')
- grad_inputs: bfloat16 [128, 28, 28, 1024], P('img', 'ha')
- grad_w_first: float32 [1024, 256], replicated
- grad_gain_first: float32 [256], replicated
- grad_bias_first: float32 [256], replicated
- grad_w_group: float32 [2, 3, 3, 128, 256], replicated
- grad_gain_group: float32 [512], replicated
- grad_bias_group: float32 [512], replicated
- grad_w_squeeze: float32 [256, 128], replicated
- grad_gain_squeeze: float32 [128], replicated
- grad_bias_squeeze: float32 [128], replicated
- grad_w_excite: float32 [128, 512], replicated
- grad_bias_excite: float32 [512], replicated
- grad_w_last: float32 [256, 1024], replicated
- grad_gain_last: float32 [1024], replicated
- grad_bias_last: float32 [1024], replicated
Inputs may be any that keep to these rules, and one draw needn't show every extreme that they name: `image_count`: some index of img has all 16 slots live and some has 8; live slots come first on every index.
All inputs are finite; a program needn't handle non-finite values. No bound on the sum of `pixel_mask` on one device may be relied on, other than what follows from the above.
Results may differ from a plain program's by a relative error of at most 0.012.
Values may be sent and summed in bfloat16 or wider, within the bound.
A program may use at most 192 MiB of HBM per device.

v0:
```python
import jax
import jax.numpy as jnp
from jax import lax
from jax.sharding import PartitionSpec as P

epsilon = 1e-05
highest = lax.Precision.HIGHEST


def extended(cells, sides, width):
    for axis, dim in sides:
        count = lax.axis_size(axis)
        ends = count - 1
        head = lax.slice_in_dim(cells, 0, width, axis=dim)
        tail = lax.slice_in_dim(cells, cells.shape[dim] - width, cells.shape[dim], axis=dim)
        cells = jnp.concatenate(
            [
                lax.ppermute(tail, axis, [(i, (i + 1) % count) for i in range(ends)]),
                cells,
                lax.ppermute(head, axis, [((i + 1) % count, i) for i in range(ends)]),
            ],
            axis=dim,
        )
    return cells


def silu_slope(values):
    sigma = jax.nn.sigmoid(values)
    return sigma * (1.0 + values * (1.0 - sigma))


def pixel_stats(values, weight):
    return lax.psum(
        (
            jnp.sum(values * weight, axis=0),
            jnp.sum(values * values * weight, axis=0),
            jnp.sum(weight),
        ),
        ("img", "ha"),
    )


def standardize(values, sums, squares, total):
    mean = sums / total
    spread = squares / total - mean * mean
    rscale = lax.rsqrt(spread + epsilon)
    return ((values - mean) * rscale, rscale)


def norm_back(grad_norm, centered, weight, gain, rscale, total):
    grad_bias, grad_gain = lax.psum(
        (jnp.sum(grad_norm, axis=0), jnp.sum(grad_norm * centered, axis=0)), ("img", "ha")
    )
    grad_values = gain * rscale * (grad_norm - weight * (grad_bias + centered * grad_gain) / total)
    return (grad_values, grad_gain, grad_bias)


def pad_columns(block):
    return jnp.pad(block, ((0, 0), (0, 0), (1, 1), (0, 0)))


def gather_taps(padded, starts, height_dev, columns, lower, upper):
    taps = [
        padded[:, row_tap : row_tap + height_dev, col_tap : col_tap + columns, lower:upper]
        for row_tap, col_tap in starts
    ]
    return jnp.concatenate(taps, axis=-1).reshape(-1, len(taps) * (upper - lower))


def transposed_conv(padded_grad, w_group, height_dev, columns):
    radix_count = w_group.shape[0]
    group_in = w_group.shape[3]
    mid_width = w_group.shape[4]
    backward_starts = [(2 - row_tap, 2 - col_tap) for row_tap in range(3) for col_tap in range(3)]
    grad_parts = []
    for branch in range(radix_count):
        grad_patch = gather_taps(
            padded_grad,
            backward_starts,
            height_dev,
            columns,
            branch * mid_width,
            (branch + 1) * mid_width,
        )
        flipped = jnp.transpose(w_group[branch].reshape(9, group_in, mid_width), (0, 2, 1)).reshape(
            9 * mid_width, group_in
        )
        grad_parts.append(jnp.dot(grad_patch, flipped, preferred_element_type=jnp.float32))
    return jnp.concatenate(grad_parts, axis=1)


def on_device(
    inputs,
    image_count,
    pixel_mask,
    w_first,
    gain_first,
    bias_first,
    w_group,
    gain_group,
    bias_group,
    w_squeeze,
    gain_squeeze,
    bias_squeeze,
    w_excite,
    bias_excite,
    w_last,
    gain_last,
    bias_last,
    cotangent,
):
    images_dev, height_dev, columns, in_channels = inputs.shape
    radix_count = w_group.shape[0]
    group_in = w_group.shape[3]
    mid_width = w_group.shape[4]
    area = height_dev * columns
    slots = lax.broadcasted_iota(jnp.int32, (images_dev,), 0)
    live = (slots < image_count[0]).astype(jnp.float32)
    live_col = live[:, None]
    valid = pixel_mask.astype(jnp.float32) * live[:, None, None]
    weight = valid.reshape(-1, 1)
    flat_in = inputs.reshape(-1, in_channels)
    squeeze_full = w_squeeze.astype(jnp.float32)
    excite_full = w_excite.astype(jnp.float32)
    y_first = jnp.dot(flat_in, w_first, preferred_element_type=jnp.float32)
    sums, squares, total = pixel_stats(y_first, weight)
    centered_first, rscale_first = standardize(y_first, sums, squares, total)
    norm_first = centered_first * gain_first + bias_first
    act_first = (jax.nn.silu(norm_first) * weight).astype(jnp.bfloat16)
    padded_first = pad_columns(
        extended(act_first.reshape(images_dev, height_dev, columns, mid_width), (("ha", 1),), 1)
    )
    forward_starts = [(row_tap, col_tap) for row_tap in range(3) for col_tap in range(3)]
    patch_list = [
        gather_taps(
            padded_first,
            forward_starts,
            height_dev,
            columns,
            branch * group_in,
            (branch + 1) * group_in,
        )
        for branch in range(radix_count)
    ]
    y_group = jnp.concatenate(
        [
            jnp.dot(
                patch_list[branch],
                w_group[branch].reshape(9 * group_in, mid_width),
                preferred_element_type=jnp.float32,
            )
            for branch in range(radix_count)
        ],
        axis=1,
    )
    sums, squares, total = pixel_stats(y_group, weight)
    centered_group, rscale_group = standardize(y_group, sums, squares, total)
    norm_group = centered_group * gain_group + bias_group
    act_group = jax.nn.silu(norm_group) * weight
    split_view = act_group.reshape(images_dev, area, radix_count, mid_width)
    local_pool = jnp.sum(jnp.sum(split_view, axis=2), axis=1)
    local_count = jnp.sum(valid.reshape(images_dev, area), axis=1)
    pool_total, pixel_count = lax.psum((local_pool, local_count), "ha")
    pixel_floor = jnp.maximum(pixel_count, 1.0)[:, None]
    pooled = pool_total / pixel_floor
    squeezed = jnp.dot(pooled, squeeze_full, precision=highest)
    fc_sum, fc_square, image_total = lax.psum(
        (
            jnp.sum(squeezed * live_col, axis=0),
            jnp.sum(squeezed * squeezed * live_col, axis=0),
            jnp.sum(live),
        ),
        "img",
    )
    centered_fc, rscale_fc = standardize(squeezed, fc_sum, fc_square, image_total)
    norm_fc = centered_fc * gain_squeeze + bias_squeeze
    hidden_fc = jax.nn.silu(norm_fc)
    logits = (jnp.dot(hidden_fc, excite_full, precision=highest) + bias_excite).reshape(
        images_dev, radix_count, mid_width
    )
    attention = jax.nn.softmax(logits, axis=1)
    mixed = (
        jnp.sum(split_view * attention[:, None], axis=2).reshape(-1, mid_width).astype(jnp.bfloat16)
    )
    y_last = jnp.dot(mixed, w_last, preferred_element_type=jnp.float32)
    sums, squares, total = pixel_stats(y_last, weight)
    centered_last, rscale_last = standardize(y_last, sums, squares, total)
    before = centered_last * gain_last + bias_last + flat_in.astype(jnp.float32)
    output = (jax.nn.silu(before) * weight).astype(jnp.bfloat16).reshape(inputs.shape)
    first_row = (lax.axis_index("ha") == 0).astype(jnp.float32)
    grad_before = (
        cotangent.reshape(-1, in_channels).astype(jnp.float32) * weight * silu_slope(before)
    )
    grad_y_last, grad_gain_last, grad_bias_last = norm_back(
        grad_before, centered_last, weight, gain_last, rscale_last, total
    )
    grad_y_last = grad_y_last.astype(jnp.bfloat16)
    grad_w_last = jnp.einsum("pc,pd->cd", mixed, grad_y_last, preferred_element_type=jnp.float32)
    grad_mixed = jnp.einsum(
        "pd,cd->pc", grad_y_last, w_last, preferred_element_type=jnp.float32
    ).reshape(images_dev, area, 1, mid_width)
    grad_attention = lax.psum(
        jnp.sum(grad_mixed * split_view, axis=1).astype(jnp.bfloat16), "ha"
    ).astype(jnp.float32)
    grad_logits = attention * (
        grad_attention - jnp.sum(attention * grad_attention, axis=1, keepdims=True)
    )
    grad_logits = grad_logits.reshape(images_dev, radix_count * mid_width)
    grad_w_excite = jnp.dot(hidden_fc.T, grad_logits, precision=highest)
    grad_bias_excite = jnp.sum(grad_logits, axis=0)
    grad_norm_fc = jnp.dot(grad_logits, excite_full.T, precision=highest) * silu_slope(norm_fc)
    grad_bias_squeeze, grad_gain_squeeze = lax.psum(
        (jnp.sum(grad_norm_fc, axis=0), jnp.sum(grad_norm_fc * centered_fc, axis=0)), "img"
    )
    grad_squeezed = (
        gain_squeeze
        * rscale_fc
        * (
            grad_norm_fc
            - live_col * (grad_bias_squeeze + centered_fc * grad_gain_squeeze) / image_total
        )
    )
    grad_w_squeeze = jnp.dot(pooled.T, grad_squeezed, precision=highest)
    grad_pooled = jnp.dot(grad_squeezed, squeeze_full.T, precision=highest) / pixel_floor
    grad_act_group = grad_mixed * attention[:, None] + grad_pooled[
        :, None, None, :
    ] * valid.reshape(images_dev, area, 1, 1)
    grad_norm_group = (
        grad_act_group.reshape(-1, radix_count * mid_width) * weight * silu_slope(norm_group)
    )
    grad_y_group, grad_gain_group, grad_bias_group = norm_back(
        grad_norm_group, centered_group, weight, gain_group, rscale_group, total
    )
    grad_y_group = grad_y_group.astype(jnp.bfloat16)
    grad_w_group = jnp.stack(
        [
            jnp.einsum(
                "pk,po->ko",
                patch_list[branch],
                grad_y_group[:, branch * mid_width : (branch + 1) * mid_width],
                preferred_element_type=jnp.float32,
            ).reshape(3, 3, group_in, mid_width)
            for branch in range(radix_count)
        ],
        axis=0,
    )
    grad_block = grad_y_group.reshape(images_dev, height_dev, columns, radix_count * mid_width)
    padded_grad = pad_columns(extended(grad_block, (("ha", 1),), 1))
    grad_act_first = transposed_conv(padded_grad, w_group, height_dev, columns)
    grad_norm_first = grad_act_first * weight * silu_slope(norm_first)
    grad_y_first, grad_gain_first, grad_bias_first = norm_back(
        grad_norm_first, centered_first, weight, gain_first, rscale_first, total
    )
    grad_y_first = grad_y_first.astype(jnp.bfloat16)
    grad_w_first = jnp.einsum(
        "pc,pd->cd", flat_in, grad_y_first, preferred_element_type=jnp.float32
    )
    grad_inputs = (
        (
            grad_before
            + jnp.einsum("pd,cd->pc", grad_y_first, w_first, preferred_element_type=jnp.float32)
        )
        .astype(jnp.bfloat16)
        .reshape(inputs.shape)
    )
    grad_w_first, grad_w_group, grad_w_last, grad_w_squeeze, grad_w_excite, grad_bias_excite = (
        lax.psum(
            (
                grad_w_first,
                grad_w_group,
                grad_w_last,
                grad_w_squeeze * first_row,
                grad_w_excite * first_row,
                grad_bias_excite * first_row,
            ),
            ("img", "ha"),
        )
    )
    return (
        output,
        grad_inputs,
        grad_w_first,
        grad_gain_first,
        grad_bias_first,
        grad_w_group,
        grad_gain_group,
        grad_bias_group,
        grad_w_squeeze,
        grad_gain_squeeze,
        grad_bias_squeeze,
        grad_w_excite,
        grad_bias_excite,
        grad_w_last,
        grad_gain_last,
        grad_bias_last,
    )


def solution(mesh):
    placed = (
        P("img", "ha", None, None),
        P("img"),
        P("img", "ha", None),
        P(),
        P(),
        P(),
        P(),
        P(),
        P(),
        P(),
        P(),
        P(),
        P(),
        P(),
        P(),
        P(),
        P(),
        P("img", "ha", None, None),
    )
    return jax.shard_map(
        on_device,
        mesh=mesh,
        in_specs=placed,
        out_specs=(
            P("img", "ha", None, None),
            P("img", "ha", None, None),
            P(),
            P(),
            P(),
            P(),
            P(),
            P(),
            P(),
            P(),
            P(),
            P(),
            P(),
            P(),
            P(),
            P(),
        ),
        check_vma=False,
    )
```

profile of v0, /device:TPU:0, one launch (start us, length us, event | category | flops | bytes accessed | tf_op | source)
XLA Modules:
  0.0 995.7 jit_solution(6116472910159602331)
XLA Ops:
  9.6 9.4 copy.63
  19.0 9.8 reshape.388
  28.8 6.5 multiply_reduce_fusion.9
  35.3 42.2 %all-reduce.7 = (f32[256]{0:T(256)S(1)}, f32[]{:T(128)}, f32[256]{0:T(256)S(1)}) all-reduce(f32[256]{0:T(256)S(1)} %get-tuple-element.73, f32[]{:T(128)} %get-tuple-element.77, f32[256]{0:T(256)S(1)} %get-tuple-element.72), channel_id=1, replica_groups=mesh['img'=8,'ha'=4] {'img','ha'}, use_global_device_ids=true, to_apply=%region_1.0 | all-reduce | flops 513 | bytes 4104 | tf_op jit(solution)/shard_map/psum | solution.py:33
  78.7 3.8 multiply_convert_fusion.5
  96.1 11.7 %copy.69 = f32[16,7,28,1024]{3,2,1,0:T(8,128)} copy(bf16[16,7,28,1024]{3,0,2,1:T(8,128)(2,1)} %param.35) | data formatting | bytes 19267584 | tf_op jit(solution)/shard_map/convert_element_type | solution.py:192
  107.9 14.3 %reshape.402 = f32[3136,1024]{1,0:T(8,128)} reshape(f32[16,7,28,1024]{3,2,1,0:T(8,128)} %copy.69) | data formatting | bytes 25690112 | tf_op jit(solution)/shard_map/convert_element_type | solution.py:192
  143.7 11.2 %reshape.390 = bf16[3136,1152]{1,0:T(8,128)(2,1)} reshape(bf16[16,7,28,1152]{3,2,1,0:T(8,128)(2,1)} %get-tuple-element.138) | data formatting | bytes 14450688 | tf_op jit(solution)/shard_map/reshape | solution.py:67
  154.9 7.1 fusion.51
  162.0 4.6 concatenate.56
  170.4 11.2 %reshape.391 = bf16[3136,1152]{1,0:T(8,128)(2,1)} reshape(bf16[16,7,28,1152]{3,2,1,0:T(8,128)(2,1)} %slice_dynamic-update-slice_fusion.14) | data formatting | bytes 14450688 | tf_op jit(solution)/shard_map/reshape | solution.py:67
  181.5 7.0 fusion.52
  188.5 4.6 concatenate.57
  193.1 5.3 multiply_reduce_fusion.7
  198.4 43.7 %all-reduce.6 = (f32[512]{0:T(512)S(1)}, f32[512]{0:T(512)S(1)}) all-reduce(f32[512]{0:T(512)S(1)} %get-tuple-element.69, f32[512]{0:T(512)S(1)} %get-tuple-element.68), channel_id=1, replica_groups=mesh['img'=8,'ha'=4] {'img','ha'}, use_global_device_ids=true, to_apply=%region_9.10 | all-reduce | flops 1024 | bytes 8192 | tf_op jit(solution)/shard_map/psum | solution.py:33
  243.3 8.3 concatenate.55
  251.7 15.0 %fusion.45 = (f32[16,256]{1,0:T(8,128)S(1)}, f32[16,196,2,256]{3,2,0,1:T(2,128)}) fusion(f32[16,196]{0,1:T(8,128)S(1)} %copy-done.24, f32[2,256]{1,0:T(2,128)S(1)} %add.276, f32[2,256]{1,0:T(2,128)S(1)} %mul.574, f32[2,256]{1,0:T(2,128)S(1)} %mul.571, f32[2,256]{1,0:T(2,128)S(1)} %sub.130, f32[16,196,2,256]{3,2,1,0:T(2,128)} %concatenate.55), kind=kLoop, calls=%fused_computation.156 | loop fusion | flops 16052224 | bytes 12882176 | tf_op jit(solution)/shard_map/reduce_sum | solution.py:161
  266.7 10.9 %all-reduce.11 = (f32[16,256]{1,0:T(8,128)S(1)}, f32[16]{0:T(128)S(1)}) all-reduce(f32[16,256]{1,0:T(8,128)S(1)} %get-tuple-element.121, f32[16]{0:T(128)S(1)} %get-tuple-element.76), channel_id=1, replica_groups=mesh['img'=8,'ha'=4] {'ha'}, use_global_device_ids=true, to_apply=%region_11.12 | all-reduce | flops 4112 | bytes 32896 | tf_op jit(solution)/shard_map/psum | solution.py:163
  277.8 21.1 %all-reduce.10 = (f32[128]{0:T(128)S(1)}, f32[]{:T(128)}, f32[128]{0:T(128)S(1)}) all-reduce(f32[128]{0:T(128)S(1)} %get-tuple-element.79, f32[]{:T(128)} %fusion.33, f32[128]{0:T(128)S(1)} %get-tuple-element.78), channel_id=1, replica_groups=mesh['img'=8,'ha'=4] {'img'}, use_global_device_ids=true, to_apply=%region_15.16 | all-reduce | flops 257 | bytes 2056 | tf_op jit(solution)/shard_map/psum | solution.py:167
  300.9 29.7 %multiply_reduce_fusion.5 = bf16[16,196,256]{2,0,1:T(8,128)(2,1)S(1)} fusion(f32[16,196,2,256]{3,2,0,1:T(2,128)} %get-tuple-element.122, f32[16,2,256]{2,1,0:T(2,128)S(1)} %fusion.28), kind=kLoop, calls=%fused_computation.31 | loop fusion | flops 2408448 | bytes 8060928 | tf_op jit(solution)/shard_map/reduce_sum | solution.py:183
  334.8 5.9 multiply_reduce_fusion.1
  340.7 37.1 %all-reduce.5 = (f32[1024]{0:T(1024)S(1)}, f32[1024]{0:T(1024)S(1)}) all-reduce(f32[1024]{0:T(1024)S(1)} %get-tuple-element.65, f32[1024]{0:T(1024)S(1)} %get-tuple-element.64), channel_id=1, replica_groups=mesh['img'=8,'ha'=4] {'img','ha'}, use_global_device_ids=true, to_apply=%region_24.25 | all-reduce | flops 2048 | bytes 16384 | tf_op jit(solution)/shard_map/psum | solution.py:33
  379.1 20.1 %fusion.36 = (f32[1024]{0:T(1024)S(1)}, f32[1024]{0:T(1024)S(1)}, f32[3136,1024]{1,0:T(8,128)}, bf16[3136,1024]{1,0:T(8,128)(2,1)}) fusion(f32[1024]{0:T(1024)S(1)} %add_rsqrt_fusion, f32[3136,1024]{1,0:T(8,128)} %get-tuple-element.157, f32[1024]{0:T(1024)S(1)} %get-tuple-element.119, bf16[3136,1024]{1,0:T(8,128)(2,1)} %reshape.388, ...), kind=kLoop, calls=%fused_computation.148 | loop fusion | flops 67434496 | bytes 51417344 | tf_op jit(solution)/shard_map/reduce_sum | solution.py:52
  399.3 42.4 %all-reduce.4 = (f32[1024]{0:T(1024)S(1)}, f32[1024]{0:T(1024)S(1)}) all-reduce(f32[1024]{0:T(1024)S(1)} %get-tuple-element.67, f32[1024]{0:T(1024)S(1)} %get-tuple-element.66), channel_id=1, replica_groups=mesh['img'=8,'ha'=4] {'img','ha'}, use_global_device_ids=true, to_apply=%region_30.31 | all-reduce | flops 2048 | bytes 16384 | tf_op jit(solution)/shard_map/psum | solution.py:51
  441.7 10.6 %multiply_convert_fusion = bf16[3136,1024]{1,0:T(8,128)(2,1)S(1)} fusion(f32[3136,1024]{1,0:T(8,128)} %get-tuple-element.120, f32[3136,1024]{1,0:T(8,128)} %get-tuple-element.157, f32[]{:T(128)} %get-tuple-element.94, f32[1024]{0:T(1024)S(1)} %get-tuple-element.175, f32[1024]{0:T(1024)S(1)} %get-tuple-element.176, f32[1024]{0:T(1024)S(1)} %get-tuple-element.118, ...), kind=kLoop, calls=%fused_computation.4 | loop fusion | flops 28901376 | bytes 32145668 | tf_op jit(solution)/shard_map/convert_element_type | solution.py:197
  455.0 3.6 fusion.53
  458.6 4.2 mul.619
  465.8 7.1 multiply_reduce_fusion.4
  472.9 10.2 %psum.209 = bf16[16,2,256]{2,1,0:T(2,128)(2,1)S(1)} all-reduce(bf16[16,2,256]{2,1,0:T(2,128)(2,1)S(1)} %multiply_reduce_fusion.4), channel_id=1, replica_groups=mesh['img'=8,'ha'=4] {'ha'}, use_global_device_ids=true, to_apply=%region_32.33 | all-reduce | flops 8192 | bytes 32768 | tf_op jit(solution)/shard_map/psum | solution.py:202
  485.7 20.7 %all-reduce.9 = (f32[128]{0:T(128)S(1)}, f32[128]{0:T(128)S(1)}) all-reduce(f32[128]{0:T(128)} %get-tuple-element.81, f32[128]{0:T(128)} %get-tuple-element.80), channel_id=1, replica_groups=mesh['img'=8,'ha'=4] {'img'}, use_global_device_ids=true, to_apply=%region_37.38 | all-reduce | flops 256 | bytes 2048 | tf_op jit(solution)/shard_map/psum | solution.py:212
  512.9 5.6 copy.73
  518.5 3.5 copy.74
  522.1 11.4 %copy.82 = bf16[1152,3136]{1,0:T(8,128)(2,1)} copy(bf16[1152,3136]{0,1:T(8,128)(2,1)} %bitcast.86) | data formatting | bytes 14450688 | tf_op jit(solution)/shard_map/pk,po->ko/dot_general | solution.py:237
  533.6 11.4 %copy.80 = bf16[1152,3136]{1,0:T(8,128)(2,1)} copy(bf16[1152,3136]{0,1:T(8,128)(2,1)} %bitcast.85) | data formatting | bytes 14450688 | tf_op jit(solution)/shard_map/pk,po->ko/dot_general | solution.py:237
  547.1 7.7 multiply_add_fusion
  554.8 7.7 copy.75
  562.5 3.7 copy.94
  567.2 5.7 fusion.37
  572.9 37.2 %all-reduce.3 = (f32[512]{0:T(512)S(1)}, f32[512]{0:T(512)S(1)}) all-reduce(f32[512]{0:T(512)S(1)} %get-tuple-element.71, f32[512]{0:T(512)S(1)} %get-tuple-element.70), channel_id=1, replica_groups=mesh['img'=8,'ha'=4] {'img','ha'}, use_global_device_ids=true, to_apply=%region_41.42 | all-reduce | flops 1024 | bytes 8192 | tf_op jit(solution)/shard_map/psum | solution.py:51
  610.1 6.4 multiply_convert_fusion.2
  616.6 6.3 fusion.24
  622.8 6.3 fusion.23
  629.1 4.6 mul.620
  633.7 9.2 mul.621
  642.9 4.6 add.299
  647.5 9.1 add.300
  656.7 10.1 %multiply_convert_fusion.3 = bf16[16,7,28,512]{3,0,2,1:T(8,128)(2,1)S(1)} fusion(f32[16,7,28,256]{3,0,2,1:T(8,128)} %copy.74, f32[16,7,28,256]{3,0,2,1:T(8,128)} %copy.73, f32[16,7,28,512]{3,0,2,1:T(8,128)} %add.300, f32[16,7,28,512]{3,0,2,1:T(8,128)} %mul.621, f32[]{:T(128)} %get-tuple-element.94, f32[512]{0:T(512)S(1)} %get-tuple-element.167, ...), kind=kLoop, calls=%fused_computation.25 | loop fusion | flops 36929536 | bytes 22538500 | tf_op jit(solution)/shard_map/convert_element_type | solution.py:234
  678.5 5.1 copy-done.13
  683.7 11.7 %copy.76 = bf16[16,7,28,2304]{3,2,1,0:T(8,128)(2,1)} copy(bf16[16,7,28,2304]{3,0,2,1:T(8,128)(2,1)S(1)} %get-tuple-element.126) | data formatting | bytes 28901376 | tf_op jit(solution)/shard_map/concatenate | solution.py:67
  695.4 21.0 %reshape.395 = bf16[3136,2304]{1,0:T(8,128)(2,1)} reshape(bf16[16,7,28,2304]{3,2,1,0:T(8,128)(2,1)} %copy.76) | data formatting | bytes 28901376 | tf_op jit(solution)/shard_map/reshape | solution.py:67
  721.5 16.2 %copy.78 = bf16[16,7,28,2304]{3,2,1,0:T(8,128)(2,1)} copy(bf16[16,7,28,2304]{3,0,2,1:T(8,128)(2,1)} %slice_dynamic-update-slice_fusion) | data formatting | bytes 28901376 | tf_op jit(solution)/shard_map/concatenate | solution.py:67
  737.7 21.1 %reshape.397 = bf16[3136,2304]{1,0:T(8,128)(2,1)} reshape(bf16[16,7,28,2304]{3,2,1,0:T(8,128)(2,1)} %copy.78) | data formatting | bytes 28901376 | tf_op jit(solution)/shard_map/reshape | solution.py:67
  758.8 7.4 fusion.54
  768.1 4.1 fusion.55
  772.3 3.6 fusion.38
  775.9 45.8 %all-reduce.2 = (f32[256]{0:T(256)S(1)}, f32[256]{0:T(256)S(1)}, f32[512]{0:T(512)}) all-reduce(f32[256]{0:T(256)S(1)} %get-tuple-element.75, f32[256]{0:T(256)S(1)} %get-tuple-element.74, f32[512]{0:T(512)S(1)} %bitcast.102), channel_id=1, replica_groups=mesh['img'=8,'ha'=4] {'img','ha'}, use_global_device_ids=true, to_apply=%region_45.46 | all-reduce | flops 1024 | bytes 8192 | tf_op jit(solution)/shard_map/psum | solution.py:51
  821.7 3.5 multiply_convert_fusion.4
  826.4 5.8 convolution_bitcast_fusion
  832.2 9.8 reshape.393
  842.0 10.2 %copy.84 = bf16[16,7,28,1024]{3,0,2,1:T(8,128)(2,1)} copy(bf16[16,7,28,1024]{3,2,1,0:T(8,128)(2,1)} %reshape.393) | data formatting | bytes 12845056
  852.2 9.6 add_convert_fusion
  861.7 10.1 %reshape.399 = bf16[16,7,28,1024]{3,2,1,0:T(8,128)(2,1)} reshape(bf16[3136,1024]{1,0:T(8,128)(2,1)} %add_convert_fusion) | data formatting | bytes 12845056 | tf_op jit(solution)/shard_map/reshape | solution.py:264
  871.8 10.1 %copy.85 = bf16[16,7,28,1024]{3,0,2,1:T(8,128)(2,1)} copy(bf16[16,7,28,1024]{3,2,1,0:T(8,128)(2,1)} %reshape.399) | data formatting | bytes 12845056
  882.0 98.3 %all-reduce.14.cloned.1.call-done = (f32[1024,256]{0,1:T(8,128)}, f32[2,3,3,128,256]{4,3,2,1,0:T(8,128)}, f32[256,128]{1,0:T(8,128)}, f32[128,512]{1,0:T(8,128)}, f32[256,1024]{1,0:T(8,128)}) async-done(((f32[1024,256]{0,1:T(8,128)}, f32[2,3,3,128,256]{4,3,2,1,0:T(8,128)}, f32[256,128]{1,0:T(8,128)}, f32[128,512]{1,0:T(8,128)}, f32[256,1024]{1,0:T(8,128)}), (f32[1024,256]{0,1:T(8,128)}, ...) | async-done | bytes 4849680 | tf_op jit(solution)/shard_map/psum | solution.py:267
  (253 shorter events, 96.6 us)
Async XLA Ops:
  7.2 327.5 %copy-start = (bf16[256,1024]{1,0:T(8,128)(2,1)S(1)}, bf16[256,1024]{1,0:T(8,128)(2,1)}, u32[]{:S(2)}) copy-start(bf16[256,1024]{1,0:T(8,128)(2,1)} %param.32) | copy-start | bytes 1572868
  7.2 973.1 %all-reduce.14.cloned.1.call-start = ((), (), s32[]{:S(2)}) async-start(), calls=%async_computation | async-start | bytes 9699328 | tf_op jit(solution)/shard_map/psum | solution.py:267
  7.9 269.6 %copy-start.69 = (f32[16]{0:T(128)}, f32[16]{0:T(128)S(1)}, u32[]{:S(2)}) copy-start(f32[16]{0:T(128)S(1)} %compare_convert_fusion) | copy-start | bytes 196
  19.0 9.8 copy-start.29
  28.8 48.7 %copy-start.56 = (f32[256]{0:T(256)S(1)}, f32[256]{0:T(256)}, u32[]{:S(2)}) copy-start(f32[256]{0:T(256)} %param.22) | copy-start | bytes 3076
  28.8 49.8 %copy-start.64 = (f32[256]{0:T(256)S(1)}, f32[256]{0:T(256)}, u32[]{:S(2)}) copy-start(f32[256]{0:T(256)} %param.23) | copy-start | bytes 3076
  35.3 54.7 %copy-start.44 = (f32[512]{0:T(512)S(1)}, f32[512]{0:T(512)}, u32[]{:S(2)}) copy-start(f32[512]{0:T(512)} %param.26) | copy-start | bytes 6148
  35.3 54.8 %copy-start.42 = (f32[512]{0:T(512)S(1)}, f32[512]{0:T(512)}, u32[]{:S(2)}) copy-start(f32[512]{0:T(512)} %param.25) | copy-start | bytes 6148
  78.7 9.9 copy-start.49
  78.7 9.9 copy-start.51
  84.9 37.3 %copy-start.6 = (bf16[16,7,28,256]{3,2,1,0:T(8,128)(2,1)}, bf16[16,7,28,256]{3,2,1,0:T(8,128)(2,1)S(1)}, u32[]{:S(2)}) copy-start(bf16[16,7,28,256]{3,2,1,0:T(8,128)(2,1)S(1)} %reshape.389) | copy-start | bytes 4816900
  85.8 36.4 %collective-permute-start = (bf16[16,1,28,256]{3,2,1,0:T(8,128)(2,1)}, bf16[16,1,28,256]{3,2,1,0:T(8,128)(2,1)S(1)}, u32[]{:S(2)}, u32[]{:S(2)}) collective-permute-start(bf16[16,1,28,256]{3,2,1,0:T(8,128)(2,1)} %get-tuple-element.150), channel_id=1, source_target_pairs={{0,1},{1,2},{2,3},{4,5},{5,6},{6,7},{8,9},{9,10},{10,11},{12,13},{... | collective-permute-start | bytes 688136 | tf_op jit(solution)/shard_map/ppermute | solution.py:18
  87.1 35.8 %collective-permute-start.1 = (bf16[16,1,28,256]{3,2,1,0:T(8,128)(2,1)}, bf16[16,1,28,256]{3,2,1,0:T(8,128)(2,1)}, u32[]{:S(2)}, u32[]{:S(2)}) collective-permute-start(bf16[16,1,28,256]{3,2,1,0:T(8,128)(2,1)} %get-tuple-element.151), channel_id=1, source_target_pairs={{1,0},{2,1},{3,2},{5,4},{6,5},{7,6},{9,8},{10,9},{11,10},{13,12},{... | collective-permute-start | bytes 688136 | tf_op jit(solution)/shard_map/ppermute | solution.py:20
  125.4 7.1 copy-start.7
  243.3 8.4 copy-start.38
  243.3 8.4 copy-start.40
  243.3 8.4 copy-start.24
  251.6 26.0 %copy-start.76 = (bf16[256,128]{1,0:T(8,128)(2,1)S(1)}, bf16[256,128]{1,0:T(8,128)(2,1)}, u32[]{:S(2)}) copy-start(bf16[256,128]{1,0:T(8,128)(2,1)} %param.27) | copy-start | bytes 196612
  251.7 47.3 %copy-start.58 = (f32[128]{0:T(128)S(1)}, f32[128]{0:T(128)}, u32[]{:S(2)}) copy-start(f32[128]{0:T(128)} %param.28) | copy-start | bytes 1540
  251.7 48.5 %copy-start.27 = (bf16[128,512]{1,0:T(8,128)(2,1)S(1)}, bf16[128,512]{1,0:T(8,128)(2,1)}, u32[]{:S(2)}) copy-start(bf16[128,512]{1,0:T(8,128)(2,1)} %param.30) | copy-start | bytes 393220
  251.7 48.5 %copy-start.61 = (f32[128]{0:T(128)S(1)}, f32[128]{0:T(128)}, u32[]{:S(2)}) copy-start(f32[128]{0:T(128)} %param.29) | copy-start | bytes 1540
  251.7 48.5 %copy-start.68 = (f32[512]{0:T(512)S(1)}, f32[512]{0:T(512)}, u32[]{:S(2)}) copy-start(f32[512]{0:T(512)} %param.31) | copy-start | bytes 6148
  277.6 22.6 %copy-start.48 = (f32[16,256]{1,0:T(8,128)}, f32[16,256]{1,0:T(8,128)S(1)}, u32[]{:S(2)}) copy-start(f32[16,256]{1,0:T(8,128)S(1)} %get-tuple-element.106) | copy-start | bytes 49156
  277.6 21.4 %copy-start.75 = (f32[16]{0:T(128)}, f32[16]{0:T(128)S(1)}, u32[]{:S(2)}) copy-start(f32[16]{0:T(128)S(1)} %broadcast_maximum_fusion) | copy-start | bytes 196
  300.2 34.5 %copy-start.53 = (f32[128]{0:T(128)}, f32[128]{0:T(128)S(1)}, u32[]{:S(2)}) copy-start(f32[128]{0:T(128)S(1)} %get-tuple-element.116) | copy-start | bytes 1540
  300.7 29.9 %copy-start.32 = (f32[16,512]{1,0:T(8,128)}, f32[16,512]{1,0:T(8,128)S(1)}, u32[]{:S(2)}) copy-start(f32[16,512]{1,0:T(8,128)S(1)} %convolution_add_fusion) | copy-start | bytes 98308
  300.8 33.9 %copy-start.35 = (f32[16,256]{1,0:T(8,128)}, f32[16,256]{1,0:T(8,128)S(1)}, u32[]{:S(2)}) copy-start(f32[16,256]{1,0:T(8,128)S(1)} %fusion.29) | copy-start | bytes 49156
  334.7 6.0 copy-start.16
  334.7 43.1 %copy-start.47 = (f32[1024]{0:T(1024)S(1)}, f32[1024]{0:T(1024)}, u32[]{:S(2)}) copy-start(f32[1024]{0:T(1024)} %param.33) | copy-start | bytes 12292
  334.8 44.4 %copy-start.62 = (f32[1024]{0:T(1024)S(1)}, f32[1024]{0:T(1024)}, u32[]{:S(2)}) copy-start(f32[1024]{0:T(1024)} %param.34) | copy-start | bytes 12292
  441.7 10.6 %copy-start.66 = (f32[1024]{0:T(1024)}, f32[1024]{0:T(1024)S(1)}, u32[]{:S(2)}) copy-start(f32[1024]{0:T(1024)S(1)} %get-tuple-element.175) | copy-start | bytes 12292
  441.7 10.7 %copy-start.67 = (f32[1024]{0:T(1024)}, f32[1024]{0:T(1024)S(1)}, u32[]{:S(2)}) copy-start(f32[1024]{0:T(1024)S(1)} %get-tuple-element.176) | copy-start | bytes 12292
  465.7 18.0 %copy-start.28 = (bf16[128,512]{1,0:T(8,128)(2,1)S(1)}, bf16[128,512]{1,0:T(8,128)(2,1)}, u32[]{:S(2)}) copy-start(bf16[128,512]{1,0:T(8,128)(2,1)} %param.30) | copy-start | bytes 393220
  465.8 18.0 %copy-start.54 = (f32[128]{0:T(128)S(1)}, f32[128]{0:T(128)}, u32[]{:S(2)}) copy-start(f32[128]{0:T(128)} %copy-done.53) | copy-start | bytes 1540
  506.4 12.1 %copy-start.14 = (f32[16,7,28,256]{3,2,1,0:T(8,128)S(1)}, f32[16,7,28,256]{3,2,1,0:T(8,128)}, u32[]{:S(2)}) copy-start(f32[16,7,28,256]{3,2,1,0:T(8,128)} %concatenate.57) | copy-start | bytes 9633796
  512.9 9.1 copy-start.36
  533.5 11.4 %copy-start.70 = (f32[2,256]{1,0:T(2,128)S(1)}, f32[2,256]{1,0:T(2,128)}, u32[]{:S(2)}) copy-start(f32[2,256]{1,0:T(2,128)} %get-tuple-element.159) | copy-start | bytes 6148
  562.4 4.7 copy-start.39
  562.5 4.7 copy-start.41
  567.2 42.9 %copy-start.46 = (f32[512]{0:T(512)S(1)}, f32[512]{0:T(512)}, u32[]{:S(2)}) copy-start(f32[512]{0:T(512)} %get-tuple-element.112) | copy-start | bytes 6148
  610.1 46.5 %copy-start.59 = (f32[512]{0:T(512)}, f32[512]{0:T(512)S(1)}, u32[]{:S(2)}) copy-start(f32[512]{0:T(512)S(1)} %get-tuple-element.167) | copy-start | bytes 6148
  610.1 46.5 %copy-start.60 = (f32[512]{0:T(512)}, f32[512]{0:T(512)S(1)}, u32[]{:S(2)}) copy-start(f32[512]{0:T(512)S(1)} %get-tuple-element.168) | copy-start | bytes 6148
  633.7 9.2 copy-start.10
  647.5 9.1 copy-start.33
  647.5 9.2 copy-start.31
  656.6 14.7 %slice-start = ((s8[6422528]{0:T(1024)(128)(4,1)}), s8[4194304]{0:T(1024)(128)(4,1)S(1)}, s32[]{:S(2)}) async-start(s8[6422528]{0:T(1024)(128)(4,1)} %bitcast.83), calls=%async_computation.1 | async-start | bytes 8388608
  656.7 13.0 %copy-start.20 = (f32[1,3,3,128,256]{4,3,2,1,0:T(8,128)S(1)}, f32[1,3,3,128,256]{4,3,2,1,0:T(8,128)}, u32[]{:S(2)}) copy-start(f32[1,3,3,128,256]{4,3,2,1,0:T(8,128)} %fusion.24) | copy-start | bytes 3538948
  656.7 13.0 %copy-start.21 = (f32[1,3,3,128,256]{4,3,2,1,0:T(8,128)S(1)}, f32[1,3,3,128,256]{4,3,2,1,0:T(8,128)}, u32[]{:S(2)}) copy-start(f32[1,3,3,128,256]{4,3,2,1,0:T(8,128)} %fusion.23) | copy-start | bytes 3538948
  656.7 14.6 %slice-start.1 = ((s8[6422528]{0:T(1024)(128)(4,1)}), s8[2228224]{0:T(1024)(128)(4,1)S(1)}, s32[]{:S(2)}) async-start(s8[6422528]{0:T(1024)(128)(4,1)} %bitcast.83), calls=%async_computation.2 | async-start | bytes 4456448
  666.9 7.3 collective-permute-start.2
  668.4 6.2 collective-permute-start.3
  678.5 5.1 copy-start.13
  737.7 21.1 %copy-start.26 = (bf16[1,3,3,128,256]{3,4,2,1,0:T(8,128)(2,1)S(1)}, bf16[1,3,3,128,256]{3,4,2,1,0:T(8,128)(2,1)}, u32[]{:S(2)}) copy-start(bf16[1,3,3,128,256]{3,4,2,1,0:T(8,128)(2,1)} %copy.77) | copy-start | bytes 1769476
  758.8 9.2 copy-start.15
  758.8 9.3 copy-start.25
  772.3 49.4 %copy-start.63 = (f32[256]{0:T(256)S(1)}, f32[256]{0:T(256)}, u32[]{:S(2)}) copy-start(f32[256]{0:T(256)} %get-tuple-element.108) | copy-start | bytes 3076
  821.7 10.5 %copy-start.71 = (f32[256]{0:T(256)}, f32[256]{0:T(256)S(1)}, u32[]{:S(2)}) copy-start(f32[256]{0:T(256)S(1)} %get-tuple-element.164) | copy-start | bytes 3076
  821.7 10.5 %copy-start.72 = (f32[256]{0:T(256)}, f32[256]{0:T(256)S(1)}, u32[]{:S(2)}) copy-start(f32[256]{0:T(256)S(1)} %get-tuple-element.165) | copy-start | bytes 3076
  842.0 10.2 %copy-start.12 = (bf16[3136,256]{1,0:T(8,128)(2,1)S(1)}, bf16[3136,256]{1,0:T(8,128)(2,1)}, u32[]{:S(2)}) copy-start(bf16[3136,256]{1,0:T(8,128)(2,1)} %copy-done.11) | copy-start | bytes 4816900
  842.0 10.2 %copy-start.30 = (bf16[1024,256]{1,0:T(8,128)(2,1)S(1)}, bf16[1024,256]{1,0:T(8,128)(2,1)}, u32[]{:S(2)}) copy-start(bf16[1024,256]{1,0:T(8,128)(2,1)} %param.21) | copy-start | bytes 1572868
  871.8 116.8 %copy-start.1 = (bf16[256,1024]{1,0:T(8,128)(2,1)S(1)}, bf16[256,1024]{1,0:T(8,128)(2,1)}, u32[]{:S(2)}) copy-start(bf16[256,1024]{1,0:T(8,128)(2,1)} %param.32) | copy-start | bytes 1572868
  980.3 5.9 copy-start.37
  980.3 6.6 copy-start.34
  980.3 7.3 copy-start.23
  (20 other events, 66.7 us)
Sparse Core Ops, SparseCore 0:
  832.3 147.9 all-reduce.13
where the time goes:
time: 1010 us; the launch traced here: 996 us
  local copies, waits for them, and re-layouts  338 us (33%)
  blocking collectives  311 us (31%)
  other arithmetic  145 us (14%)
  waiting for transfers between devices  98.7 us (10%)
  matrix products  81.2 us (8%)
  between operations  16 us (2%)
    psum x3, blocking collectives, norm_back(): lax.psum((jnp.sum(grad_norm, axis=0), jnp.sum(grad_norm * centered, axis=...  125 us
    psum x3, blocking collectives, pixel_stats(): lax.psum((jnp.sum(values * weight, axis=0), jnp.sum(values * values * wei...  123 us
    psum x1, waiting for transfers between devices, on_device(): lax.psum((grad_w_first, grad_w_group, grad_w_last, grad_w_squeeze * first...  98.3 us
    unnamed x191, local copies, waits for them, and re-layouts  76.5 us
    reshape x4, local copies, waits for them, and re-layouts, gather_taps(): jnp.concatenate(taps, axis=-1).reshape(-1, len(taps) * (upper - lower))  64.5 us
    concatenate x6, local copies, waits for them, and re-layouts, gather_taps(): jnp.concatenate(taps, axis=-1).reshape(-1, len(taps) * (upper - lower))  34.2 us
    reduce_sum x1, other arithmetic, on_device(): jnp.sum(split_view * attention[:, None], axis=2).reshape(-1, mid_width)  29.7 us
    reduce_sum x3, other arithmetic, norm_back(): jnp.sum(grad_norm, axis=0)  29.4 us
  transfers between devices with their start and end apart: 5, of which 2 were waited for; matrix products, arithmetic and copies ran while one was open for 9% of the time, Pallas kernels for 0%

commit v1 on v0

v1 whole, which is shorter than its diff:
```python
import functools

import jax
import jax.numpy as jnp
from jax import lax
from jax.experimental import pallas as pl
from jax.experimental.pallas import tpu as pltpu
from jax.sharding import PartitionSpec as P

EPS = 1e-05
F32 = jnp.float32
BF16 = jnp.bfloat16
HIGH = lax.Precision.HIGHEST
MESH = pl.DeviceIdType.MESH
LANES = 128


def dot(a, b, precision=None):
    return jnp.dot(a, b, preferred_element_type=F32, precision=precision)


def dot_nt(a, b, precision=None):
    return lax.dot_general(
        a, b, (((1,), (1,)), ((), ())), preferred_element_type=F32, precision=precision
    )


def dot_tn(a, b, precision=None):
    return lax.dot_general(
        a, b, (((0,), (0,)), ((), ())), preferred_element_type=F32, precision=precision
    )


def wide(cell, lanes):
    return jnp.concatenate([cell] * (lanes // LANES), axis=1)


def fold(cells):
    rows, lanes = cells.shape
    return jnp.sum(cells.reshape(rows // 8, 8, lanes), axis=0)


def fold_images(cells, images):
    rows, lanes = cells.shape
    return jnp.sum(cells.reshape(rows // images, images, lanes), axis=0)


def total_row(cells):
    return jnp.sum(cells, axis=0, keepdims=True)


def put(ref, at, row, vector):
    for j in range(vector.shape[1] // LANES):
        ref[at, row + j : row + j + 1, :] = vector[:, j * LANES : (j + 1) * LANES]


def get(cells, row, lanes):
    return jnp.concatenate(
        [cells[row + j : row + j + 1, :] for j in range(lanes // LANES)], axis=1
    )


def moments(sums, squares, total):
    mean = sums / total
    spread = squares / total - mean * mean
    return mean, lax.rsqrt(spread + EPS)


def gate(half):
    bend = jnp.tanh(half)
    rise = 1.0 + bend
    return half * rise, 0.5 * (rise + half * (1.0 - bend * bend))


def split_bf16(cells):
    high = cells.astype(BF16)
    return high, (cells - high.astype(F32)).astype(BF16)


class Dims:
    def __init__(self, n_img, n_ha, inputs, w_group, w_squeeze):
        self.n_img, self.n_ha = n_img, n_ha
        self.nb, self.nh, self.nw, self.cin = inputs
        self.radix, _, _, self.gin, self.width = w_group
        self.mid = self.radix * self.gin
        self.wide = self.radix * self.width
        self.inter = w_squeeze[1]
        self.line = self.nw * self.nb
        self.rows = self.nh * self.line
        self.padded = (self.nw + 2) * self.nb
        self.half = (
            self.cin // 2,
            9 * self.gin + self.width,
            self.cin // 2,
        )
        self.inside = n_img == 8 and n_ha == 4


def block_kernel(
    d,
    x_hbm, ct_hbm, m, live, w1, g1, c1, w2, g2, c2, wsq, gs, cs, wex, bex, w3, g3, c3,
    out_hbm, dn_hbm, dy_hbm, wg0_hbm, wg1_hbm, wg2_hbm, small,
    xv, ctv, y1, a1p, y2, act2, slope2, mixed, y3, ostage, dm, acc_c, acc_g, w3p, w2t,
    att, q2, q4, vecs, pools,
    part0, part1, part2, rc0, rc1, rc2, rxy0, rxy1, rxy2, rz0, rz1, rz2, p0, p1, p2, res0, res1, res2,
    sa, si, ba, bi, ga_src, ga_buf, pf_src, pf_buf,
    sem_x, sem_ct, sem_out, sem_dn, sem_misc, ssa, rsa, ssi, rsi, ssh, rsh, ssw, rsw,
):
    n_img, n_ha = d.n_img, d.n_ha
    nb, nh, nw = d.nb, d.nh, d.nw
    cin, mid, wd, wide2, line, rows = d.cin, d.mid, d.width, d.wide, d.line, d.rows
    gin = d.gin
    dyp = ctv
    half = cin // 2
    i = lax.axis_index("img")
    h = lax.axis_index("ha")

    def ha_peer(k):
        return (i, lax.rem(h + k, n_ha))

    def img_peer(k):
        return (lax.rem(i + k, n_img), h)

    z_of, x_of, y_of, core = i // 2, lax.rem(i, 2), h // 2, lax.rem(h, 2)
    spot = x_of * 2 + y_of

    def core_peer():
        return (i, y_of * 2 + (1 - core))

    def plane_peer(k):
        other = lax.rem(spot + k, 4)
        return (z_of * 2 + other // 2, lax.rem(other, 2) * 2 + core)

    def z_peer(k):
        return (lax.rem(z_of + k, 4) * 2 + x_of, h)

    def line_rows(t):
        return pl.ds(pl.multiple_of(t * line, line), line)

    def x_copy(t):
        return pltpu.make_async_copy(x_hbm.at[line_rows(t)], xv.at[line_rows(t)], sem_x.at[t])

    def half_rows(t, c):
        return pl.ds(pl.multiple_of(c * rows + t * line, nb), line)

    def ct_copy(t, c):
        return pltpu.make_async_copy(
            ct_hbm.at[line_rows(t), pl.ds(c * half, half)], ctv.at[half_rows(t, c)], sem_ct.at[c, t]
        )

    def start_inputs(t, carry):
        x_copy(t).start()
        return carry

    lax.fori_loop(0, nh, start_inputs, 0)

    barrier = pltpu.get_barrier_semaphore()
    peers = [ha_peer(k) for k in range(1, n_ha)] + [img_peer(k) for k in range(1, n_img)]
    if d.inside:
        peers.append(((z_of * 2 + (1 - x_of)), (1 - y_of) * 2 + core))
    for peer in peers:
        pl.semaphore_signal(barrier, inc=1, device_id=peer, device_id_type=MESH)

    padded = d.padded

    def inner_rows(t, at=nb, count=line):
        return pl.ds(pl.multiple_of(t * padded + at, nb), count)

    def clear(ref):
        zero = jnp.zeros((nb, ref.shape[1]), BF16)

        def body(t, carry):
            ref[inner_rows(t, 0, nb), :] = zero
            ref[inner_rows(t, nb + line, nb), :] = zero
            return carry

        lax.fori_loop(0, nh + 2, body, 0)

        def edge(t, carry):
            ref[inner_rows(0, t * nb, nb), :] = zero
            ref[inner_rows(nh + 1, t * nb, nb), :] = zero
            return carry

        lax.fori_loop(0, nw + 2, edge, 0)

    clear(a1p)
    pl.semaphore_wait(barrier, len(peers))

    def swap(src, buf, send, recv, peer, n):
        def copy(k):
            return pltpu.make_async_remote_copy(
                src_ref=src,
                dst_ref=buf.at[k],
                send_sem=send.at[k],
                recv_sem=recv.at[k],
                device_id=peer(k),
                device_id_type=MESH,
            )

        def start(k, carry):
            copy(k).start()
            return carry

        def sent(k, carry):
            copy(k).wait_send()
            return carry

        def take(k, carry):
            copy(k).wait_recv()
            return carry + buf[k].astype(F32)

        if n <= 8:
            for k in range(1, n):
                start(k, 0)
            total = src[...].astype(F32)
            for k in range(1, n):
                total = take(k, total)
            for k in range(1, n):
                sent(k, 0)
            return total
        lax.fori_loop(1, n, start, 0)
        total = lax.fori_loop(1, n, take, src[...].astype(F32))
        lax.fori_loop(1, n, sent, 0)
        return total

    def sum_ha(at, count):
        span = pl.ds(0, count)
        return swap(
            sa.at[at, span], ba.at[at, :, span], ssa.at[at], rsa.at[at], ha_peer, n_ha
        )

    def sum_img(at, count):
        span = pl.ds(0, count)
        return swap(
            si.at[at, span], bi.at[at, :, span], ssi.at[at], rsi.at[at], img_peer, n_img
        )

    def sum_all(at, count):
        si[at, 0:count, :] = sum_ha(at, count)
        return sum_img(at, count)

    def halo(ref, at):
        def down():
            return pltpu.make_async_remote_copy(
                src_ref=ref.at[inner_rows(nh)], dst_ref=ref.at[inner_rows(0)],
                send_sem=ssh.at[at, 0], recv_sem=rsh.at[at, 0],
                device_id=(i, jnp.minimum(h + 1, n_ha - 1)), device_id_type=MESH,
            )

        def up():
            return pltpu.make_async_remote_copy(
                src_ref=ref.at[inner_rows(1)], dst_ref=ref.at[inner_rows(nh + 1)],
                send_sem=ssh.at[at, 1], recv_sem=rsh.at[at, 1],
                device_id=(i, jnp.maximum(h - 1, 0)), device_id_type=MESH,
            )

        def start():
            @pl.when(h < n_ha - 1)
            def _():
                down().start()

            @pl.when(h > 0)
            def _():
                up().start()

        def wait_recv():
            @pl.when(h > 0)
            def _():
                down().wait_recv()

            @pl.when(h < n_ha - 1)
            def _():
                up().wait_recv()

        def wait_send():
            @pl.when(h < n_ha - 1)
            def _():
                down().wait_send()

            @pl.when(h > 0)
            def _():
                up().wait_send()

        return start, wait_recv, wait_send

    parts, rcs, rxys, rzs, mids = (
        (part0, part1, part2), (rc0, rc1, rc2), (rxy0, rxy1, rxy2), (rz0, rz1, rz2), (p0, p1, p2),
    )
    ress = (res0, res1, res2)
    plane_rows, z_rows = wd // 4, wd // 16

    def w_copy(s, stage, k):
        sem = (s, stage * 4 + k)
        part, res, inner = parts[s], ress[s], mids[s]
        own_plane = pl.ds(pl.multiple_of(spot * plane_rows, plane_rows), plane_rows)
        own_rows = pl.ds(pl.multiple_of(spot * plane_rows + z_of * z_rows, z_rows), z_rows)
        if stage == 0:
            src, dst, peer = part.at[1 - core], rcs[s], core_peer()
        elif stage == 1:
            other = lax.rem(spot + k, 4)
            src = part.at[core, pl.ds(pl.multiple_of(other * plane_rows, plane_rows), plane_rows)]
            dst, peer = rxys[s].at[k - 1], plane_peer(k)
        elif stage == 2:
            other = lax.rem(z_of + k, 4)
            src = inner.at[pl.ds(pl.multiple_of(other * z_rows, z_rows), z_rows)]
            dst, peer = rzs[s].at[k - 1], z_peer(k)
        elif stage == 3:
            src = dst = res.at[core, own_rows]
            peer = z_peer(k)
        elif stage == 4:
            src = dst = res.at[core, own_plane]
            peer = plane_peer(k)
        else:
            src = dst = res.at[core]
            peer = core_peer()
        return pltpu.make_async_remote_copy(
            src_ref=src, dst_ref=dst, send_sem=ssw.at[sem], recv_sem=rsw.at[sem], device_id=peer, device_id_type=MESH
        )

    def w_ks(stage):
        return (1,) if stage in (0, 5) else (1, 2, 3)

    def w_arrival(s, stage, k):
        res = ress[s]
        sem = (s, stage * 4 + k)
        if stage == 3:
            other = lax.rem(z_of - k + 4, 4)
            dst = res.at[core, pl.ds(pl.multiple_of(spot * plane_rows + other * z_rows, z_rows), z_rows)]
        elif stage == 4:
            other = lax.rem(spot - k + 4, 4)
            dst = res.at[core, pl.ds(pl.multiple_of(other * plane_rows, plane_rows), plane_rows)]
        else:
            dst = res.at[1 - core]
        return pltpu.make_async_remote_copy(
            src_ref=dst, dst_ref=dst, send_sem=ssw.at[sem], recv_sem=rsw.at[sem], device_id=core_peer(), device_id_type=MESH
        )

    def w_start(s, stage):
        if d.inside:
            for k in w_ks(stage):
                w_copy(s, stage, k).start()

    def w_finish(s, stage):
        if not d.inside:
            return
        for k in w_ks(stage):
            if stage <= 2:
                w_copy(s, stage, k).wait_recv()
            else:
                w_arrival(s, stage, k).wait_recv()
        part, res, inner = parts[s], ress[s], mids[s]
        if stage == 0:
            rc = rcs[s]

            def add(t, carry):
                at = pl.ds(pl.multiple_of(t * 16, 16), 16)
                part[core, at, :] = (part[core, at, :].astype(F32) + rc[at, :].astype(F32)).astype(BF16)
                return carry

            lax.fori_loop(0, wd // 16, add, 0)
        elif stage == 1:
            buf = rxys[s]

            def add(t, carry):
                at = pl.ds(pl.multiple_of(t * 16, 16), 16)
                own = pl.ds(pl.multiple_of(spot * plane_rows + t * 16, 16), 16)
                total = part[core, own, :].astype(F32)
                for k in range(3):
                    total = total + buf[k, at, :].astype(F32)
                inner[at, :] = total.astype(BF16)
                return carry

            lax.fori_loop(0, plane_rows // 16, add, 0)
        elif stage == 2:
            buf = rzs[s]
            total = inner[pl.ds(pl.multiple_of(z_of * z_rows, z_rows), z_rows), :].astype(F32)
            for k in range(3):
                total = total + buf[k].astype(F32)
            res[core, pl.ds(pl.multiple_of(spot * plane_rows + z_of * z_rows, z_rows), z_rows), :] = total.astype(BF16)

    def w_step(s, stage):
        w_finish(s, stage)
        if stage < 5:
            w_start(s, stage + 1)

    def w_sent(s):
        if d.inside:
            for stage in range(6):
                for k in w_ks(stage):
                    w_copy(s, stage, k).wait_send()

    def first(t, carry):
        sums, squares = carry
        x_copy(t).wait()
        ct_copy(t, 0).start()
        ct_copy(t, 1).start()
        at = line_rows(t)
        y = dot(xv[at, :], w1[...])
        y1[at, :] = y
        masked = y * wide(m[at, :], mid)
        return sums + fold(masked), squares + fold(masked * y)

    zeros = jnp.zeros((8, mid), F32)
    sums, squares = lax.fori_loop(0, nh, first, (zeros, zeros))

    def count_pixels(t, carry):
        return carry + fold_images(m[line_rows(t), :], nb)

    pixels = lax.fori_loop(0, nh, count_pixels, jnp.zeros((nb, LANES), F32))
    sa[0, 0:8, :] = jnp.zeros((8, LANES), F32)
    put(sa, 0, 0, total_row(sums))
    put(sa, 0, 2, total_row(squares))
    put(sa, 0, 4, total_row(pixels))
    put(sa, 0, 5, total_row(live[...]) * (1.0 / n_ha))
    got = sum_all(0, 8)
    total = got[4:5, :]
    images = got[5:6, :]
    mean1, scale1 = moments(get(got, 0, mid), get(got, 2, mid), wide(total, mid))
    half_a1 = 0.5 * g1[...] * scale1
    half_b1 = 0.5 * c1[...] - half_a1 * mean1

    step1 = 4 * nb

    def act_first(t, carry):
        def cells(u, carry):
            at = pl.ds(pl.multiple_of(t * line + u * step1, step1), step1)
            value, _ = gate(y1[at, :] * half_a1 + half_b1)
            value = value * wide(m[at, :], mid)
            a1p[inner_rows(t + 1, nb + u * step1, step1), :] = value.astype(BF16)
            return carry + fold(value)

        return lax.fori_loop(0, line // step1, cells, carry)

    sum_act1 = total_row(lax.fori_loop(0, nh, act_first, jnp.zeros((8, mid), F32)))
    halo1_start, halo1_recv, halo1_sent = halo(a1p, 0)
    halo1_start()

    def taps(t, r):
        return jnp.concatenate(
            [
                a1p[inner_rows(t + ky, kx * nb), r * gin : (r + 1) * gin]
                for ky in range(3)
                for kx in range(3)
            ],
            axis=1,
        )

    def group(t, carry):
        at = line_rows(t)
        done = []
        for r in range(d.radix):
            sums, squares = carry[r]
            y = dot(taps(t, r), w2[r])
            y2[at, r * wd : (r + 1) * wd] = y
            masked = y * wide(m[at, :], wd)
            done.append((sums + fold(masked), squares + fold(masked * y)))
        return tuple(done)

    zeros = jnp.zeros((8, wd), F32)
    sums2 = lax.fori_loop(1, nh - 1, group, ((zeros, zeros),) * d.radix)
    halo1_recv()
    sums2 = lax.fori_loop(0, 2, lambda t, carry: group(t * (nh - 1), carry), sums2)
    put(sa, 1, 0, jnp.concatenate([total_row(s) for s, _ in sums2], axis=1))
    put(sa, 1, 4, jnp.concatenate([total_row(q) for _, q in sums2], axis=1))
    got = sum_all(1, 8)
    mean2, scale2 = moments(get(got, 0, wide2), get(got, 4, wide2), wide(total, wide2))
    half_a2 = 0.5 * g2[...] * scale2
    half_b2 = 0.5 * c2[...] - half_a2 * mean2

    lane_blocks = wd // LANES
    step2 = 4 * nb
    for r in range(d.radix):
        for j in range(lane_blocks):
            col = r * wd + j * LANES
            lanes = slice(col, col + LANES)
            ha2, hb2 = half_a2[:, lanes], half_b2[:, lanes]

            def act_group(t, carry):
                pool, slopes, bends = carry
                at = pl.ds(pl.multiple_of(t * step2, step2), step2)
                y = y2[at, lanes]
                mask = m[at, :]
                value, slope = gate(y * ha2 + hb2)
                value = value * mask
                slope = slope * mask
                act2[at, lanes] = value.astype(BF16)
                slope2[at, lanes] = slope.astype(BF16)
                return (
                    pool + fold_images(value, nb),
                    slopes + fold_images(slope, nb),
                    bends + fold_images(slope * y, nb),
                )

            zero = jnp.zeros((nb, LANES), F32)
            pool, slopes, bends = lax.fori_loop(0, rows // step2, act_group, (zero, zero, zero))
            q2[:, lanes] = slopes
            q4[:, lanes] = bends
            at = slice(j * LANES, (j + 1) * LANES)
            if r == 0:
                pools[:, at] = pool
            else:
                pools[:, at] = pools[:, at] + pool

    pool = pools[...]
    squeeze = wsq[...].astype(F32)
    excite = wex[...].astype(F32)
    pf_src[:, 0 : d.inter] = dot(pool, squeeze, HIGH)
    pf_src[:, d.inter :] = pixels
    both = swap(pf_src, pf_buf, ssa.at[8], rsa.at[8], ha_peer, n_ha)
    floor = jnp.maximum(both[:, d.inter :], 1.0)
    squeezed = both[:, 0 : d.inter] / floor
    live_now = live[...]
    si[2, 0:8, :] = jnp.zeros((8, LANES), F32)
    put(si, 2, 0, total_row(squeezed * live_now))
    put(si, 2, 1, total_row(squeezed * squeezed * live_now))
    got = sum_img(2, 8)
    mean_s, scale_s = moments(got[0:1, :], got[1:2, :], images)
    centered = (squeezed - mean_s) * scale_s
    hidden, hidden_slope = gate(0.5 * (centered * gs[...] + cs[...]))
    logits = dot(hidden, excite, HIGH) + bex[...]
    gap = logits[:, 0:wd] - logits[:, wd:]
    att[:, 0:wd] = jax.nn.sigmoid(gap)
    att[:, wd:] = jax.nn.sigmoid(-gap)

    step3 = 2 * nb

    def mix(t, carry):
        def cells(u, carry):
            at = pl.ds(pl.multiple_of(t * line + u * step3, step3), step3)
            weight = att[...]
            weight = jnp.concatenate([weight] * (step3 // nb), axis=0)
            both = act2[at, :].astype(F32) * weight
            mixed[at, :] = (both[:, 0:wd] + both[:, wd:]).astype(BF16)
            return carry

        lax.fori_loop(0, line // step3, cells, 0)
        gram, sums = carry
        cells = mixed[line_rows(t), :]
        return gram + dot_tn(cells, cells), sums + fold(cells.astype(F32))

    gram, sums = lax.fori_loop(
        0, nh, mix, (jnp.zeros((wd, wd), F32), jnp.zeros((8, wd), F32))
    )
    mix_sum = total_row(sums)
    gram_high, gram_low = split_bf16(gram)
    acc_g[0, :, 0:cin] = dot(gram_high, w3[...]) + dot(gram_low, w3[...])
    mix_high, mix_low = split_bf16(mix_sum)
    sum_last = dot(jnp.broadcast_to(mix_high, (16, wd)), w3[...]) + dot(
        jnp.broadcast_to(mix_low, (16, wd)), w3[...]
    )
    put(sa, 3, 0, sum_last[0:1, :])
    put(sa, 3, 8, total_row(acc_g[0, :, 0:cin] * w3[...].astype(F32)))
    got = sum_all(3, 16)
    mean3, scale3 = moments(get(got, 0, cin), get(got, 8, cin), wide(total, cin))
    grow3 = g3[...] * scale3
    half_a3 = 0.5 * grow3
    half_b3 = 0.5 * c3[...] - half_a3 * mean3
    w3p[...] = (w3[...].astype(F32) * grow3).astype(BF16)

    step4 = 4 * nb
    blocks4 = 2 * LANES

    def out_copy(t):
        return pltpu.make_async_copy(ostage.at[lax.rem(t, 2)], out_hbm.at[line_rows(t)], sem_out.at[t])

    def dn_copy(t, c):
        return pltpu.make_async_copy(
            ctv.at[half_rows(t, c)], dn_hbm.at[line_rows(t), pl.ds(c * half, half)], sem_dn.at[c, t]
        )

    acc_c[...] = jnp.zeros((wd, cin), F32)
    vecs[...] = jnp.zeros((8, cin), F32)

    def last(t, carry):
        at_line = line_rows(t)
        y3[...] = dot(mixed[at_line, :], w3[...])
        ct_copy(t, 0).wait()
        ct_copy(t, 1).wait()

        @pl.when(t >= 2)
        def _():
            out_copy(t - 2).wait()

        slot = lax.rem(t, 2)
        for j in range(cin // blocks4):
            lanes = slice(j * blocks4, (j + 1) * blocks4)
            a3, b3 = half_a3[:, lanes], half_b3[:, lanes]

            def cells(u, carry):
                own = pl.ds(pl.multiple_of(u * step4, step4), step4)
                at = pl.ds(pl.multiple_of(t * line + u * step4, step4), step4)
                value, slope = gate(y3[own, lanes] * a3 + (b3 + 0.5 * xv[at, lanes].astype(F32)))
                mask = wide(m[at, :], blocks4)
                ostage[slot, own, lanes] = (value * mask).astype(BF16)
                side = j * blocks4 // half
                there = pl.ds(pl.multiple_of(side * rows + t * line + u * step4, nb), step4)
                inner = slice(j * blocks4 - side * half, (j + 1) * blocks4 - side * half)
                grad = ctv[there, inner].astype(F32) * mask * slope
                ctv[there, inner] = grad.astype(BF16)
                return carry + fold(grad)

            vecs[:, lanes] = lax.fori_loop(0, line // step4, cells, vecs[:, lanes])
        out_copy(t).start()
        dn_copy(t, 0).start()
        dn_copy(t, 1).start()
        grad = jnp.concatenate([ctv[half_rows(t, 0), :], ctv[half_rows(t, 1), :]], axis=1)
        dm[at_line, :] = dot_nt(grad, w3p[...])
        acc_c[...] += dot_tn(mixed[at_line, :], grad)
        return carry

    lax.fori_loop(0, nh, last, 0)
    sum_grad = total_row(vecs[...])
    put(sa, 4, 0, sum_grad)
    put(sa, 4, 8, scale3 * (total_row(acc_c[...] * w3[...].astype(F32)) - mean3 * sum_grad))
    got = sum_all(4, 16)
    bias3, gain3 = get(got, 0, cin), get(got, 8, cin)
    put(small, 0, 0, bias3)
    put(small, 0, 8, gain3)
    all_wide = wide(total, cin)
    slant3 = scale3 * gain3 / all_wide
    level3 = bias3 / all_wide - mean3 * slant3
    fix = (w3[...].astype(F32) * slant3).astype(BF16)
    fix = dot_nt(fix, w3p[...]).astype(BF16)
    level_high, level_low = split_bf16(level3)
    shift = dot_nt(jnp.broadcast_to(level_high, (16, cin)), w3p[...]) + dot_nt(
        jnp.broadcast_to(level_low, (16, cin)), w3p[...]
    )
    shift = shift[0:1, :]
    mix_column = jnp.transpose(jnp.broadcast_to(mix_sum, (LANES, wd)))
    for j in range(cin // LANES):
        lanes = slice(j * LANES, (j + 1) * LANES)
        to = j * LANES - (0 if j * LANES < cin // 2 else cin // 2)
        grad = grow3[:, lanes] * (
            acc_c[:, lanes]
            - mix_column * level3[:, lanes]
            - acc_g[0, :, lanes] * slant3[:, lanes]
        )
        part2[0 if j * LANES < cin // 2 else 1, :, to : to + LANES] = grad.astype(BF16)
    w_start(2, 0)

    def back_mix(t, carry):
        at = line_rows(t)
        mask = wide(m[at, :], wd)
        dm[at, :] = dm[at, :] - dot(mixed[at, :], fix) - mask * shift
        return carry

    lax.fori_loop(0, nh, back_mix, 0)
    w_step(2, 0)
    step5 = 4 * nb
    sums5 = []
    for j in range(lane_blocks):
        lanes = slice(j * LANES, (j + 1) * LANES)

        def image_sums(t, carry):
            at = pl.ds(pl.multiple_of(t * step5, step5), step5)
            grad = dm[at, lanes]
            done = []
            for r in range(d.radix):
                own = slice(r * wd + j * LANES, r * wd + (j + 1) * LANES)
                a, b, c = carry[r]
                a = a + fold_images(grad * act2[at, own].astype(F32), nb)
                part = grad * slope2[at, own].astype(F32)
                b = b + fold_images(part, nb)
                c = c + fold_images(part * y2[at, own], nb)
                done.append((a, b, c))
            return tuple(done)

        zero = jnp.zeros((nb, LANES), F32)
        sums5.append(
            lax.fori_loop(0, rows // step5, image_sums, ((zero, zero, zero),) * d.radix)
        )
    pick = lambda which: jnp.concatenate(
        [sums5[j][r][which] for r in range(d.radix) for j in range(lane_blocks)], axis=1
    )
    def dn_out(t, carry):
        dn_copy(t, 0).wait()
        dn_copy(t, 1).wait()
        return carry

    lax.fori_loop(0, nh, dn_out, 0)
    clear(dyp)
    ga_src[...] = pick(0).astype(BF16)
    q1, q3 = pick(1), pick(2)
    w_step(2, 1)
    grad_att = swap(ga_src, ga_buf, ssa.at[9], rsa.at[9], ha_peer, n_ha)
    w_step(2, 2)

    weight = att[...]
    weighed = weight * grad_att
    both = weighed[:, 0:wd] + weighed[:, wd:]
    grad_logits = weight * (grad_att - jnp.concatenate([both, both], axis=1))
    grad_excite = dot_tn(hidden, grad_logits, HIGH)
    grad_bex = total_row(grad_logits) * (1.0 / n_ha)
    grad_fc = dot_nt(grad_logits, excite, HIGH) * hidden_slope
    si[5, 0:8, :] = jnp.zeros((8, LANES), F32)
    put(si, 5, 0, total_row(grad_fc))
    put(si, 5, 1, total_row(grad_fc * centered))
    pooled = pool / wide(floor, wd)
    put(si, 5, 2, total_row(pooled))
    got = sum_img(5, 8)
    bias_s, gain_s = got[0:1, :], got[1:2, :]
    w_step(2, 3)
    put(small, 0, 16, bias_s)
    put(small, 0, 17, gain_s)
    grad_squeezed = (gs[...] * scale_s) * (
        grad_fc - live_now * (bias_s + centered * gain_s) / images
    )
    level = get(got, 2, wd) / wide(images, wd)
    grad_squeeze = dot_tn(pooled - level, grad_squeezed, HIGH)
    grad_pool = dot_nt(grad_squeezed, squeeze, HIGH) / wide(floor, wd)
    pool2 = jnp.concatenate([grad_pool] * d.radix, axis=1)
    sum_grad = total_row(weight * q1 + pool2 * q2[...])
    sum_bend = total_row(weight * q3 + pool2 * q4[...])
    sa[6, 14:16, :] = jnp.zeros((2, LANES), F32)
    put(sa, 6, 12, sum_act1)
    put(sa, 6, 0, sum_grad)
    put(sa, 6, 4, scale2 * (sum_bend - mean2 * sum_grad))
    put(sa, 6, 8, grad_bex)
    got = sum_all(6, 16)
    w_step(2, 4)
    bias2, gain2 = get(got, 0, wide2), get(got, 4, wide2)
    mean_act1 = get(got, 12, mid) / (wide(images, mid) * float(nh * n_ha * nw))
    put(small, 0, 20, bias2)
    put(small, 0, 24, gain2)
    put(small, 0, 28, get(got, 8, wide2))
    grow2 = g2[...] * scale2
    slant2 = grow2 * scale2 * gain2 / wide(total, wide2)
    level2 = grow2 * bias2 / wide(total, wide2) - mean2 * slant2
    att[...] = weight * grow2
    q2[...] = pool2 * grow2

    step6 = 2 * nb

    def back_group(t, carry):
        def cells(u, carry):
            at = pl.ds(pl.multiple_of(t * line + u * step6, step6), step6)
            to = inner_rows(t + 1, nb + u * step6, step6)
            again = step6 // nb
            grad = dm[at, :]
            sums = []
            for r in range(d.radix):
                own = slice(r * wd, (r + 1) * wd)
                grow = jnp.concatenate([att[:, own]] * again, axis=0)
                lift = jnp.concatenate([q2[:, own]] * again, axis=0)
                push = (grow * grad + lift) * slope2[at, own].astype(F32)
                pull = wide(m[at, :], wd) * (level2[:, own] + slant2[:, own] * y2[at, own])
                dyp[to, own] = (push - pull).astype(BF16)
                sums.append(carry[r] + fold(push - pull))
            return tuple(sums)

        return lax.fori_loop(0, line // step6, cells, carry)

    zeros = jnp.zeros((8, wd), F32)
    sum_dy2 = [total_row(s) for s in lax.fori_loop(0, nh, back_group, (zeros,) * d.radix)]
    halo2_start, halo2_recv, halo2_sent = halo(dyp, 1)
    halo2_start()

    acc_g[...] = jnp.zeros((d.radix, wd, 9 * gin), F32)

    def weights_group(t, carry):
        for r in range(d.radix):
            grad = dyp[inner_rows(t + 1), r * wd : (r + 1) * wd]
            acc_g[r] += dot_tn(grad, taps(t, r))
        return carry

    lax.fori_loop(0, nh, weights_group, 0)
    for r in range(d.radix):
        base = wide(mean_act1[:, r * gin : (r + 1) * gin], 9 * gin)
        column = jnp.transpose(jnp.broadcast_to(sum_dy2[r], (LANES, wd)))
        part1[r, :, 0 : 9 * gin] = (acc_g[r] - wide(column, 9 * gin) * base).astype(BF16)
    part1[0, :, 9 * gin :] = jnp.concatenate(
        [grad_excite[:, 0:wd], grad_excite[:, wd:]], axis=0
    ).astype(BF16) * (1.0 / n_ha)
    part1[1, :, 9 * gin : 9 * gin + LANES] = grad_squeeze.astype(BF16)
    part1[1, :, 9 * gin + LANES :] = jnp.zeros((wd, wd - LANES), BF16)
    w_start(1, 0)
    w_step(2, 5)

    for r in range(d.radix):
        for tap in range(9):
            w2t[r, :, tap * wd : (tap + 1) * wd] = w2[r, tap * gin : (tap + 1) * gin, :]
    halo2_recv()

    def transposed(t, carry):
        sums, bends = carry
        at = line_rows(t)
        done = []
        for r in range(d.radix):
            cells = jnp.concatenate(
                [
                    dyp[inner_rows(t + 2 - ky, (2 - kx) * nb), r * wd : (r + 1) * wd]
                    for ky in range(3)
                    for kx in range(3)
                ],
                axis=1,
            )
            done.append(dot_nt(cells, w2t[r]))
        dm[at, :] = jnp.concatenate(done, axis=1)

        def cells(u, carry):
            sums, bends = carry
            at = pl.ds(pl.multiple_of(t * line + u * step1, step1), step1)
            y = y1[at, :]
            _, slope = gate(y * half_a1 + half_b1)
            grad = dm[at, :] * (slope * wide(m[at, :], mid))
            dm[at, :] = grad
            return sums + fold(grad), bends + fold(grad * y)

        return lax.fori_loop(0, line // step1, cells, (sums, bends))

    zeros = jnp.zeros((8, mid), F32)
    sums, bends = lax.fori_loop(0, nh, transposed, (zeros, zeros))
    w_step(1, 0)
    sum_grad = total_row(sums)
    put(sa, 7, 0, sum_grad)
    put(sa, 7, 4, jnp.concatenate(sum_dy2, axis=1))
    put(sa, 7, 2, scale1 * (total_row(bends) - mean1 * sum_grad))
    got = sum_all(7, 8)
    w_step(1, 1)
    bias1, gain1 = get(got, 0, mid), get(got, 2, mid)
    put(small, 0, 32, bias1)
    put(small, 0, 34, gain1)
    put(small, 0, 36, mean_act1)
    small[0, 38:40, :] = jnp.zeros((2, LANES), F32)
    put(small, 0, 40, get(got, 4, wide2))
    small[0, 44:48, :] = jnp.zeros((4, LANES), F32)
    small[0, 18:20, :] = jnp.zeros((2, LANES), F32)
    grow1 = g1[...] * scale1
    slant1 = grow1 * scale1 * gain1 / wide(total, mid)
    level1 = grow1 * bias1 / wide(total, mid) - mean1 * slant1

    acc_c[...] = jnp.zeros((wd, cin), F32)

    def dy_copy(t):
        return pltpu.make_async_copy(mixed.at[line_rows(t)], dy_hbm.at[line_rows(t)], sem_misc.at[t])

    def back_first(t, carry):
        def cells(u, carry):
            at = pl.ds(pl.multiple_of(t * line + u * step1, step1), step1)
            pull = wide(m[at, :], mid) * (level1 + slant1 * y1[at, :])
            mixed[at, :] = (grow1 * dm[at, :] - pull).astype(BF16)
            return carry

        lax.fori_loop(0, line // step1, cells, 0)
        dy_copy(t).start()
        at = line_rows(t)
        acc_c[...] += dot_tn(mixed[at, :], xv[at, :])
        return carry

    lax.fori_loop(0, nh, back_first, 0)
    w_step(1, 2)
    part0[0] = acc_c[:, 0 : cin // 2].astype(BF16)
    part0[1] = acc_c[:, cin // 2 :].astype(BF16)
    w_start(0, 0)
    w_step(1, 3)
    w_step(0, 0)
    w_step(1, 4)
    w_step(0, 1)
    w_step(1, 5)
    for stage in range(2, 6):
        w_step(0, stage)

    results = ((wg0_hbm, 0), (wg1_hbm, 1), (wg2_hbm, 2))
    for hbm, s in results:
        pltpu.make_async_copy((ress if d.inside else parts)[s], hbm, sem_misc.at[nh + s]).start()

    def finish(t, carry):
        dy_copy(t).wait()
        return carry

    lax.fori_loop(0, nh, finish, 0)
    for t in range(max(nh - 2, 0), nh):
        out_copy(t).wait()
    for s in range(3):
        w_sent(s)
    halo1_sent()
    halo2_sent()
    for hbm, s in results:
        pltpu.make_async_copy((ress if d.inside else parts)[s], hbm, sem_misc.at[nh + s]).wait()


def call_block(d, args):
    f32, bf16 = F32, BF16
    cin, wd, mid, rows, nb, nh = d.cin, d.width, d.mid, d.rows, d.nb, d.nh
    vmem, dma = pltpu.VMEM, pltpu.SemaphoreType.DMA
    halves = [(2, wd, lanes) for lanes in d.half]
    shape = jax.ShapeDtypeStruct
    outs = [
        shape((rows, cin), bf16),
        shape((rows, cin), bf16),
        shape((rows, mid), bf16),
        *[shape(s, bf16) for s in halves],
        shape((1, 48, LANES), f32),
    ]
    anywhere = pl.BlockSpec(memory_space=pl.ANY)
    inside = pl.BlockSpec(memory_space=pltpu.VMEM)
    plane, zed = wd // 4, wd // 16
    scratch = [
        vmem((rows, cin), bf16),
        vmem((max(2 * rows, (nh + 2) * d.padded), cin // 2), bf16),
        vmem((rows, mid), f32),
        vmem(((nh + 2) * d.padded, mid), bf16),
        vmem((rows, d.wide), f32),
        vmem((rows, d.wide), bf16),
        vmem((rows, d.wide), bf16),
        vmem((rows, wd), bf16),
        vmem((d.line, cin), f32),
        vmem((2, d.line, cin), bf16),
        vmem((rows, wd), f32),
        vmem((wd, cin), f32),
        vmem((d.radix, wd, 9 * d.gin), f32),
        vmem((wd, cin), bf16),
        vmem((d.radix, d.gin, 9 * wd), bf16),
        vmem((nb, d.wide), f32),
        vmem((nb, d.wide), f32),
        vmem((nb, d.wide), f32),
        vmem((8, cin), f32),
        vmem((nb, wd), f32),
        *[vmem(s, bf16) for s in halves],
        *[vmem((wd, lanes), bf16) for lanes in d.half],
        *[vmem((3, plane, lanes), bf16) for lanes in d.half],
        *[vmem((3, zed, lanes), bf16) for lanes in d.half],
        *[vmem((plane, lanes), bf16) for lanes in d.half],
        *[vmem(s, bf16) for s in halves],
        vmem((8, 16, LANES), f32),
        vmem((8, 16, LANES), f32),
        vmem((8, d.n_ha, 16, LANES), f32),
        vmem((8, d.n_img, 16, LANES), f32),
        vmem((nb, d.wide), bf16),
        vmem((d.n_ha, nb, d.wide), bf16),
        vmem((nb, 2 * LANES), f32),
        vmem((d.n_ha, nb, 2 * LANES), f32),
        dma((nh,)),
        dma((2, nh)),
        dma((nh,)),
        dma((2, nh)),
        dma((nh + 3,)),
        dma((10, d.n_ha)),
        dma((10, d.n_ha)),
        dma((8, d.n_img)),
        dma((8, d.n_img)),
        dma((2, 2)),
        dma((2, 2)),
        dma((3, 24)),
        dma((3, 24)),
    ]
    return pl.pallas_call(
        functools.partial(block_kernel, d),
        out_shape=outs,
        in_specs=[anywhere, anywhere] + [inside] * 16,
        out_specs=[anywhere] * 6 + [inside],
        scratch_shapes=scratch,
        name="block",
        compiler_params=pltpu.CompilerParams(
            collective_id=0, has_side_effects=True, vmem_limit_bytes=60 << 20
        ),
    )(*args)


def finish_kernel(d, out_in, dn, dy, w1, wg0, wg1, wg2, small, *outs):
    (out, gin, gw1, gg1, gb1, gw2, gg2, gb2, gwsq, ggs, gbs, gwex, gbex, gw3, gg3, gb3) = outs
    wd, gin_group = d.width, d.gin
    out[...] = out_in[...]
    gin[...] = (dn[...].astype(F32) + dot_nt(dy[...], w1[...])).astype(BF16)

    @pl.when(pl.program_id(0) == 0)
    def _():
        half = d.cin // 2
        for c in range(2):
            gw1[c * half : (c + 1) * half, :] = jnp.transpose(wg0[c].astype(F32))
            gw3[:, c * half : (c + 1) * half] = wg2[c].astype(F32)
        rows = small[0]
        means, taken = get(rows, 36, d.mid), get(rows, 40, d.wide)
        for r in range(d.radix):
            mean = means[:, r * gin_group : (r + 1) * gin_group]
            mean = jnp.transpose(jnp.broadcast_to(mean, (LANES, gin_group)))
            back = wide(mean, wd) * taken[:, r * wd : (r + 1) * wd]
            for tap in range(9):
                cells = wg1[r, :, tap * gin_group : (tap + 1) * gin_group]
                gw2[r, tap] = jnp.transpose(cells.astype(F32)) + back
        cells = wg1[0, :, 9 * gin_group :].astype(F32)
        gwex[:, 0:wd] = cells[0 : d.inter, :]
        gwex[:, wd:] = cells[d.inter :, :]
        gwsq[...] = wg1[1, :, 9 * gin_group : 9 * gin_group + d.inter].astype(F32)
        gb3[...] = get(rows, 0, d.cin)
        gg3[...] = get(rows, 8, d.cin)
        gbs[...] = rows[16:17, :]
        ggs[...] = rows[17:18, :]
        gb2[...] = get(rows, 20, d.wide)
        gg2[...] = get(rows, 24, d.wide)
        gbex[...] = get(rows, 28, d.wide)
        gb1[...] = get(rows, 32, d.mid)
        gg1[...] = get(rows, 34, d.mid)


def call_finish(d, out_in, dn, dy, w1, wg0, wg1, wg2, small):
    shape = jax.ShapeDtypeStruct
    cin, wd, mid, line = d.cin, d.width, d.mid, d.line

    def whole(*dims):
        return pl.BlockSpec(dims, lambda t: (0,) * len(dims))

    def block(lanes):
        return pl.BlockSpec((line, lanes), lambda t: (t, 0))

    small_dims = [
        (cin, mid), (1, mid), (1, mid), (d.radix, 9, d.gin, wd), (1, d.wide), (1, d.wide), (wd, d.inter),
        (1, d.inter), (1, d.inter), (d.inter, d.wide), (1, d.wide), (wd, cin), (1, cin), (1, cin),
    ]
    return pl.pallas_call(
        functools.partial(finish_kernel, d),
        grid=(d.nh,),
        out_shape=[shape((d.rows, cin), BF16), shape((d.rows, cin), BF16)]
        + [shape(s, F32) for s in small_dims],
        in_specs=[
            block(cin), block(cin), block(mid), whole(cin, mid),
            whole(*wg0.shape), whole(*wg1.shape), whole(*wg2.shape), whole(*small.shape),
        ],
        out_specs=[block(cin), block(cin)] + [whole(*s) for s in small_dims],
        name="finish",
        compiler_params=pltpu.CompilerParams(vmem_limit_bytes=60 << 20),
    )(out_in, dn, dy, w1, wg0, wg1, wg2, small)


def on_device(
    inputs, image_count, pixel_mask, w_first, gain_first, bias_first, w_group, gain_group, bias_group,
    w_squeeze, gain_squeeze, bias_squeeze, w_excite, bias_excite, w_last, gain_last, bias_last, cotangent,
):
    n_img, n_ha = lax.axis_size("img"), lax.axis_size("ha")
    d = Dims(n_img, n_ha, inputs.shape, w_group.shape, w_squeeze.shape)
    nb, nh, nw, cin = inputs.shape

    def by_rows(cells):
        return jnp.transpose(cells, (1, 2, 0, 3)).reshape(d.rows, cin)

    def by_image(cells):
        return jnp.transpose(cells.reshape(nh, nw, nb, cin), (2, 0, 1, 3))

    live = (lax.broadcasted_iota(jnp.int32, (nb,), 0) < image_count[0]).astype(F32)
    valid = pixel_mask.astype(F32) * live[:, None, None]
    valid = jnp.transpose(valid, (1, 2, 0)).reshape(d.rows, 1)
    valid = jnp.broadcast_to(valid, (d.rows, LANES))
    live = jnp.broadcast_to(live[:, None], (nb, LANES))
    row = lambda v: v.reshape(1, -1)
    args = (
        by_rows(inputs), by_rows(cotangent), valid, live,
        w_first, row(gain_first), row(bias_first),
        w_group.reshape(d.radix, 9 * d.gin, d.width), row(gain_group), row(bias_group),
        w_squeeze, row(gain_squeeze), row(bias_squeeze), w_excite, row(bias_excite),
        w_last, row(gain_last), row(bias_last),
    )
    out, dn, dy, wg0, wg1, wg2, small = call_block(d, args)
    if not d.inside:
        wg0, wg1, wg2 = lax.psum((wg0, wg1, wg2), ("img", "ha"))
    done = call_finish(d, out, dn, dy, w_first, wg0, wg1, wg2, small)
    (out, gin, gw1, gg1, gb1, gw2, gg2, gb2, gwsq, ggs, gbs, gwex, gbex, gw3, gg3, gb3) = done
    flat = lambda v: v.reshape(-1)
    return (
        by_image(out), by_image(gin), gw1, flat(gg1), flat(gb1), gw2.reshape(w_group.shape), flat(gg2), flat(gb2),
        gwsq, flat(ggs), flat(gbs), gwex, flat(gbex), gw3, flat(gg3), flat(gb3),
    )


def solution(mesh):
    cells = P("img", "ha", None, None)
    placed = (cells, P("img"), P("img", "ha", None)) + (P(),) * 14 + (cells,)
    return jax.shard_map(
        on_device,
        mesh=mesh,
        in_specs=placed,
        out_specs=(cells, cells) + (P(),) * 14,
        check_vma=False,
    )
```

time: 1010 us -> 198 us (0.20); the launches traced: 996 us -> 197 us
  local copies, waits for them, and re-layouts: 338 us -> 2.52 us
  blocking collectives: 311 us -> 0 us
  Pallas kernels: 0 us -> 192 us
  other arithmetic: 145 us -> 0.9 us
  waiting for transfers between devices: 98.7 us -> 0 us
  matrix products: 81.2 us -> 0 us
  between operations: 16 us -> 1.32 us
    psum x10 -> x0, blocking collectives: 311 us -> none  [the longest x3 125 us: norm_back(): lax.psum((jnp.sum(grad_norm, axis=0), jnp.sum(grad_norm * centered, axis=...]
    pallas_call x0 -> x2, Pallas kernels: none -> 192 us  [the longest x1 175 us: call_block(): pl.pallas_call(functools.partial(block_kernel, d), out_shape=outs, in_spe...]
    psum x1 -> x0, waiting for transfers between devices: 98.3 us -> none  [on_device(): lax.psum((grad_w_first, grad_w_group, grad_w_last, grad_w_squeeze * first...]
    reshape x9 -> x0, local copies, waits for them, and re-layouts: 96.5 us -> none  [the longest x4 64.5 us: gather_taps(): jnp.concatenate(taps, axis=-1).reshape(-1, len(taps) * (upper - lower))]
    reduce_sum x10 -> x0, other arithmetic: 88.7 us -> none  [the longest x1 29.7 us: on_device(): jnp.sum(split_view * attention[:, None], axis=2).reshape(-1, mid_width)]
    dot_general x18 -> x0, matrix products: 81.2 us -> none  [the longest x2 14.1 us: on_device(): jnp.dot(patch_list[branch], w_group[branch].reshape(9 * group_in, mid_wid...]
    unnamed x191 -> x0, local copies, waits for them, and re-layouts: 76.5 us -> none
    concatenate x12 -> x0, local copies, waits for them, and re-layouts: 61.8 us -> none  [the longest x6 34.2 us: gather_taps(): jnp.concatenate(taps, axis=-1).reshape(-1, len(taps) * (upper - lower))]
  transfers between devices with their start and end apart: 5 -> 0, of which waited for: 2 -> 0; matrix products, arithmetic and copies ran while one was open for 9% -> 0% of each run, Pallas kernels for 0% -> 0%
where the time goes in v1:
time: 198 us; the launch traced here: 197 us
  Pallas kernels  192 us (97%)
  local copies, waits for them, and re-layouts  2.52 us (1%)
    pallas_call x1, Pallas kernels, call_block(): pl.pallas_call(functools.partial(block_kernel, d), out_shape=outs, in_spe...  175 us
    pallas_call x1, Pallas kernels, call_finish(): pl.pallas_call(functools.partial(finish_kernel, d), grid=(d.nh,), out_sha...  16.8 us

profile of v1, /device:TPU:0, one launch (start us, length us, event | category | flops | bytes accessed | tf_op | source)
XLA Modules:
  0.0 196.7 jit_solution(356597486648105216)
XLA Ops:
  1.3 0.7 broadcast_in_dim.16.live
  2.0 0.9 multiply_bitcast_fusion
  2.9 0.1 copy.34
  3.0 0.1 broadcast_in_dim.6
  3.1 1.6 broadcast_in_dim.7.m
  4.7 175.2 %block.1 = (bf16[3136,1024]{1,0:T(8,128)(2,1)}, bf16[3136,1024]{1,0:T(8,128)(2,1)}, bf16[3136,256]{1,0:T(8,128)(2,1)}, bf16[2,256,512]{2,1,0:T(8,128)(2,1)}, bf1...) custom-call(bf16[3136,1024]{1,0:T(8,128)(2,1)} %bitcast.36, ...), custom_call_target="tpu_custom_call" | custom-call | tf_op jit(solution)/shard_map/block/pallas_call | solution.py:947
  179.9 16.8 %finish.1 = (bf16[3136,1024]{1,0:T(8,128)(2,1)}, bf16[3136,1024]{1,0:T(8,128)(2,1)}, f32[1024,256]{1,0:T(8,128)}, f32[1,256]{1,0:T(1,128)}, f32[1,256]{1,0:T(1,1...) custom-call(bf16[3136,1024]{1,0:T(8,128)(2,1)} %get-tuple-element.39, ...), custom_call_target="tpu_custom_call" | custom-call | tf_op jit(solution)/shard_map/finish/pallas_call | solution.py:1010
  (1 shorter events, 0.0 us)

commit v2 on v1

v2 whole, which is shorter than its diff:
```python
import functools

import jax
import jax.numpy as jnp
from jax import lax
from jax.experimental import pallas as pl
from jax.experimental.pallas import tpu as pltpu
from jax.sharding import PartitionSpec as P

EPS = 1e-05
F32 = jnp.float32
BF16 = jnp.bfloat16
HIGH = lax.Precision.HIGHEST
MESH = pl.DeviceIdType.MESH
LANES = 128


def dot(a, b, precision=None):
    return jnp.dot(a, b, preferred_element_type=F32, precision=precision)


def dot_nt(a, b, precision=None):
    return lax.dot_general(
        a, b, (((1,), (1,)), ((), ())), preferred_element_type=F32, precision=precision
    )


def dot_tn(a, b, precision=None):
    return lax.dot_general(
        a, b, (((0,), (0,)), ((), ())), preferred_element_type=F32, precision=precision
    )


def wide(cell, lanes):
    return jnp.concatenate([cell] * (lanes // LANES), axis=1)


def fold(cells):
    rows, lanes = cells.shape
    return jnp.sum(cells.reshape(rows // 8, 8, lanes), axis=0)


def fold_images(cells, images):
    rows, lanes = cells.shape
    return jnp.sum(cells.reshape(rows // images, images, lanes), axis=0)


def total_row(cells):
    return jnp.sum(cells, axis=0, keepdims=True)


def put(ref, row, vector):
    for j in range(vector.shape[1] // LANES):
        ref[row + j : row + j + 1, :] = vector[:, j * LANES : (j + 1) * LANES]


def get(cells, row, lanes):
    return jnp.concatenate(
        [cells[row + j : row + j + 1, :] for j in range(lanes // LANES)], axis=1
    )


def moments(sums, squares, total):
    mean = sums / total
    spread = squares / total - mean * mean
    return mean, lax.rsqrt(spread + EPS)


def gate(half):
    bend = jnp.tanh(half)
    rise = 1.0 + bend
    value = half * rise
    return value, 0.5 * (rise + value * (1.0 - bend))


def split_bf16(cells):
    high = cells.astype(BF16)
    return high, (cells - high.astype(F32)).astype(BF16)


class Dims:
    def __init__(self, n_img, n_ha, inputs, w_group, w_squeeze):
        self.n_img, self.n_ha = n_img, n_ha
        self.nb, self.nh, self.nw, self.cin = inputs
        self.radix, _, _, self.gin, self.width = w_group
        self.mid = self.radix * self.gin
        self.wide = self.radix * self.width
        self.inter = w_squeeze[1]
        self.line = self.nw * self.nb
        self.rows = self.nh * self.line
        self.padded = (self.nw + 2) * self.nb
        self.half = (self.cin // 2, 6 * self.gin, self.cin // 2, 3 * self.gin + self.width, self.cin // 2)
        self.sets = 4
        self.inside = n_img == 8 and n_ha == 4
        self.sums = dict(cnt=4, s1=4, s2=8, act=4, v0=8, s3=16, b3=16, b2=8, misc=8, b1=4)
        self.paired = ("s3", "b3")


def block_kernel(
    d,
    x_hbm, ct_hbm, mask_in, count_in, w1, g1, c1, w2, g2, c2, wsq, gs, cs, wex, bex, w3, g3, c3,
    out_hbm, dn_hbm, dy_hbm, wg0_hbm, wg1_hbm, wg2_hbm, wg3_hbm, small,
    mb, live, xv, ctv, y1, a1p, y2, act2, slope2, mixed, ost, dm, acc_c, acc_g, w3p, w2x, w2l, w2r,
    att, q2, q4, vecs, pools, v0, cols,
    parts, rcs, rxys, rzs, mids, ress, vres, sums, ga_src, ga_buf, pf_src, pf_buf, fc_src, fc_buf,
    sem_x, sem_ct, sem_out, sem_dn, sem_misc, ssa, rsa, ssi, rsi, ssh, rsh, ssw, rsw,
):
    n_img, n_ha = d.n_img, d.n_ha
    nb, nh, nw = d.nb, d.nh, d.nw
    cin, mid, wd, wide2, line, rows = d.cin, d.mid, d.width, d.wide, d.line, d.rows
    gin, padded = d.gin, d.padded
    dyp = ctv
    half = cin // 2
    i = lax.axis_index("img")
    h = lax.axis_index("ha")

    def ha_peer(k):
        return (i, lax.rem(h + k, n_ha))

    def img_peer(k):
        return (lax.rem(i + k, n_img), h)

    z_of, x_of, y_of, core = i // 2, lax.rem(i, 2), h // 2, lax.rem(h, 2)
    spot = x_of * 2 + y_of

    def core_peer():
        return (i, y_of * 2 + (1 - core))

    def plane_peer(k):
        other = lax.rem(spot + k, 4)
        return (z_of * 2 + other // 2, lax.rem(other, 2) * 2 + core)

    def z_peer(k):
        return (lax.rem(z_of + k, 4) * 2 + x_of, h)

    def any_peer(k):
        return (lax.rem(i + k // 4, 8), lax.rem(h + k % 4, 4))

    def chip_peer(k):
        return (lax.rem(i + k // 2, 8), lax.rem(y_of + k % 2, 2) * 2 + core)

    def remote(src, dst, send, recv, peer):
        return pltpu.make_async_remote_copy(
            src_ref=src, dst_ref=dst, send_sem=send, recv_sem=recv, device_id=peer, device_id_type=MESH
        )

    def line_rows(t):
        return pl.ds(pl.multiple_of(t * line, line), line)

    def block_rows(t, u, step):
        return pl.ds(pl.multiple_of(t * line + u * step, nb), step)

    def x_copy(t):
        return pltpu.make_async_copy(x_hbm.at[line_rows(t)], xv.at[line_rows(t)], sem_x.at[t])

    def half_rows(t, c):
        return pl.ds(pl.multiple_of(c * rows + t * line, nb), line)

    def ct_copy(t, c):
        return pltpu.make_async_copy(
            ct_hbm.at[line_rows(t), pl.ds(c * half, half)], ctv.at[half_rows(t, c)], sem_ct.at[c, t]
        )

    def start_inputs(t, carry):
        x_copy(t).start()
        return carry

    lax.fori_loop(0, nh, start_inputs, 0)

    barrier = pltpu.get_barrier_semaphore()
    if d.inside:
        peers = [any_peer(k) for k in range(1, 32)]
    else:
        peers = [ha_peer(k) for k in range(1, n_ha)] + [img_peer(k) for k in range(1, n_img)]
    for peer in peers:
        pl.semaphore_signal(barrier, inc=1, device_id=peer, device_id_type=MESH)

    slots = lax.broadcasted_iota(jnp.int32, (nb, LANES), 0)
    live[...] = (slots < count_in[0]).astype(F32)

    def spread(t, carry):
        cells = mask_in[t].astype(F32)
        alive = live[...]
        for w in range(nw):
            cell = jnp.broadcast_to(cells[:, w : w + 1], (nb, LANES)) * alive
            mb[block_rows(t, w, nb), :] = cell.astype(BF16)
            carry = carry + cell
        return carry

    pixels = lax.fori_loop(0, nh, spread, jnp.zeros((nb, LANES), F32))

    def mask_of(at, lanes):
        return wide(mb[at, :].astype(F32), lanes)

    def inner_rows(t, at=nb, count=line):
        return pl.ds(pl.multiple_of(t * padded + at, nb), count)

    def clear(ref):
        zero = jnp.zeros((nb, ref.shape[1]), BF16)

        def body(t, carry):
            ref[inner_rows(t, 0, nb), :] = zero
            ref[inner_rows(t, nb + line, nb), :] = zero
            return carry

        lax.fori_loop(0, nh + 2, body, 0)

        def edge(t, carry):
            ref[inner_rows(0, t * nb, nb), :] = zero
            ref[inner_rows(nh + 1, t * nb, nb), :] = zero
            return carry

        lax.fori_loop(0, nw + 2, edge, 0)

    clear(a1p)
    pl.semaphore_wait(barrier, len(peers))

    def swap(src, buf, send, recv, peer, n):
        def copy(k):
            return remote(src, buf.at[k], send.at[k], recv.at[k], peer(k))

        def each(act, carry):
            if n > 32:
                return lax.fori_loop(1, n, act, carry)
            for k in range(1, n):
                carry = act(k, carry)
            return carry

        def begin(k, carry):
            copy(k).start()
            return carry

        def sent(k, carry):
            copy(k).wait_send()
            return carry

        def take(k, carry):
            copy(k).wait_recv()
            return carry + buf[k].astype(F32)

        def finish():
            total = each(take, src[...].astype(F32))
            each(sent, 0)
            return total

        return (lambda: each(begin, 0)), finish

    class Everywhere:
        def __init__(self, name):
            self.at, refs = sums[name]["src"], sums[name]
            self.refs = refs
            if not d.inside:
                return
            send, recv = refs["send"], refs["recv"]
            if name in d.paired:
                self.pair = remote(self.at, refs["other"], send.at[0], recv.at[0], core_peer())
                self.start_far, self.finish_far = swap(refs["mid"], refs["buf"], send, recv, chip_peer, 16)
            else:
                self.pair = None
                self.start_far, self.finish_far = swap(self.at, refs["buf"], send, recv, any_peer, 32)

        def start(self):
            if d.inside:
                if self.pair is not None:
                    self.pair.start()
                    self.pair.wait_recv()
                    self.refs["mid"][...] = self.at[...] + self.refs["other"][...]
                self.start_far()

        def finish(self):
            if d.inside:
                total = self.finish_far()
                if self.pair is not None:
                    self.pair.wait_send()
                return total
            refs = self.refs
            start, finish = swap(self.at, refs["buf_ha"], refs["send_ha"], refs["recv_ha"], ha_peer, n_ha)
            start()
            refs["mid"][...] = finish()
            start, finish = swap(refs["mid"], refs["buf_img"], refs["send"], refs["recv"], img_peer, n_img)
            start()
            return finish()

    def halo(ref, at):
        def down():
            return remote(
                ref.at[inner_rows(nh)], ref.at[inner_rows(0)], ssh.at[at, 0], rsh.at[at, 0],
                (i, jnp.minimum(h + 1, n_ha - 1)),
            )

        def up():
            return remote(
                ref.at[inner_rows(1)], ref.at[inner_rows(nh + 1)], ssh.at[at, 1], rsh.at[at, 1],
                (i, jnp.maximum(h - 1, 0)),
            )

        def start():
            @pl.when(h < n_ha - 1)
            def _():
                down().start()

            @pl.when(h > 0)
            def _():
                up().start()

        def wait_recv():
            @pl.when(h > 0)
            def _():
                down().wait_recv()

            @pl.when(h < n_ha - 1)
            def _():
                up().wait_recv()

        def wait_send():
            @pl.when(h < n_ha - 1)
            def _():
                down().wait_send()

            @pl.when(h > 0)
            def _():
                up().wait_send()

        return start, wait_recv, wait_send

    plane_rows, z_rows = wd // 4, wd // 16

    def plane_at(other):
        return pl.ds(pl.multiple_of(other * plane_rows, plane_rows), plane_rows)

    def z_at(other, base=0):
        return pl.ds(pl.multiple_of(base + other * z_rows, z_rows), z_rows)

    def w_copy(s, stage, k):
        sem = (s, stage * 4 + k)
        if stage == 0:
            src, dst, peer = parts[s].at[1 - core], rcs[s], core_peer()
        elif stage == 1:
            src = parts[s].at[core, plane_at(lax.rem(spot + k, 4))]
            dst, peer = rxys[s].at[k - 1], plane_peer(k)
        elif stage == 2:
            src = mids[s].at[z_at(lax.rem(z_of + k, 4))]
            dst, peer = rzs[s].at[k - 1], z_peer(k)
        elif stage == 3:
            src = dst = ress[s].at[core, z_at(z_of, spot * plane_rows)]
            peer = z_peer(k)
        elif stage == 4:
            src = dst = ress[s].at[core, plane_at(spot)]
            peer = plane_peer(k)
        else:
            src = dst = ress[s].at[core]
            peer = core_peer()
        return remote(src, dst, ssw.at[sem], rsw.at[sem], peer)

    def w_ks(stage):
        return (1,) if stage in (0, 5) else (1, 2, 3)

    def w_arrival(s, stage, k):
        sem = (s, stage * 4 + k)
        if stage == 3:
            dst = ress[s].at[core, z_at(lax.rem(z_of - k + 4, 4), spot * plane_rows)]
        elif stage == 4:
            dst = ress[s].at[core, plane_at(lax.rem(spot - k + 4, 4))]
        else:
            dst = ress[s].at[1 - core]
        return remote(dst, dst, ssw.at[sem], rsw.at[sem], core_peer())

    def w_start(s, stage):
        if d.inside:
            for k in w_ks(stage):
                w_copy(s, stage, k).start()

    def w_finish(s, stage, fix=None):
        if not d.inside:
            return
        for k in w_ks(stage):
            if stage <= 2:
                w_copy(s, stage, k).wait_recv()
            else:
                w_arrival(s, stage, k).wait_recv()
        part, inner = parts[s], mids[s]
        if stage == 0:
            rc = rcs[s]

            def add(t, carry):
                at = pl.ds(pl.multiple_of(t * 16, 16), 16)
                part[core, at, :] = (part[core, at, :].astype(F32) + rc[at, :].astype(F32)).astype(BF16)
                return carry

            lax.fori_loop(0, wd // 16, add, 0)
        elif stage == 1:
            buf = rxys[s]

            def add(t, carry):
                at = pl.ds(pl.multiple_of(t * 16, 16), 16)
                own = pl.ds(pl.multiple_of(spot * plane_rows + t * 16, 16), 16)
                total = part[core, own, :].astype(F32)
                for k in range(3):
                    total = total + buf[k, at, :].astype(F32)
                inner[at, :] = total.astype(BF16)
                return carry

            lax.fori_loop(0, plane_rows // 16, add, 0)
        elif stage == 2:
            buf = rzs[s]
            total = inner[z_at(z_of), :].astype(F32)
            for k in range(3):
                total = total + buf[k].astype(F32)
            if s >= d.sets:
                vres[...] = total
                return
            if fix is not None:
                total = fix(total)
            ress[s][core, z_at(z_of, spot * plane_rows), :] = total.astype(BF16)

    def w_step(s, stage, fix=None):
        w_finish(s, stage, fix)
        if stage < 5:
            w_start(s, stage + 1)

    def w_sent(s):
        if d.inside:
            for stage in range(6 if s < d.sets else 3):
                for k in w_ks(stage):
                    w_copy(s, stage, k).wait_send()

    count = Everywhere("cnt")
    count.at[...] = jnp.zeros((4, LANES), F32)
    count.at[0:1, :] = total_row(pixels)
    count.at[1:2, :] = total_row(live[...]) * (1.0 / n_ha)
    count.start()

    def first(t, carry):
        sums, squares = carry
        x_copy(t).wait()
        ct_copy(t, 0).start()
        ct_copy(t, 1).start()
        at = line_rows(t)
        y = dot(xv[at, :], w1[...])
        y1[at, :] = y
        masked = y * mask_of(at, mid)
        return sums + fold(masked), squares + fold(masked * y)

    zeros = jnp.zeros((8, mid), F32)
    totals, squares = lax.fori_loop(0, nh, first, (zeros, zeros))
    norm1 = Everywhere("s1")
    put(norm1.at, 0, total_row(totals))
    put(norm1.at, 2, total_row(squares))
    norm1.start()
    for r in range(d.radix):
        for ky in range(3):
            for e in range(4):
                if e <= 2:
                    left = w2[r, (ky * 3 + 2 - e) * gin : (ky * 3 + 3 - e) * gin, :]
                if e >= 1:
                    right = w2[r, (ky * 3 + 3 - e) * gin : (ky * 3 + 4 - e) * gin, :]
                if e == 0:
                    w2l[r, :, ky * wd : (ky + 1) * wd] = left
                elif e == 3:
                    w2r[r, :, ky * wd : (ky + 1) * wd] = right
                else:
                    lanes = slice((ky * 2 + e - 1) * wd, (ky * 2 + e) * wd)
                    w2x[r, 0:gin, lanes] = left
                    w2x[r, gin:, lanes] = right
    got = count.finish()
    total, images = got[0:1, :], got[1:2, :]
    got = norm1.finish()
    mean1, scale1 = moments(get(got, 0, mid), get(got, 2, mid), wide(total, mid))
    half_a1 = 0.5 * g1[...] * scale1
    half_b1 = 0.5 * c1[...] - half_a1 * mean1

    step1 = 4 * nb

    def act_first(t, carry):
        def cells(u, carry):
            at = block_rows(t, u, step1)
            value, _ = gate(y1[at, :] * half_a1 + half_b1)
            value = value * mask_of(at, mid)
            a1p[inner_rows(t + 1, nb + u * step1, step1), :] = value.astype(BF16)
            return carry + fold(value)

        return lax.fori_loop(0, line // step1, cells, carry)

    def edges(body, carry):
        return lax.fori_loop(0, 2, lambda t, c: body(t * (nh - 1), c), carry)

    totals = edges(act_first, jnp.zeros((8, mid), F32))
    halo1_start, halo1_recv, halo1_sent = halo(a1p, 0)
    halo1_start()
    totals = lax.fori_loop(1, nh - 1, act_first, totals)
    act_sum = Everywhere("act")
    act_sum.at[...] = jnp.zeros((4, LANES), F32)
    put(act_sum.at, 0, total_row(totals))
    act_sum.start()

    def taps(t, r, first=0, last=9):
        return jnp.concatenate(
            [
                a1p[inner_rows(t + tap // 3, (tap % 3) * nb), r * gin : (r + 1) * gin]
                for tap in range(first, last)
            ],
            axis=1,
        )

    def group(t, carry):
        at = line_rows(t)
        mask = mask_of(at, wd)
        done = []
        for r in range(d.radix):
            sums, squares = carry[r]
            y = dot(taps(t, r), w2[r])
            y2[at, r * wd : (r + 1) * wd] = y.astype(BF16)
            masked = y * mask
            done.append((sums + fold(masked), squares + fold(masked * y)))
        return tuple(done)

    zeros = jnp.zeros((8, wd), F32)
    sums2 = lax.fori_loop(1, nh - 1, group, ((zeros, zeros),) * d.radix)
    halo1_recv()
    sums2 = edges(group, sums2)
    norm2 = Everywhere("s2")
    put(norm2.at, 0, jnp.concatenate([total_row(s) for s, _ in sums2], axis=1))
    put(norm2.at, 4, jnp.concatenate([total_row(q) for _, q in sums2], axis=1))
    norm2.start()

    acc_c[...] = jnp.zeros((wd, cin), F32)
    vecs[...] = jnp.zeros((8, cin), F32)

    def norm_products(t, carry):
        at = line_rows(t)
        mask = mask_of(at, mid)
        hat = ((y1[at, :] - mean1) * scale1 * mask).astype(BF16)
        x = xv[at, :]
        acc_c[...] += dot_tn(hat, x)
        vecs[...] += dot_tn(mb[at, :], x)[0:8, :]
        return carry

    lax.fori_loop(0, nh, norm_products, 0)
    norm2_done = norm2.finish()
    for c in range(2):
        parts[4][c] = acc_c[:, c * half : (c + 1) * half].astype(BF16)
    w_start(4, 0)
    v0_sum = Everywhere("v0")
    put(v0_sum.at, 0, vecs[0:1, :])
    v0_sum.start()
    mean2, scale2 = moments(get(norm2_done, 0, wide2), get(norm2_done, 4, wide2), wide(total, wide2))
    half_a2 = 0.5 * g2[...] * scale2
    half_b2 = 0.5 * c2[...] - half_a2 * mean2

    lane_blocks = wd // LANES
    step2 = 4 * nb
    zero = jnp.zeros((nb, LANES), F32)
    for j in range(lane_blocks):
        own = slice(j * LANES, (j + 1) * LANES)

        def act_group(t, pool):
            at = pl.ds(pl.multiple_of(t * step2, step2), step2)
            mask = mb[at, :]
            full = mask.astype(F32)
            for r in range(d.radix):
                lanes = slice(r * wd + j * LANES, r * wd + (j + 1) * LANES)
                value, _ = gate(y2[at, lanes].astype(F32) * half_a2[:, lanes] + half_b2[:, lanes])
                value = value * full
                act2[at, lanes] = value.astype(BF16)
                pool = pool + fold_images(value, nb)
            return pool

        pools[:, own] = lax.fori_loop(0, rows // step2, act_group, zero)

    pool = pools[...]
    squeeze = wsq[...].astype(F32)
    excite = wex[...].astype(F32)
    pf_src[:, 0 : d.inter] = dot(pool, squeeze, HIGH)
    pf_src[:, d.inter :] = pixels
    pf_start, pf_finish = swap(pf_src, pf_buf, ssa.at[0], rsa.at[0], ha_peer, n_ha)
    pf_start()

    def slopes(block):
        lanes = slice(block * LANES, (block + 1) * LANES)
        ha2, hb2 = half_a2[:, lanes], half_b2[:, lanes]

        def body(t, carry):
            slopes, bends = carry
            at = pl.ds(pl.multiple_of(t * step2, step2), step2)
            y = y2[at, lanes].astype(F32)
            _, slope = gate(y * ha2 + hb2)
            slope = slope * mb[at, :].astype(F32)
            slope2[at, lanes] = slope.astype(BF16)
            return slopes + fold_images(slope, nb), bends + fold_images(slope * y, nb)

        q2[:, lanes], q4[:, lanes] = lax.fori_loop(0, rows // step2, body, (zero, zero))

    total_blocks = d.radix * lane_blocks
    for block in range(total_blocks // 4):
        slopes(block)
    w_step(4, 0)
    both = pf_finish()
    floor = jnp.maximum(both[:, d.inter :], 1.0)
    squeezed = both[:, 0 : d.inter] / floor
    live_now = live[...]
    fc_src[...] = jnp.zeros(fc_src.shape, F32)
    put(fc_src.at[0], 0, total_row(squeezed * live_now))
    put(fc_src.at[0], 1, total_row(squeezed * squeezed * live_now))
    fc_start, fc_finish = swap(fc_src.at[0], fc_buf.at[0], ssi.at[0], rsi.at[0], img_peer, n_img)
    fc_start()
    for block in range(total_blocks // 4, total_blocks):
        slopes(block)
    got = fc_finish()
    mean_s, scale_s = moments(got[0:1, :], got[1:2, :], images)
    centered = (squeezed - mean_s) * scale_s
    hidden, hidden_slope = gate(0.5 * (centered * gs[...] + cs[...]))
    logits = dot(hidden, excite, HIGH) + bex[...]
    gap = logits[:, 0:wd] - logits[:, wd:]
    att[:, 0:wd] = jax.nn.sigmoid(gap)
    att[:, wd:] = jax.nn.sigmoid(-gap)

    step3 = 2 * nb

    def mix(t, carry):
        def cells(u, carry):
            at = block_rows(t, u, step3)
            weight = jnp.concatenate([att[...]] * (step3 // nb), axis=0)
            both = act2[at, :].astype(F32) * weight
            mixed[at, :] = (both[:, 0:wd] + both[:, wd:]).astype(BF16)
            return carry

        lax.fori_loop(0, line // step3, cells, 0)
        gram, sums = carry
        cells = mixed[line_rows(t), :]
        return gram + dot_tn(cells, cells), sums + fold(cells.astype(F32))

    gram, totals = lax.fori_loop(0, nh, mix, (jnp.zeros((wd, wd), F32), jnp.zeros((8, wd), F32)))
    mix_sum = total_row(totals)
    gram_high, gram_low = split_bf16(gram)
    acc_g[0, :, 0:cin] = dot(gram_high, w3[...]) + dot(gram_low, w3[...])
    mix_high, mix_low = split_bf16(mix_sum)
    sum_last = dot(jnp.broadcast_to(mix_high, (16, wd)), w3[...]) + dot(
        jnp.broadcast_to(mix_low, (16, wd)), w3[...]
    )
    norm3 = Everywhere("s3")
    put(norm3.at, 0, sum_last[0:1, :])
    put(norm3.at, 8, total_row(acc_g[0, :, 0:cin] * w3[...].astype(F32)))
    norm3.start()

    def last_product(t, carry):
        at = line_rows(t)
        ost[at, :] = dot(mixed[at, :], w3[...]).astype(BF16)
        ct_copy(t, 0).wait()
        ct_copy(t, 1).wait()
        return carry

    lax.fori_loop(0, nh, last_product, 0)
    w_step(4, 1)
    got = norm3.finish()
    mean3, scale3 = moments(get(got, 0, cin), get(got, 8, cin), wide(total, cin))
    grow3 = g3[...] * scale3
    half_a3 = 0.5 * grow3
    half_b3 = 0.5 * c3[...] - half_a3 * mean3

    step4 = 4 * nb
    blocks4 = 2 * LANES

    def out_copy(t):
        return pltpu.make_async_copy(ost.at[line_rows(t)], out_hbm.at[line_rows(t)], sem_out.at[t])

    def dn_copy(t, c):
        return pltpu.make_async_copy(
            ctv.at[half_rows(t, c)], dn_hbm.at[line_rows(t), pl.ds(c * half, half)], sem_dn.at[c, t]
        )

    def grad_of(t):
        return jnp.concatenate([ctv[half_rows(t, 0), :], ctv[half_rows(t, 1), :]], axis=1)

    acc_c[...] = jnp.zeros((wd, cin), F32)
    vecs[...] = jnp.zeros((8, cin), F32)

    def last(t, carry):
        for j in range(cin // blocks4):
            lanes = slice(j * blocks4, (j + 1) * blocks4)
            a3, b3 = half_a3[:, lanes], half_b3[:, lanes]

            def cells(u, carry):
                at = block_rows(t, u, step4)
                mask = wide(mb[at, :], blocks4)
                x = xv[at, lanes] * jnp.asarray(0.5, BF16)
                arg = ost[at, lanes].astype(F32) * a3 + (b3 + x.astype(F32))
                bend = jnp.tanh(arg)
                rise = 1.0 + bend
                value = arg * rise
                ost[at, lanes] = value.astype(BF16) * mask
                side = j * blocks4 // half
                there = pl.ds(pl.multiple_of(side * rows + t * line + u * step4, nb), step4)
                inner = slice(j * blocks4 - side * half, (j + 1) * blocks4 - side * half)
                push = ctv[there, inner] * (mask * jnp.asarray(0.5, BF16))
                grad = push.astype(F32) * (rise + value * (1.0 - bend))
                ctv[there, inner] = grad.astype(BF16)
                return carry + fold(grad)

            vecs[:, lanes] = lax.fori_loop(0, line // step4, cells, vecs[:, lanes])
        out_copy(t).start()
        dn_copy(t, 0).start()
        dn_copy(t, 1).start()
        acc_c[...] += dot_tn(mixed[line_rows(t), :], grad_of(t))
        return carry

    lax.fori_loop(0, nh, last, 0)
    sum_grad = total_row(vecs[...])
    back3 = Everywhere("b3")
    put(back3.at, 0, sum_grad)
    put(back3.at, 8, scale3 * (total_row(acc_c[...] * w3[...].astype(F32)) - mean3 * sum_grad))
    back3.start()

    w3p[...] = (w3[...].astype(F32) * grow3).astype(BF16)

    def plain_back(t, carry):
        dm[line_rows(t), :] = dot_nt(grad_of(t), w3p[...])
        return carry

    lax.fori_loop(0, nh, plain_back, 0)
    w_finish(4, 2)
    got = back3.finish()
    bias3, gain3 = get(got, 0, cin), get(got, 8, cin)
    put(small.at[0], 0, bias3)
    put(small.at[0], 8, gain3)
    all_wide = wide(total, cin)
    slant3 = scale3 * gain3 / all_wide
    level3 = bias3 / all_wide - mean3 * slant3
    fix = (w3[...].astype(F32) * slant3).astype(BF16)
    fix = dot_nt(fix, w3p[...]).astype(BF16)
    level_high, level_low = split_bf16(level3)
    shift = dot_nt(jnp.broadcast_to(level_high, (16, cin)), w3p[...]) + dot_nt(
        jnp.broadcast_to(level_low, (16, cin)), w3p[...]
    )
    shift = shift[0:1, :]

    def back_mix(t, carry):
        at = line_rows(t)
        dm[at, :] = dm[at, :] - dot(mixed[at, :], fix) - mask_of(at, wd) * shift
        return carry

    lax.fori_loop(0, nh, back_mix, 0)

    step5 = 4 * nb
    sums5 = []
    for j in range(lane_blocks):
        lanes = slice(j * LANES, (j + 1) * LANES)

        def image_sums(t, carry):
            at = pl.ds(pl.multiple_of(t * step5, step5), step5)
            grad = dm[at, lanes]
            done = []
            for r in range(d.radix):
                own = slice(r * wd + j * LANES, r * wd + (j + 1) * LANES)
                a, b, c = carry[r]
                a = a + fold_images(grad * act2[at, own].astype(F32), nb)
                part = grad * slope2[at, own].astype(F32)
                b = b + fold_images(part, nb)
                c = c + fold_images(part * y2[at, own].astype(F32), nb)
                done.append((a, b, c))
            return tuple(done)

        sums5.append(lax.fori_loop(0, rows // step5, image_sums, ((zero, zero, zero),) * d.radix))
    pick = lambda which: jnp.concatenate(
        [sums5[j][r][which] for r in range(d.radix) for j in range(lane_blocks)], axis=1
    )
    q1, q3 = pick(1), pick(2)

    def dn_out(t, carry):
        dn_copy(t, 0).wait()
        dn_copy(t, 1).wait()
        return carry

    lax.fori_loop(0, nh, dn_out, 0)
    clear(dyp)
    ga_src[...] = pick(0).astype(BF16)
    ga_start, ga_finish = swap(ga_src, ga_buf, ssa.at[1], rsa.at[1], ha_peer, n_ha)
    ga_start()

    mix_column = jnp.transpose(jnp.broadcast_to(mix_sum, (LANES, wd)))
    for j in range(cin // LANES):
        lanes = slice(j * LANES, (j + 1) * LANES)
        c = 0 if j * LANES < half else 1
        grad = grow3[:, lanes] * (
            acc_c[:, lanes] - mix_column * level3[:, lanes] - acc_g[0, :, lanes] * slant3[:, lanes]
        )
        parts[2][c, :, j * LANES - c * half : (j + 1) * LANES - c * half] = grad.astype(BF16)
    w_start(2, 0)

    grad_att = ga_finish()
    weight = att[...]
    weighed = weight * grad_att
    both = weighed[:, 0:wd] + weighed[:, wd:]
    grad_logits = weight * (grad_att - jnp.concatenate([both, both], axis=1))
    grad_fc = dot_nt(grad_logits, excite, HIGH) * hidden_slope
    put(fc_src.at[1], 0, total_row(grad_fc))
    put(fc_src.at[1], 1, total_row(grad_fc * centered))
    pooled = pool / wide(floor, wd)
    put(fc_src.at[1], 2, total_row(pooled))
    fc_start, fc_finish = swap(fc_src.at[1], fc_buf.at[1], ssi.at[1], rsi.at[1], img_peer, n_img)
    fc_start()
    w_step(2, 0)
    grad_excite = dot_tn(hidden, grad_logits, HIGH)
    grad_bex = total_row(grad_logits) * (1.0 / n_ha)
    acc_g[...] = jnp.zeros((d.radix, wd, 9 * gin), F32)
    got = fc_finish()
    bias_s, gain_s = got[0:1, :], got[1:2, :]
    put(small.at[0], 16, bias_s)
    put(small.at[0], 17, gain_s)
    grad_squeezed = (gs[...] * scale_s) * (
        grad_fc - live_now * (bias_s + centered * gain_s) / images
    )
    grad_pool = dot_nt(grad_squeezed, squeeze, HIGH) / wide(floor, wd)
    pool2 = jnp.concatenate([grad_pool] * d.radix, axis=1)
    sum_grad = total_row(weight * q1 + pool2 * q2[...])
    sum_bend = total_row(weight * q3 + pool2 * q4[...])
    back2 = Everywhere("b2")
    put(back2.at, 0, sum_grad)
    put(back2.at, 4, scale2 * (sum_bend - mean2 * sum_grad))
    back2.start()
    level = get(got, 2, wd) / wide(images, wd)
    grad_squeeze = dot_tn(pooled - level, grad_squeezed, HIGH)
    grow2 = g2[...] * scale2
    att[...] = weight * grow2
    q2[...] = pool2 * grow2
    w_step(2, 1)
    mean_act1 = get(act_sum.finish(), 0, mid) / (wide(images, mid) * float(nh * n_ha * nw))
    got = back2.finish()
    bias2, gain2 = get(got, 0, wide2), get(got, 4, wide2)
    put(small.at[0], 20, bias2)
    put(small.at[0], 24, gain2)
    slant2 = grow2 * scale2 * gain2 / wide(total, wide2)
    level2 = grow2 * bias2 / wide(total, wide2) - mean2 * slant2

    step6 = 2 * nb

    def back_group(t, carry):
        def cells(u, carry):
            at = block_rows(t, u, step6)
            to = inner_rows(t + 1, nb + u * step6, step6)
            again = step6 // nb
            grad = dm[at, :]
            mask = mask_of(at, wd)
            sums = []
            for r in range(d.radix):
                own = slice(r * wd, (r + 1) * wd)
                grow = jnp.concatenate([att[:, own]] * again, axis=0)
                lift = jnp.concatenate([q2[:, own]] * again, axis=0)
                push = (grow * grad + lift) * slope2[at, own].astype(F32)
                pull = mask * (level2[:, own] + slant2[:, own] * y2[at, own].astype(F32))
                dyp[to, own] = (push - pull).astype(BF16)
                sums.append(carry[r] + fold(push - pull))
            return tuple(sums)

        return lax.fori_loop(0, line // step6, cells, carry)

    zeros = jnp.zeros((8, wd), F32)
    sums2 = edges(back_group, (zeros,) * d.radix)
    halo2_start, halo2_recv, halo2_sent = halo(dyp, 1)
    halo2_start()
    sums2 = lax.fori_loop(1, nh - 1, back_group, sums2)
    sum_dy2 = [total_row(s) for s in sums2]
    misc = Everywhere("misc")
    put(misc.at, 0, jnp.concatenate(sum_dy2, axis=1))
    put(misc.at, 4, grad_bex)
    misc.start()
    w_step(2, 2)

    def weights_group(first, last):
        def body(t, carry):
            for r in range(d.radix):
                grad = dyp[inner_rows(t + 1), r * wd : (r + 1) * wd]
                acc_g[r, :, first * gin : last * gin] += dot_tn(grad, taps(t, r, first, last))
            return carry

        lax.fori_loop(0, nh, body, 0)

    def send_group(s, first, last):
        lanes = (last - first) * gin
        for r in range(d.radix):
            base = wide(mean_act1[:, r * gin : (r + 1) * gin], lanes)
            column = jnp.transpose(jnp.broadcast_to(sum_dy2[r], (LANES, wd)))
            grad = acc_g[r, :, first * gin : last * gin] - wide(column, lanes) * base
            parts[s][r, :, 0:lanes] = grad.astype(BF16)
        w_start(s, 0)

    weights_group(0, 6)
    send_group(1, 0, 6)
    parts[3][0, :, 3 * gin :] = jnp.concatenate(
        [grad_excite[:, 0:wd], grad_excite[:, wd:]], axis=0
    ).astype(BF16) * jnp.asarray(1.0 / n_ha, BF16)
    parts[3][1, :, 3 * gin : 3 * gin + d.inter] = grad_squeeze.astype(BF16)
    parts[3][1, :, 3 * gin + d.inter :] = jnp.zeros((wd, wd - d.inter), BF16)
    weights_group(6, 9)
    send_group(3, 6, 9)
    w_step(1, 0)
    w_step(2, 3)

    pairs = nw // 2

    def back_taps(t, r, which):
        cells = []
        for ky in range(3):
            for e in which:
                block = dyp[inner_rows(t + 2 - ky, e * nb), r * wd : (r + 1) * wd]
                block = block.reshape(pairs, 2 * nb, wd)[:, 0:nb, :].reshape(pairs * nb, wd)
                cells.append(block)
        return jnp.concatenate(cells, axis=1)

    def transposed(t, carry):
        sums, bends = carry
        at = line_rows(t)
        done = []
        for r in range(d.radix):
            both = dot_nt(back_taps(t, r, (1, 2)), w2x[r])
            left = both[:, 0:gin] + dot_nt(back_taps(t, r, (0,)), w2l[r])
            right = both[:, gin:] + dot_nt(back_taps(t, r, (3,)), w2r[r])
            both = jnp.concatenate(
                [left.reshape(pairs, nb, gin), right.reshape(pairs, nb, gin)], axis=1
            )
            done.append(both.reshape(line, gin))
        dm[at, :] = jnp.concatenate(done, axis=1)

        def cells(u, carry):
            sums, bends = carry
            at = block_rows(t, u, step1)
            y = y1[at, :]
            _, slope = gate(y * half_a1 + half_b1)
            grad = dm[at, :] * (slope * mask_of(at, mid))
            dm[at, :] = grad
            mixed[at, :] = grad.astype(BF16)
            return sums + fold(grad), bends + fold(grad * y)

        return lax.fori_loop(0, line // step1, cells, (sums, bends))

    zeros = jnp.zeros((8, mid), F32)
    sums1 = lax.fori_loop(1, nh - 1, transposed, (zeros, zeros))
    halo2_recv()
    sums1 = edges(transposed, sums1)
    sum_grad = total_row(sums1[0])
    back1 = Everywhere("b1")
    put(back1.at, 0, sum_grad)
    put(back1.at, 2, scale1 * (total_row(sums1[1]) - mean1 * sum_grad))
    back1.start()

    acc_c[...] = jnp.zeros((wd, cin), F32)

    def first_weights(t, carry):
        at = line_rows(t)
        acc_c[...] += dot_tn(mixed[at, :], xv[at, :])
        return carry

    lax.fori_loop(0, nh, first_weights, 0)
    w_step(1, 1)
    w_step(3, 0)
    if d.inside:
        for c in range(2):
            parts[0][c] = acc_c[:, c * half : (c + 1) * half].astype(BF16)
    w_start(0, 0)
    got = back1.finish()
    bias1, gain1 = get(got, 0, mid), get(got, 2, mid)
    grow1 = g1[...] * scale1
    bias_all, gain_all = bias1 / wide(total, mid), gain1 / wide(total, mid)
    slant1 = grow1 * scale1 * gain_all
    level1 = grow1 * bias_all - mean1 * slant1
    w_step(0, 0)

    def dy_copy(t):
        return pltpu.make_async_copy(mixed.at[line_rows(t)], dy_hbm.at[line_rows(t)], sem_misc.at[t])

    def back_first(t, carry):
        def cells(u, carry):
            at = block_rows(t, u, step1)
            pull = mask_of(at, mid) * (level1 + slant1 * y1[at, :])
            mixed[at, :] = (grow1 * dm[at, :] - pull).astype(BF16)
            return carry

        lax.fori_loop(0, line // step1, cells, 0)
        dy_copy(t).start()
        return carry

    lax.fori_loop(0, nh, back_first, 0)
    put(small.at[0], 32, bias1)
    put(small.at[0], 34, gain1)
    put(small.at[0], 36, mean_act1)
    small[0, 18:20, :] = jnp.zeros((2, LANES), F32)
    small[0, 38:40, :] = jnp.zeros((2, LANES), F32)
    small[0, 44:48, :] = jnp.zeros((4, LANES), F32)
    got = misc.finish()
    put(small.at[0], 28, get(got, 4, wide2))
    put(small.at[0], 40, get(got, 0, wide2))
    got = v0_sum.finish()
    for c in range(2):
        v0[c] = jnp.broadcast_to(get(got, 0, cin)[:, c * half : (c + 1) * half], (8, half))
    for j, vector in enumerate((grow1, bias_all, gain_all)):
        cols[j] = jnp.transpose(jnp.broadcast_to(vector, (LANES, mid)))

    def norm_terms(total, at, taken, flat):
        lanes = total.shape[1]
        grow, level, slant = (wide(cols[j, at, :], lanes) for j in range(3))
        return grow * (total - level * flat - slant * taken)

    def fix_first(total):
        return norm_terms(total, z_at(z_of, spot * plane_rows), vres[...], v0[core, 0:1, :])

    w_step(1, 2)
    w_step(0, 1)
    w_step(3, 1)
    w_step(1, 3)
    w_step(0, 2, fix_first)
    w_step(3, 2)
    w_step(1, 4)
    w_step(0, 3)
    w_step(3, 3)
    w_step(0, 4)
    w_step(3, 4)
    w_step(2, 4)
    for s in (1, 0, 3, 2):
        w_step(s, 5)
    if not d.inside:
        whole = slice(0, wd)
        for c in range(2):
            lanes = slice(c * half, (c + 1) * half)
            local = wide(cols[0, whole, :], half) * (
                acc_c[:, lanes]
                - wide(cols[1, whole, :], half) * get(v0_sum.at[...], 0, cin)[:, lanes]
                - wide(cols[2, whole, :], half) * parts[4][c].astype(F32)
            )
            parts[0][c] = local.astype(BF16)

    results = tuple(enumerate((wg0_hbm, wg1_hbm, wg2_hbm, wg3_hbm)))
    for s, hbm in results:
        pltpu.make_async_copy((ress if d.inside else parts)[s], hbm, sem_misc.at[nh + s]).start()

    def finish(t, carry):
        dy_copy(t).wait()
        out_copy(t).wait()
        return carry

    lax.fori_loop(0, nh, finish, 0)
    for s in range(d.sets + 1):
        w_sent(s)
    halo1_sent()
    halo2_sent()
    for s, hbm in results:
        pltpu.make_async_copy((ress if d.inside else parts)[s], hbm, sem_misc.at[nh + s]).wait()


def call_block(d, args):
    f32, bf16 = F32, BF16
    cin, wd, mid, rows, nb, nh = d.cin, d.width, d.mid, d.rows, d.nb, d.nh
    vmem, dma = pltpu.VMEM, pltpu.SemaphoreType.DMA
    halves = [(2, wd, lanes) for lanes in d.half]
    shape = jax.ShapeDtypeStruct
    outs = [
        shape((rows, cin), bf16),
        shape((rows, cin), bf16),
        shape((rows, mid), bf16),
        *[shape(s, bf16) for s in halves[: d.sets]],
        shape((1, 48, LANES), f32),
    ]
    anywhere = pl.BlockSpec(memory_space=pl.ANY)
    inside = pl.BlockSpec(memory_space=pltpu.VMEM)
    plane, zed = wd // 4, wd // 16

    def sums_of(name, count):
        if not d.inside:
            return dict(
                src=vmem((count, LANES), f32),
                mid=vmem((count, LANES), f32),
                buf_ha=vmem((d.n_ha, count, LANES), f32),
                buf_img=vmem((d.n_img, count, LANES), f32),
                send_ha=dma((d.n_ha,)), recv_ha=dma((d.n_ha,)),
                send=dma((d.n_img,)), recv=dma((d.n_img,)),
            )
        if name in d.paired:
            return dict(
                src=vmem((count, LANES), f32),
                mid=vmem((count, LANES), f32),
                other=vmem((count, LANES), f32),
                buf=vmem((16, count, LANES), f32),
                send=dma((16,)), recv=dma((16,)),
            )
        return dict(
            src=vmem((count, LANES), f32),
            buf=vmem((32, count, LANES), f32),
            send=dma((32,)), recv=dma((32,)),
        )

    scratch = [
        vmem((rows, LANES), bf16),
        vmem((nb, LANES), f32),
        vmem((rows, cin), bf16),
        vmem((max(2 * rows, (nh + 2) * d.padded), cin // 2), bf16),
        vmem((rows, mid), f32),
        vmem(((nh + 2) * d.padded, mid), bf16),
        vmem((rows, d.wide), bf16),
        vmem((rows, d.wide), bf16),
        vmem((rows, d.wide), bf16),
        vmem((rows, wd), bf16),
        vmem((rows, cin), bf16),
        vmem((rows, wd), f32),
        vmem((wd, cin), f32),
        vmem((d.radix, wd, 9 * d.gin), f32),
        vmem((wd, cin), bf16),
        vmem((d.radix, 2 * d.gin, 6 * wd), bf16),
        vmem((d.radix, d.gin, 3 * wd), bf16),
        vmem((d.radix, d.gin, 3 * wd), bf16),
        vmem((nb, d.wide), f32),
        vmem((nb, d.wide), f32),
        vmem((nb, d.wide), f32),
        vmem((8, cin), f32),
        vmem((nb, wd), f32),
        vmem((2, 8, cin // 2), f32),
        vmem((3, mid, LANES), f32),
        [vmem(s, bf16) for s in halves],
        [vmem((wd, lanes), bf16) for lanes in d.half],
        [vmem((3, plane, lanes), bf16) for lanes in d.half],
        [vmem((3, zed, lanes), bf16) for lanes in d.half],
        [vmem((plane, lanes), bf16) for lanes in d.half],
        [vmem(s, bf16) for s in halves[: d.sets]],
        vmem((zed, d.half[0]), f32),
        {name: sums_of(name, count) for name, count in d.sums.items()},
        vmem((nb, d.wide), bf16),
        vmem((d.n_ha, nb, d.wide), bf16),
        vmem((nb, 2 * LANES), f32),
        vmem((d.n_ha, nb, 2 * LANES), f32),
        vmem((2, 4, LANES), f32),
        vmem((2, d.n_img, 4, LANES), f32),
        dma((nh,)),
        dma((2, nh)),
        dma((nh,)),
        dma((2, nh)),
        dma((nh + 4,)),
        dma((2, d.n_ha)),
        dma((2, d.n_ha)),
        dma((2, d.n_img)),
        dma((2, d.n_img)),
        dma((2, 2)),
        dma((2, 2)),
        dma((5, 24)),
        dma((5, 24)),
    ]
    return pl.pallas_call(
        functools.partial(block_kernel, d),
        out_shape=outs,
        in_specs=[anywhere, anywhere, inside, pl.BlockSpec(memory_space=pltpu.SMEM)] + [inside] * 14,
        out_specs=[anywhere] * 7 + [inside],
        scratch_shapes=scratch,
        name="block",
        compiler_params=pltpu.CompilerParams(
            collective_id=0, has_side_effects=True, vmem_limit_bytes=61 << 20
        ),
    )(*args)


def finish_kernel(
    d, out_in, dn_hbm, dy_hbm, w1_hbm, wg0_hbm, wg1_hbm, wg2_hbm, wg3_hbm, small_hbm,
    out, gin_hbm, gw1_hbm, gg1, gb1, gw2_hbm, gg2, gb2, gwsq, ggs, gbs, gwex, gbex, gw3_hbm, gg3, gb3,
    passing, dn, dy, w1, wg0, wg1, wg2, wg3, small, gw1, gw2, gw3, sem_in, sem_out, sem_w, sem_gw,
):
    nh, line, wd, taps = d.nh, d.line, d.width, 3 * d.gin

    def at(t):
        return pl.ds(t * line, line)

    def copy(t, which):
        src, dst = ((out_in, passing), (dn_hbm, dn), (dy_hbm, dy))[which]
        return pltpu.make_async_copy(src.at[at(t)], dst.at[at(t)], sem_in.at[which, t])

    def back(t, which):
        src, dst = ((passing, out), (dn, gin_hbm))[which]
        return pltpu.make_async_copy(src.at[at(t)], dst.at[at(t)], sem_out.at[which, t])

    loads = [
        pltpu.make_async_copy(src, dst, sem_w.at[j])
        for j, (src, dst) in enumerate(
            ((w1_hbm, w1), (small_hbm, small), (wg0_hbm, wg0), (wg2_hbm, wg2), (wg1_hbm, wg1), (wg3_hbm, wg3))
        )
    ]
    stores = [
        pltpu.make_async_copy(src, dst, sem_gw.at[j])
        for j, (src, dst) in enumerate(((gw1, gw1_hbm), (gw3, gw3_hbm), (gw2, gw2_hbm)))
    ]
    loads[0].start()
    for t in range(nh):
        for which in (1, 2, 0):
            copy(t, which).start()
        if t < 5:
            loads[t + 1].start()

    def weights(step):
        half = d.cin // 2
        if step == 0:
            loads[2].wait()
            loads[3].wait()
        elif step == 2:
            loads[1].wait()
            loads[4].wait()
            loads[5].wait()
        if step < 2:
            gw1[step * half : (step + 1) * half, :] = jnp.transpose(wg0[step].astype(F32))
            gw3[:, step * half : (step + 1) * half] = wg2[step].astype(F32)
        elif step < 4:
            r = step - 2
            rows = small[0]
            mean = get(rows, 36, d.mid)[:, r * d.gin : (r + 1) * d.gin]
            taken = get(rows, 40, d.wide)[:, r * wd : (r + 1) * wd]
            mean = jnp.transpose(jnp.broadcast_to(mean, (LANES, d.gin)))
            back = wide(mean, wd) * taken
            for tap in range(9):
                held, first = (wg1, 0) if tap < 6 else (wg3, 6)
                cells = held[r, :, (tap - first) * d.gin : (tap - first + 1) * d.gin]
                gw2[r, tap] = jnp.transpose(cells.astype(F32)) + back
        elif step == 4:
            cells = wg3[0, :, taps:].astype(F32)
            gwex[:, 0:wd] = cells[0 : d.inter, :]
            gwex[:, wd:] = cells[d.inter :, :]
            gwsq[...] = wg3[1, :, taps : taps + d.inter].astype(F32)
            rows = small[0]
            gb3[...] = get(rows, 0, d.cin)
            gg3[...] = get(rows, 8, d.cin)
            gbs[...] = rows[16:17, :]
            ggs[...] = rows[17:18, :]
            gb2[...] = get(rows, 20, d.wide)
            gg2[...] = get(rows, 24, d.wide)
            gbex[...] = get(rows, 28, d.wide)
            gb1[...] = get(rows, 32, d.mid)
            gg1[...] = get(rows, 34, d.mid)

    for t in range(max(nh, 5)):
        if t == 0:
            loads[0].wait()
        if t < nh:
            copy(t, 1).wait()
            copy(t, 2).wait()
            dn[at(t), :] = (dn[at(t), :].astype(F32) + dot_nt(dy[at(t), :], w1[...])).astype(BF16)
            back(t, 1).start()
            copy(t, 0).wait()
            back(t, 0).start()
        weights(t)
        if t == 1:
            stores[0].start()
            stores[1].start()
        elif t == 3:
            stores[2].start()
    for store in stores:
        store.wait()
    for t in range(nh):
        back(t, 0).wait()
        back(t, 1).wait()


def call_finish(d, out_in, dn, dy, w1, wg0, wg1, wg2, wg3, small):
    shape = jax.ShapeDtypeStruct
    cin, wd, mid = d.cin, d.width, d.mid
    vmem, dma = pltpu.VMEM, pltpu.SemaphoreType.DMA
    small_dims = [
        (cin, mid), (1, mid), (1, mid), (d.radix, 9, d.gin, wd), (1, d.wide), (1, d.wide), (wd, d.inter),
        (1, d.inter), (1, d.inter), (d.inter, d.wide), (1, d.wide), (wd, cin), (1, cin), (1, cin),
    ]
    anywhere = pl.BlockSpec(memory_space=pl.ANY)
    inside = pl.BlockSpec(memory_space=pltpu.VMEM)
    return pl.pallas_call(
        functools.partial(finish_kernel, d),
        out_shape=[shape((d.rows, cin), BF16), shape((d.rows, cin), BF16)]
        + [shape(s, F32) for s in small_dims],
        in_specs=[anywhere] * 9,
        out_specs=[anywhere] * 3 + [inside] * 2 + [anywhere] + [inside] * 7 + [anywhere] + [inside] * 2,
        scratch_shapes=[
            vmem((d.rows, cin), BF16), vmem((d.rows, cin), BF16), vmem((d.rows, mid), BF16),
            vmem((cin, mid), BF16), vmem(wg0.shape, BF16), vmem(wg1.shape, BF16), vmem(wg2.shape, BF16), vmem(wg3.shape, BF16),
            vmem(small.shape, F32), vmem((cin, mid), F32), vmem((d.radix, 9, d.gin, wd), F32), vmem((wd, cin), F32),
            dma((3, d.nh)), dma((2, d.nh)), dma((6,)), dma((3,)),
        ],
        name="finish",
        compiler_params=pltpu.CompilerParams(vmem_limit_bytes=60 << 20),
    )(out_in, dn, dy, w1, wg0, wg1, wg2, wg3, small)


def on_device(
    inputs, image_count, pixel_mask, w_first, gain_first, bias_first, w_group, gain_group, bias_group,
    w_squeeze, gain_squeeze, bias_squeeze, w_excite, bias_excite, w_last, gain_last, bias_last, cotangent,
):
    n_img, n_ha = lax.axis_size("img"), lax.axis_size("ha")
    d = Dims(n_img, n_ha, inputs.shape, w_group.shape, w_squeeze.shape)
    nb, nh, nw, cin = inputs.shape

    def by_rows(cells):
        return jnp.transpose(cells, (1, 2, 0, 3)).reshape(d.rows, cin)

    def by_image(cells):
        return jnp.transpose(cells.reshape(nh, nw, nb, cin), (2, 0, 1, 3))

    row = lambda v: v.reshape(1, -1)
    args = (
        by_rows(inputs), by_rows(cotangent), jnp.transpose(pixel_mask, (1, 0, 2)), image_count,
        w_first, row(gain_first), row(bias_first),
        w_group.reshape(d.radix, 9 * d.gin, d.width), row(gain_group), row(bias_group),
        w_squeeze, row(gain_squeeze), row(bias_squeeze), w_excite, row(bias_excite),
        w_last, row(gain_last), row(bias_last),
    )
    out, dn, dy, *sets, small = call_block(d, args)
    if not d.inside:
        sets = lax.psum(sets, ("img", "ha"))
    done = call_finish(d, out, dn, dy, w_first, *sets, small)
    (out, gin, gw1, gg1, gb1, gw2, gg2, gb2, gwsq, ggs, gbs, gwex, gbex, gw3, gg3, gb3) = done
    flat = lambda v: v.reshape(-1)
    return (
        by_image(out), by_image(gin), gw1, flat(gg1), flat(gb1), gw2.reshape(w_group.shape), flat(gg2), flat(gb2),
        gwsq, flat(ggs), flat(gbs), gwex, flat(gbex), gw3, flat(gg3), flat(gb3),
    )


def solution(mesh):
    cells = P("img", "ha", None, None)
    placed = (cells, P("img"), P("img", "ha", None)) + (P(),) * 14 + (cells,)
    return jax.shard_map(
        on_device,
        mesh=mesh,
        in_specs=placed,
        out_specs=(cells, cells) + (P(),) * 14,
        check_vma=False,
    )
```

time: 198 us -> 160 us (0.81)
  Pallas kernels: 192 us -> 157 us
  local copies, waits for them, and re-layouts: 2.52 us -> 0 us
    pallas_call x1, Pallas kernels: 175 us -> 144 us  [call_block(): pl.pallas_call(functools.partial(block_kernel, d), out_shape=outs, in_spe...]
    pallas_call x1, Pallas kernels: 16.8 us -> 12.4 us  [call_finish(): pl.pallas_call(functools.partial(finish_kernel, d), out_shape=[shape((d.r...]
    broadcast_in_dim x3 -> x0, local copies, waits for them, and re-layouts: 2.4 us -> none  [the longest x2 1.73 us: on_device(): valid = jnp.broadcast_to(valid, (d.rows, LANES))]
where the time goes in v2:
time: 160 us; the launch traced here: 158 us
  Pallas kernels  157 us (98%)
    pallas_call x1, Pallas kernels, call_block(): pl.pallas_call(functools.partial(block_kernel, d), out_shape=outs, in_spe...  144 us
    pallas_call x1, Pallas kernels, call_finish(): pl.pallas_call(functools.partial(finish_kernel, d), out_shape=[shape((d.r...  12.4 us

profile of v2, /device:TPU:0, one launch (start us, length us, event | category | flops | bytes accessed | tf_op | source)
XLA Modules:
  0.0 158.2 jit_solution(18045260450295336827)
XLA Ops:
  1.3 144.4 %block.1 = (bf16[3136,1024]{1,0:T(8,128)(2,1)}, bf16[3136,1024]{1,0:T(8,128)(2,1)}, bf16[3136,256]{1,0:T(8,128)(2,1)}, bf16[2,256,512]{2,1,0:T(8,128)(2,1)}, bf1...) custom-call(bf16[3136,1024]{1,0:T(8,128)(2,1)} %bitcast.33, ...), custom_call_target="tpu_custom_call" | custom-call | tf_op jit(solution)/shard_map/block/pallas_call | solution.py:1143
  145.7 12.4 %finish.1 = (bf16[3136,1024]{1,0:T(8,128)(2,1)}, bf16[3136,1024]{1,0:T(8,128)(2,1)}, f32[1024,256]{1,0:T(8,128)}, f32[1,256]{1,0:T(1,128)}, f32[1,256]{1,0:T(1,1...) custom-call(bf16[3136,1024]{1,0:T(8,128)(2,1)} %get-tuple-element.40, ...), custom_call_target="tpu_custom_call" | custom-call | tf_op jit(solution)/shard_map/finish/pallas_call | solution.py:1263

commit v3 on v2

--- a/solution.py
+++ b/solution.py
@@ -94,22 +94,24 @@
         self.inside = n_img == 8 and n_ha == 4
         self.sums = dict(cnt=4, s1=4, s2=8, act=4, v0=8, s3=16, b3=16, b2=8, misc=8, b1=4)
         self.paired = ("s3", "b3")
+        self.shared = dict(b1="s1", b2="s2")
 
 
 def block_kernel(
     d,
-    x_hbm, ct_hbm, mask_in, count_in, w1, g1, c1, w2, g2, c2, wsq, gs, cs, wex, bex, w3, g3, c3,
-    out_hbm, dn_hbm, dy_hbm, wg0_hbm, wg1_hbm, wg2_hbm, wg3_hbm, small,
-    mb, live, xv, ctv, y1, a1p, y2, act2, slope2, mixed, ost, dm, acc_c, acc_g, w3p, w2x, w2l, w2r,
-    att, q2, q4, vecs, pools, v0, cols,
-    parts, rcs, rxys, rzs, mids, ress, vres, sums, ga_src, ga_buf, pf_src, pf_buf, fc_src, fc_buf,
-    sem_x, sem_ct, sem_out, sem_dn, sem_misc, ssa, rsa, ssi, rsi, ssh, rsh, ssw, rsw,
+    x_hbm, ct_hbm, mask_in, count_in, w1_hbm, g1, c1, w2_hbm, g2, c2, wsq, gs, cs, wex, bex, w3_hbm, g3, c3,
+    dn_hbm, ost, xv, wg0, wg1, wg2, wg3, small,
+    w1, w2, w3, mb, live, ctv, y1, a1p, y2, act2, slope2, mixed, dm, acc_c, acc_g, w3p, w2x, w2l, w2r,
+    mix_t, att, q2, q4, vecs, pools, v0, cols,
+    parts, rcs, rxys, rzs, mids, vres, sums, ga_src, ga_buf, pf_src, pf_buf, fc_src, fc_buf,
+    sem_w, sem_x, sem_ct, sem_dn, sem_back, ssa, rsa, ssi, rsi, ssh, rsh, ssw, rsw,
 ):
     n_img, n_ha = d.n_img, d.n_ha
     nb, nh, nw = d.nb, d.nh, d.nw
     cin, mid, wd, wide2, line, rows = d.cin, d.mid, d.width, d.wide, d.line, d.rows
     gin, padded = d.gin, d.padded
     dyp = ctv
+    ress = (wg0, wg1, wg2, wg3)
     half = cin // 2
     i = lax.axis_index("img")
     h = lax.axis_index("ha")
@@ -165,7 +167,14 @@
         x_copy(t).start()
         return carry
 
+    loads = [
+        pltpu.make_async_copy(src, dst, sem_w.at[j])
+        for j, (src, dst) in enumerate(((w1_hbm, w1), (w2_hbm, w2), (w3_hbm, w3)))
+    ]
+    loads[0].start()
     lax.fori_loop(0, nh, start_inputs, 0)
+    loads[1].start()
+    loads[2].start()
 
     barrier = pltpu.get_barrier_semaphore()
     if d.inside:
@@ -247,7 +256,8 @@
 
     class Everywhere:
         def __init__(self, name):
-            self.at, refs = sums[name]["src"], sums[name]
+            refs = sums[d.shared.get(name, name)]
+            self.at = refs["src"]
             self.refs = refs
             if not d.inside:
                 return
@@ -441,12 +451,15 @@
         masked = y * mask_of(at, mid)
         return sums + fold(masked), squares + fold(masked * y)
 
+    loads[0].wait()
     zeros = jnp.zeros((8, mid), F32)
     totals, squares = lax.fori_loop(0, nh, first, (zeros, zeros))
     norm1 = Everywhere("s1")
     put(norm1.at, 0, total_row(totals))
     put(norm1.at, 2, total_row(squares))
     norm1.start()
+    loads[1].wait()
+    loads[2].wait()
     for r in range(d.radix):
         for ky in range(3):
             for e in range(4):
@@ -548,7 +561,7 @@
     half_b2 = 0.5 * c2[...] - half_a2 * mean2
 
     lane_blocks = wd // LANES
-    step2 = 4 * nb
+    step2 = (nw // 2) * nb
     zero = jnp.zeros((nb, LANES), F32)
     for j in range(lane_blocks):
         own = slice(j * LANES, (j + 1) * LANES)
@@ -624,10 +637,11 @@
             mixed[at, :] = (both[:, 0:wd] + both[:, wd:]).astype(BF16)
             return carry
 
-        lax.fori_loop(0, line // step3, cells, 0)
+        lax.fori_loop(0, line // step3, cells, 0, unroll=7)
         gram, sums = carry
         cells = mixed[line_rows(t), :]
-        return gram + dot_tn(cells, cells), sums + fold(cells.astype(F32))
+        mix_t[t] = jnp.transpose(cells)
+        return gram + dot(mix_t[t], cells), sums + fold(cells.astype(F32))
 
     gram, totals = lax.fori_loop(0, nh, mix, (jnp.zeros((wd, wd), F32), jnp.zeros((8, wd), F32)))
     mix_sum = total_row(totals)
@@ -657,15 +671,17 @@
     half_a3 = 0.5 * grow3
     half_b3 = 0.5 * c3[...] - half_a3 * mean3
 
-    step4 = 4 * nb
+    step4 = (nw // 4) * nb
     blocks4 = 2 * LANES
-
-    def out_copy(t):
-        return pltpu.make_async_copy(ost.at[line_rows(t)], out_hbm.at[line_rows(t)], sem_out.at[t])
 
     def dn_copy(t, c):
         return pltpu.make_async_copy(
             ctv.at[half_rows(t, c)], dn_hbm.at[line_rows(t), pl.ds(c * half, half)], sem_dn.at[c, t]
+        )
+
+    def dn_back(t, c):
+        return pltpu.make_async_copy(
+            dn_hbm.at[line_rows(t), pl.ds(c * half, half)], ctv.at[half_rows(t, c)], sem_back.at[c, t]
         )
 
     def grad_of(t):
@@ -697,10 +713,9 @@
                 return carry + fold(grad)
 
             vecs[:, lanes] = lax.fori_loop(0, line // step4, cells, vecs[:, lanes])
-        out_copy(t).start()
         dn_copy(t, 0).start()
         dn_copy(t, 1).start()
-        acc_c[...] += dot_tn(mixed[line_rows(t), :], grad_of(t))
+        acc_c[...] += dot(mix_t[t], grad_of(t))
         return carry
 
     lax.fori_loop(0, nh, last, 0)
@@ -851,7 +866,7 @@
                 sums.append(carry[r] + fold(push - pull))
             return tuple(sums)
 
-        return lax.fori_loop(0, line // step6, cells, carry)
+        return lax.fori_loop(0, line // step6, cells, carry, unroll=7)
 
     zeros = jnp.zeros((8, wd), F32)
     sums2 = edges(back_group, (zeros,) * d.radix)
@@ -865,14 +880,13 @@
     misc.start()
     w_step(2, 2)
 
-    def weights_group(first, last):
-        def body(t, carry):
-            for r in range(d.radix):
-                grad = dyp[inner_rows(t + 1), r * wd : (r + 1) * wd]
-                acc_g[r, :, first * gin : last * gin] += dot_tn(grad, taps(t, r, first, last))
-            return carry
-
-        lax.fori_loop(0, nh, body, 0)
+    def weights_group(t, carry):
+        for r in range(d.radix):
+            grad = jnp.transpose(dyp[inner_rows(t + 1), r * wd : (r + 1) * wd])
+            acc_g[r] += dot(grad, taps(t, r))
+        return carry
+
+    lax.fori_loop(0, nh, weights_group, 0)
 
     def send_group(s, first, last):
         lanes = (last - first) * gin
@@ -883,14 +897,12 @@
             parts[s][r, :, 0:lanes] = grad.astype(BF16)
         w_start(s, 0)
 
-    weights_group(0, 6)
     send_group(1, 0, 6)
     parts[3][0, :, 3 * gin :] = jnp.concatenate(
         [grad_excite[:, 0:wd], grad_excite[:, wd:]], axis=0
     ).astype(BF16) * jnp.asarray(1.0 / n_ha, BF16)
     parts[3][1, :, 3 * gin : 3 * gin + d.inter] = grad_squeeze.astype(BF16)
     parts[3][1, :, 3 * gin + d.inter :] = jnp.zeros((wd, wd - d.inter), BF16)
-    weights_group(6, 9)
     send_group(3, 6, 9)
     w_step(1, 0)
     w_step(2, 3)
@@ -941,6 +953,14 @@
     put(back1.at, 0, sum_grad)
     put(back1.at, 2, scale1 * (total_row(sums1[1]) - mean1 * sum_grad))
     back1.start()
+    halo2_sent()
+
+    def fetch_back(t, carry):
+        dn_back(t, 0).start()
+        dn_back(t, 1).start()
+        return carry
+
+    lax.fori_loop(0, nh, fetch_back, 0)
 
     acc_c[...] = jnp.zeros((wd, cin), F32)
 
@@ -964,9 +984,6 @@
     level1 = grow1 * bias_all - mean1 * slant1
     w_step(0, 0)
 
-    def dy_copy(t):
-        return pltpu.make_async_copy(mixed.at[line_rows(t)], dy_hbm.at[line_rows(t)], sem_misc.at[t])
-
     def back_first(t, carry):
         def cells(u, carry):
             at = block_rows(t, u, step1)
@@ -975,7 +992,6 @@
             return carry
 
         lax.fori_loop(0, line // step1, cells, 0)
-        dy_copy(t).start()
         return carry
 
     lax.fori_loop(0, nh, back_first, 0)
@@ -1002,8 +1018,19 @@
     def fix_first(total):
         return norm_terms(total, z_at(z_of, spot * plane_rows), vres[...], v0[core, 0:1, :])
 
+    def grad_inputs(t, carry):
+        at = line_rows(t)
+        for c in range(2):
+            lanes = slice(c * half, (c + 1) * half)
+            dn_back(t, c).wait()
+            grad = ctv[half_rows(t, c), :].astype(F32) + dot_nt(mixed[at, :], w1[lanes, :])
+            xv[at, lanes] = grad.astype(BF16)
+        return carry
+
+    lax.fori_loop(0, nh // 2, grad_inputs, 0)
     w_step(1, 2)
     w_step(0, 1)
+    lax.fori_loop(nh // 2, nh, grad_inputs, 0)
     w_step(3, 1)
     w_step(1, 3)
     w_step(0, 2, fix_first)
@@ -1027,22 +1054,12 @@
             )
             parts[0][c] = local.astype(BF16)
 
-    results = tuple(enumerate((wg0_hbm, wg1_hbm, wg2_hbm, wg3_hbm)))
-    for s, hbm in results:
-        pltpu.make_async_copy((ress if d.inside else parts)[s], hbm, sem_misc.at[nh + s]).start()
-
-    def finish(t, carry):
-        dy_copy(t).wait()
-        out_copy(t).wait()
-        return carry
-
-    lax.fori_loop(0, nh, finish, 0)
     for s in range(d.sets + 1):
         w_sent(s)
     halo1_sent()
-    halo2_sent()
-    for s, hbm in results:
-        pltpu.make_async_copy((ress if d.inside else parts)[s], hbm, sem_misc.at[nh + s]).wait()
+    if not d.inside:
+        for s in range(d.sets):
+            ress[s][...] = parts[s][...]
 
 
 def call_block(d, args):
@@ -1053,10 +1070,10 @@
     shape = jax.ShapeDtypeStruct
     outs = [
         shape((rows, cin), bf16),
-        shape((rows, cin), bf16),
-        shape((rows, mid), bf16),
-        *[shape(s, bf16) for s in halves[: d.sets]],
-        shape((1, 48, LANES), f32),
+        vmem((rows, cin), bf16),
+        vmem((rows, cin), bf16),
+        *[vmem(s, bf16) for s in halves[: d.sets]],
+        vmem((1, 48, LANES), f32),
     ]
     anywhere = pl.BlockSpec(memory_space=pl.ANY)
     inside = pl.BlockSpec(memory_space=pltpu.VMEM)
@@ -1087,9 +1104,11 @@
         )
 
     scratch = [
+        vmem((cin, mid), bf16),
+        vmem((d.radix, 9 * d.gin, wd), bf16),
+        vmem((wd, cin), bf16),
         vmem((rows, LANES), bf16),
         vmem((nb, LANES), f32),
-        vmem((rows, cin), bf16),
         vmem((max(2 * rows, (nh + 2) * d.padded), cin // 2), bf16),
         vmem((rows, mid), f32),
         vmem(((nh + 2) * d.padded, mid), bf16),
@@ -1097,7 +1116,6 @@
         vmem((rows, d.wide), bf16),
         vmem((rows, d.wide), bf16),
         vmem((rows, wd), bf16),
-        vmem((rows, cin), bf16),
         vmem((rows, wd), f32),
         vmem((wd, cin), f32),
         vmem((d.radix, wd, 9 * d.gin), f32),
@@ -1105,6 +1123,7 @@
         vmem((d.radix, 2 * d.gin, 6 * wd), bf16),
         vmem((d.radix, d.gin, 3 * wd), bf16),
         vmem((d.radix, d.gin, 3 * wd), bf16),
+        vmem((nh, wd, d.line), bf16),
         vmem((nb, d.wide), f32),
         vmem((nb, d.wide), f32),
         vmem((nb, d.wide), f32),
@@ -1117,20 +1136,19 @@
         [vmem((3, plane, lanes), bf16) for lanes in d.half],
         [vmem((3, zed, lanes), bf16) for lanes in d.half],
         [vmem((plane, lanes), bf16) for lanes in d.half],
-        [vmem(s, bf16) for s in halves[: d.sets]],
         vmem((zed, d.half[0]), f32),
-        {name: sums_of(name, count) for name, count in d.sums.items()},
+        {name: sums_of(name, count) for name, count in d.sums.items() if name not in d.shared},
         vmem((nb, d.wide), bf16),
         vmem((d.n_ha, nb, d.wide), bf16),
         vmem((nb, 2 * LANES), f32),
         vmem((d.n_ha, nb, 2 * LANES), f32),
         vmem((2, 4, LANES), f32),
         vmem((2, d.n_img, 4, LANES), f32),
+        dma((3,)),
         dma((nh,)),
         dma((2, nh)),
-        dma((nh,)),
         dma((2, nh)),
-        dma((nh + 4,)),
+        dma((2, nh)),
         dma((2, d.n_ha)),
         dma((2, d.n_ha)),
         dma((2, d.n_img)),
@@ -1143,60 +1161,39 @@
     return pl.pallas_call(
         functools.partial(block_kernel, d),
         out_shape=outs,
-        in_specs=[anywhere, anywhere, inside, pl.BlockSpec(memory_space=pltpu.SMEM)] + [inside] * 14,
-        out_specs=[anywhere] * 7 + [inside],
+        in_specs=[anywhere, anywhere, inside, pl.BlockSpec(memory_space=pltpu.SMEM)]
+        + [anywhere, inside, inside, anywhere] + [inside] * 7 + [anywhere, inside, inside],
+        out_specs=[anywhere] + [inside] * 7,
         scratch_shapes=scratch,
         name="block",
         compiler_params=pltpu.CompilerParams(
-            collective_id=0, has_side_effects=True, vmem_limit_bytes=61 << 20
+            collective_id=0, has_side_effects=True, vmem_limit_bytes=47 << 20
         ),
     )(*args)
 
 
 def finish_kernel(
-    d, out_in, dn_hbm, dy_hbm, w1_hbm, wg0_hbm, wg1_hbm, wg2_hbm, wg3_hbm, small_hbm,
+    d, out_in, gin_in, wg0, wg1, wg2, wg3, small,
     out, gin_hbm, gw1_hbm, gg1, gb1, gw2_hbm, gg2, gb2, gwsq, ggs, gbs, gwex, gbex, gw3_hbm, gg3, gb3,
-    passing, dn, dy, w1, wg0, wg1, wg2, wg3, small, gw1, gw2, gw3, sem_in, sem_out, sem_w, sem_gw,
+    gw1, gw2, gw3, sem_out, sem_gw,
 ):
-    nh, line, wd, taps = d.nh, d.line, d.width, 3 * d.gin
-
-    def at(t):
-        return pl.ds(t * line, line)
-
-    def copy(t, which):
-        src, dst = ((out_in, passing), (dn_hbm, dn), (dy_hbm, dy))[which]
-        return pltpu.make_async_copy(src.at[at(t)], dst.at[at(t)], sem_in.at[which, t])
-
-    def back(t, which):
-        src, dst = ((passing, out), (dn, gin_hbm))[which]
-        return pltpu.make_async_copy(src.at[at(t)], dst.at[at(t)], sem_out.at[which, t])
-
-    loads = [
-        pltpu.make_async_copy(src, dst, sem_w.at[j])
-        for j, (src, dst) in enumerate(
-            ((w1_hbm, w1), (small_hbm, small), (wg0_hbm, wg0), (wg2_hbm, wg2), (wg1_hbm, wg1), (wg3_hbm, wg3))
-        )
+    wd, taps = d.width, 3 * d.gin
+    parts = 4
+    copies = [
+        pltpu.make_async_copy(src.at[at], dst.at[at], sem_out.at[which, t])
+        for which, (src, dst) in enumerate(((out_in, out), (gin_in, gin_hbm)))
+        for t in range(parts)
+        for at in (pl.ds(t * (d.rows // parts), d.rows // parts),)
     ]
+    for copy in copies:
+        copy.start()
     stores = [
         pltpu.make_async_copy(src, dst, sem_gw.at[j])
         for j, (src, dst) in enumerate(((gw1, gw1_hbm), (gw3, gw3_hbm), (gw2, gw2_hbm)))
     ]
-    loads[0].start()
-    for t in range(nh):
-        for which in (1, 2, 0):
-            copy(t, which).start()
-        if t < 5:
-            loads[t + 1].start()
 
     def weights(step):
         half = d.cin // 2
-        if step == 0:
-            loads[2].wait()
-            loads[3].wait()
-        elif step == 2:
-            loads[1].wait()
-            loads[4].wait()
-            loads[5].wait()
         if step < 2:
             gw1[step * half : (step + 1) * half, :] = jnp.transpose(wg0[step].astype(F32))
             gw3[:, step * half : (step + 1) * half] = wg2[step].astype(F32)
@@ -1227,30 +1224,18 @@
             gb1[...] = get(rows, 32, d.mid)
             gg1[...] = get(rows, 34, d.mid)
 
-    for t in range(max(nh, 5)):
-        if t == 0:
-            loads[0].wait()
-        if t < nh:
-            copy(t, 1).wait()
-            copy(t, 2).wait()
-            dn[at(t), :] = (dn[at(t), :].astype(F32) + dot_nt(dy[at(t), :], w1[...])).astype(BF16)
-            back(t, 1).start()
-            copy(t, 0).wait()
-            back(t, 0).start()
+    for t in range(5):
         weights(t)
         if t == 1:
             stores[0].start()
             stores[1].start()
         elif t == 3:
             stores[2].start()
-    for store in stores:
-        store.wait()
-    for t in range(nh):
-        back(t, 0).wait()
-        back(t, 1).wait()
-
-
-def call_finish(d, out_in, dn, dy, w1, wg0, wg1, wg2, wg3, small):
+    for copy in stores + copies:
+        copy.wait()
+
+
+def call_finish(d, *args):
     shape = jax.ShapeDtypeStruct
     cin, wd, mid = d.cin, d.width, d.mid
     vmem, dma = pltpu.VMEM, pltpu.SemaphoreType.DMA
@@ -1264,17 +1249,15 @@
         functools.partial(finish_kernel, d),
         out_shape=[shape((d.rows, cin), BF16), shape((d.rows, cin), BF16)]
         + [shape(s, F32) for s in small_dims],
-        in_specs=[anywhere] * 9,
+        in_specs=[inside] * 7,
         out_specs=[anywhere] * 3 + [inside] * 2 + [anywhere] + [inside] * 7 + [anywhere] + [inside] * 2,
         scratch_shapes=[
-            vmem((d.rows, cin), BF16), vmem((d.rows, cin), BF16), vmem((d.rows, mid), BF16),
-            vmem((cin, mid), BF16), vmem(wg0.shape, BF16), vmem(wg1.shape, BF16), vmem(wg2.shape, BF16), vmem(wg3.shape, BF16),
-            vmem(small.shape, F32), vmem((cin, mid), F32), vmem((d.radix, 9, d.gin, wd), F32), vmem((wd, cin), F32),
-            dma((3, d.nh)), dma((2, d.nh)), dma((6,)), dma((3,)),
+            vmem((cin, mid), F32), vmem((d.radix, 9, d.gin, wd), F32), vmem((wd, cin), F32),
+            dma((2, 4)), dma((3,)),
         ],
         name="finish",
-        compiler_params=pltpu.CompilerParams(vmem_limit_bytes=60 << 20),
-    )(out_in, dn, dy, w1, wg0, wg1, wg2, wg3, small)
+        compiler_params=pltpu.CompilerParams(vmem_limit_bytes=16 << 20),
+    )(*[pltpu.with_memory_space_constraint(arg, pltpu.VMEM) for arg in args])
 
 
 def on_device(
@@ -1299,10 +1282,10 @@
         w_squeeze, row(gain_squeeze), row(bias_squeeze), w_excite, row(bias_excite),
         w_last, row(gain_last), row(bias_last),
     )
-    out, dn, dy, *sets, small = call_block(d, args)
+    _, out, gin, *sets, small = call_block(d, args)
     if not d.inside:
         sets = lax.psum(sets, ("img", "ha"))
-    done = call_finish(d, out, dn, dy, w_first, *sets, small)
+    done = call_finish(d, out, gin, *sets, small)
     (out, gin, gw1, gg1, gb1, gw2, gg2, gb2, gwsq, ggs, gbs, gwex, gbex, gw3, gg3, gb3) = done
     flat = lambda v: v.reshape(-1)
     return (

time: 160 us -> 150 us (0.938); the launches traced: 158 us -> 150 us
  Pallas kernels: 157 us -> 148 us
    pallas_call x1, Pallas kernels: 12.4 us -> 6.94 us  [call_finish(): pl.pallas_call(functools.partial(finish_kernel, d), out_shape=[shape((d.r...]
    pallas_call x1, Pallas kernels: 144 us -> 141 us  [call_block(): pl.pallas_call(functools.partial(block_kernel, d), out_shape=outs, in_spe...]
where the time goes in v3:
time: 150 us
  Pallas kernels  148 us (99%)
    pallas_call x1, Pallas kernels, call_block(): pl.pallas_call(functools.partial(block_kernel, d), out_shape=outs, in_spe...  141 us
    pallas_call x1, Pallas kernels, call_finish(): pl.pallas_call(functools.partial(finish_kernel, d), out_shape=[shape((d.r...  6.94 us

profile of v3, /device:TPU:0, one launch (start us, length us, event | category | flops | bytes accessed | tf_op | source)
XLA Modules:
  0.0 149.9 jit_solution(17854555862850604500)
XLA Ops:
  1.3 141.5 %block.1 = (bf16[3136,1024]{1,0:T(8,128)(2,1)}, bf16[3136,1024]{1,0:T(8,128)(2,1)S(1)}, bf16[3136,1024]{1,0:T(8,128)(2,1)S(1)}, bf16[2,256,512]{2,1,0:T(8,128)(2...) custom-call(bf16[3136,1024]{1,0:T(8,128)(2,1)} %bitcast.33, ...), custom_call_target="tpu_custom_call" | custom-call | tf_op jit(solution)/shard_map/block/pallas_call | solution.py:1161
  142.8 6.9 %finish.1 = (bf16[3136,1024]{1,0:T(8,128)(2,1)}, bf16[3136,1024]{1,0:T(8,128)(2,1)}, f32[1024,256]{1,0:T(8,128)}, f32[1,256]{1,0:T(1,128)}, f32[1,256]{1,0:T(1,1...) custom-call(bf16[3136,1024]{1,0:T(8,128)(2,1)S(1)} %get-tuple-elemen, ...), custom_call_target="tpu_custom_call" | custom-call | tf_op jit(solution)/shard_map/finish/pallas_call | solution.py:1248

commit v4 on v3

--- a/solution.py
+++ b/solution.py
@@ -89,8 +89,9 @@
         self.line = self.nw * self.nb
         self.rows = self.nh * self.line
         self.padded = (self.nw + 2) * self.nb
-        self.half = (self.cin // 2, 6 * self.gin, self.cin // 2, 3 * self.gin + self.width, self.cin // 2)
-        self.sets = 4
+        self.split = 5
+        self.half = (self.cin // 2, 5 * self.gin, self.cin // 2, 4 * self.gin, self.width, self.cin // 2)
+        self.sets = 5
         self.inside = n_img == 8 and n_ha == 4
         self.sums = dict(cnt=4, s1=4, s2=8, act=4, v0=8, s3=16, b3=16, b2=8, misc=8, b1=4)
         self.paired = ("s3", "b3")
@@ -100,7 +101,7 @@
 def block_kernel(
     d,
     x_hbm, ct_hbm, mask_in, count_in, w1_hbm, g1, c1, w2_hbm, g2, c2, wsq, gs, cs, wex, bex, w3_hbm, g3, c3,
-    dn_hbm, ost, xv, wg0, wg1, wg2, wg3, small,
+    dn_hbm, ost, xv, wg0, wg1, wg2, wg3, wg4, small,
     w1, w2, w3, mb, live, ctv, y1, a1p, y2, act2, slope2, mixed, dm, acc_c, acc_g, w3p, w2x, w2l, w2r,
     mix_t, att, q2, q4, vecs, pools, v0, cols,
     parts, rcs, rxys, rzs, mids, vres, sums, ga_src, ga_buf, pf_src, pf_buf, fc_src, fc_buf,
@@ -111,7 +112,7 @@
     cin, mid, wd, wide2, line, rows = d.cin, d.mid, d.width, d.wide, d.line, d.rows
     gin, padded = d.gin, d.padded
     dyp = ctv
-    ress = (wg0, wg1, wg2, wg3)
+    ress = (wg0, wg1, wg2, wg3, wg4)
     half = cin // 2
     i = lax.axis_index("img")
     h = lax.axis_index("ha")
@@ -222,7 +223,6 @@
         lax.fori_loop(0, nw + 2, edge, 0)
 
     clear(a1p)
-    pl.semaphore_wait(barrier, len(peers))
 
     def swap(src, buf, send, recv, peer, n):
         def copy(k):
@@ -434,12 +434,6 @@
                 for k in w_ks(stage):
                     w_copy(s, stage, k).wait_send()
 
-    count = Everywhere("cnt")
-    count.at[...] = jnp.zeros((4, LANES), F32)
-    count.at[0:1, :] = total_row(pixels)
-    count.at[1:2, :] = total_row(live[...]) * (1.0 / n_ha)
-    count.start()
-
     def first(t, carry):
         sums, squares = carry
         x_copy(t).wait()
@@ -454,10 +448,16 @@
     loads[0].wait()
     zeros = jnp.zeros((8, mid), F32)
     totals, squares = lax.fori_loop(0, nh, first, (zeros, zeros))
+    pl.semaphore_wait(barrier, len(peers))
+    count = Everywhere("cnt")
+    count.at[...] = jnp.zeros((4, LANES), F32)
+    count.at[0:1, :] = total_row(pixels)
+    count.at[1:2, :] = total_row(live[...]) * (1.0 / n_ha)
     norm1 = Everywhere("s1")
     put(norm1.at, 0, total_row(totals))
     put(norm1.at, 2, total_row(squares))
     norm1.start()
+    count.start()
     loads[1].wait()
     loads[2].wait()
     for r in range(d.radix):
@@ -551,8 +551,8 @@
     lax.fori_loop(0, nh, norm_products, 0)
     norm2_done = norm2.finish()
     for c in range(2):
-        parts[4][c] = acc_c[:, c * half : (c + 1) * half].astype(BF16)
-    w_start(4, 0)
+        parts[5][c] = acc_c[:, c * half : (c + 1) * half].astype(BF16)
+    w_start(5, 0)
     v0_sum = Everywhere("v0")
     put(v0_sum.at, 0, vecs[0:1, :])
     v0_sum.start()
@@ -606,7 +606,7 @@
     total_blocks = d.radix * lane_blocks
     for block in range(total_blocks // 4):
         slopes(block)
-    w_step(4, 0)
+    w_step(5, 0)
     both = pf_finish()
     floor = jnp.maximum(both[:, d.inter :], 1.0)
     squeezed = both[:, 0 : d.inter] / floor
@@ -664,7 +664,7 @@
         return carry
 
     lax.fori_loop(0, nh, last_product, 0)
-    w_step(4, 1)
+    w_step(5, 1)
     got = norm3.finish()
     mean3, scale3 = moments(get(got, 0, cin), get(got, 8, cin), wide(total, cin))
     grow3 = g3[...] * scale3
@@ -732,7 +732,7 @@
         return carry
 
     lax.fori_loop(0, nh, plain_back, 0)
-    w_finish(4, 2)
+    w_finish(5, 2)
     got = back3.finish()
     bias3, gain3 = get(got, 0, cin), get(got, 8, cin)
     put(small.at[0], 0, bias3)
@@ -816,7 +816,6 @@
     w_step(2, 0)
     grad_excite = dot_tn(hidden, grad_logits, HIGH)
     grad_bex = total_row(grad_logits) * (1.0 / n_ha)
-    acc_g[...] = jnp.zeros((d.radix, wd, 9 * gin), F32)
     got = fc_finish()
     bias_s, gain_s = got[0:1, :], got[1:2, :]
     put(small.at[0], 16, bias_s)
@@ -837,8 +836,16 @@
     grow2 = g2[...] * scale2
     att[...] = weight * grow2
     q2[...] = pool2 * grow2
+    parts[4][0] = jnp.concatenate([grad_excite[:, 0:wd], grad_excite[:, wd:]], axis=0).astype(
+        BF16
+    ) * jnp.asarray(1.0 / n_ha, BF16)
+    parts[4][1, :, 0 : d.inter] = grad_squeeze.astype(BF16)
+    parts[4][1, :, d.inter :] = jnp.zeros((wd, wd - d.inter), BF16)
+    w_start(4, 0)
     w_step(2, 1)
+    acc_g[...] = jnp.zeros((d.radix, wd, 9 * gin), F32)
     mean_act1 = get(act_sum.finish(), 0, mid) / (wide(images, mid) * float(nh * n_ha * nw))
+    w_step(4, 0)
     got = back2.finish()
     bias2, gain2 = get(got, 0, wide2), get(got, 4, wide2)
     put(small.at[0], 20, bias2)
@@ -879,6 +886,7 @@
     put(misc.at, 4, grad_bex)
     misc.start()
     w_step(2, 2)
+    w_step(4, 1)
 
     def weights_group(t, carry):
         for r in range(d.radix):
@@ -897,15 +905,10 @@
             parts[s][r, :, 0:lanes] = grad.astype(BF16)
         w_start(s, 0)
 
-    send_group(1, 0, 6)
-    parts[3][0, :, 3 * gin :] = jnp.concatenate(
-        [grad_excite[:, 0:wd], grad_excite[:, wd:]], axis=0
-    ).astype(BF16) * jnp.asarray(1.0 / n_ha, BF16)
-    parts[3][1, :, 3 * gin : 3 * gin + d.inter] = grad_squeeze.astype(BF16)
-    parts[3][1, :, 3 * gin + d.inter :] = jnp.zeros((wd, wd - d.inter), BF16)
-    send_group(3, 6, 9)
-    w_step(1, 0)
+    send_group(1, 0, d.split)
+    send_group(3, d.split, 9)
     w_step(2, 3)
+    w_step(4, 2)
 
     pairs = nw // 2
 
@@ -945,7 +948,12 @@
         return lax.fori_loop(0, line // step1, cells, (sums, bends))
 
     zeros = jnp.zeros((8, mid), F32)
-    sums1 = lax.fori_loop(1, nh - 1, transposed, (zeros, zeros))
+    middle = 1 + (nh - 2) // 3
+    sums1 = lax.fori_loop(1, middle, transposed, (zeros, zeros))
+    w_step(1, 0)
+    w_step(3, 0)
+    sums1 = lax.fori_loop(middle, nh - 1, transposed, sums1)
+    w_step(4, 3)
     halo2_recv()
     sums1 = edges(transposed, sums1)
     sum_grad = total_row(sums1[0])
@@ -970,19 +978,21 @@
         return carry
 
     lax.fori_loop(0, nh, first_weights, 0)
-    w_step(1, 1)
-    w_step(3, 0)
     if d.inside:
         for c in range(2):
             parts[0][c] = acc_c[:, c * half : (c + 1) * half].astype(BF16)
     w_start(0, 0)
+    w_step(1, 1)
+    w_step(0, 0)
+    w_step(3, 1)
     got = back1.finish()
     bias1, gain1 = get(got, 0, mid), get(got, 2, mid)
     grow1 = g1[...] * scale1
     bias_all, gain_all = bias1 / wide(total, mid), gain1 / wide(total, mid)
     slant1 = grow1 * scale1 * gain_all
     level1 = grow1 * bias_all - mean1 * slant1
-    w_step(0, 0)
+    w_step(2, 4)
+    w_step(4, 4)
 
     def back_first(t, carry):
         def cells(u, carry):
@@ -1027,21 +1037,19 @@
             xv[at, lanes] = grad.astype(BF16)
         return carry
 
+    w_step(1, 2)
     lax.fori_loop(0, nh // 2, grad_inputs, 0)
-    w_step(1, 2)
+    w_step(3, 2)
     w_step(0, 1)
+    w_step(1, 3)
+    w_step(3, 3)
+    w_step(0, 2, fix_first)
     lax.fori_loop(nh // 2, nh, grad_inputs, 0)
-    w_step(3, 1)
-    w_step(1, 3)
-    w_step(0, 2, fix_first)
-    w_step(3, 2)
     w_step(1, 4)
     w_step(0, 3)
-    w_step(3, 3)
+    w_step(3, 4)
     w_step(0, 4)
-    w_step(3, 4)
-    w_step(2, 4)
-    for s in (1, 0, 3, 2):
+    for s in (2, 4, 1, 3, 0):
         w_step(s, 5)
     if not d.inside:
         whole = slice(0, wd)
@@ -1050,7 +1058,7 @@
             local = wide(cols[0, whole, :], half) * (
                 acc_c[:, lanes]
                 - wide(cols[1, whole, :], half) * get(v0_sum.at[...], 0, cin)[:, lanes]
-                - wide(cols[2, whole, :], half) * parts[4][c].astype(F32)
+                - wide(cols[2, whole, :], half) * parts[5][c].astype(F32)
             )
             parts[0][c] = local.astype(BF16)
 
@@ -1155,15 +1163,15 @@
         dma((2, d.n_img)),
         dma((2, 2)),
         dma((2, 2)),
-        dma((5, 24)),
-        dma((5, 24)),
+        dma((6, 24)),
+        dma((6, 24)),
     ]
     return pl.pallas_call(
         functools.partial(block_kernel, d),
         out_shape=outs,
         in_specs=[anywhere, anywhere, inside, pl.BlockSpec(memory_space=pltpu.SMEM)]
         + [anywhere, inside, inside, anywhere] + [inside] * 7 + [anywhere, inside, inside],
-        out_specs=[anywhere] + [inside] * 7,
+        out_specs=[anywhere] + [inside] * 8,
         scratch_shapes=scratch,
         name="block",
         compiler_params=pltpu.CompilerParams(
@@ -1173,11 +1181,11 @@
 
 
 def finish_kernel(
-    d, out_in, gin_in, wg0, wg1, wg2, wg3, small,
+    d, out_in, gin_in, wg0, wg1, wg2, wg3, wg4, small,
     out, gin_hbm, gw1_hbm, gg1, gb1, gw2_hbm, gg2, gb2, gwsq, ggs, gbs, gwex, gbex, gw3_hbm, gg3, gb3,
     gw1, gw2, gw3, sem_out, sem_gw,
 ):
-    wd, taps = d.width, 3 * d.gin
+    wd = d.width
     parts = 4
     copies = [
         pltpu.make_async_copy(src.at[at], dst.at[at], sem_out.at[which, t])
@@ -1205,14 +1213,14 @@
             mean = jnp.transpose(jnp.broadcast_to(mean, (LANES, d.gin)))
             back = wide(mean, wd) * taken
             for tap in range(9):
-                held, first = (wg1, 0) if tap < 6 else (wg3, 6)
+                held, first = (wg1, 0) if tap < d.split else (wg3, d.split)
                 cells = held[r, :, (tap - first) * d.gin : (tap - first + 1) * d.gin]
                 gw2[r, tap] = jnp.transpose(cells.astype(F32)) + back
         elif step == 4:
-            cells = wg3[0, :, taps:].astype(F32)
+            cells = wg4[0].astype(F32)
             gwex[:, 0:wd] = cells[0 : d.inter, :]
             gwex[:, wd:] = cells[d.inter :, :]
-            gwsq[...] = wg3[1, :, taps : taps + d.inter].astype(F32)
+            gwsq[...] = wg4[1, :, 0 : d.inter].astype(F32)
             rows = small[0]
             gb3[...] = get(rows, 0, d.cin)
             gg3[...] = get(rows, 8, d.cin)
@@ -1249,7 +1257,7 @@
         functools.partial(finish_kernel, d),
         out_shape=[shape((d.rows, cin), BF16), shape((d.rows, cin), BF16)]
         + [shape(s, F32) for s in small_dims],
-        in_specs=[inside] * 7,
+        in_specs=[inside] * 8,
         out_specs=[anywhere] * 3 + [inside] * 2 + [anywhere] + [inside] * 7 + [anywhere] + [inside] * 2,
         scratch_shapes=[
             vmem((cin, mid), F32), vmem((d.radix, 9, d.gin, wd), F32), vmem((wd, cin), F32),

time: 150 us -> 144 us (0.960)
  Pallas kernels: 148 us -> 142 us
    pallas_call x1, Pallas kernels: 141 us -> 135 us  [call_block(): pl.pallas_call(functools.partial(block_kernel, d), out_shape=outs, in_spe...]
where the time goes in v4:
time: 144 us; the launch traced here: 143 us
  Pallas kernels  142 us (99%)
  between operations  1.47 us (1%)
    pallas_call x1, Pallas kernels, call_block(): pl.pallas_call(functools.partial(block_kernel, d), out_shape=outs, in_spe...  135 us
    pallas_call x1, Pallas kernels, call_finish(): pl.pallas_call(functools.partial(finish_kernel, d), out_shape=[shape((d.r...  7.3 us

profile of v4, /device:TPU:0, one launch (start us, length us, event | category | flops | bytes accessed | tf_op | source)
XLA Modules:
  0.0 143.5 jit_solution(8243879313920315131)
XLA Ops:
  1.3 134.7 %block.1 = (bf16[3136,1024]{1,0:T(8,128)(2,1)}, bf16[3136,1024]{1,0:T(8,128)(2,1)S(1)}, bf16[3136,1024]{1,0:T(8,128)(2,1)S(1)}, bf16[2,256,512]{2,1,0:T(8,128)(2...) custom-call(bf16[3136,1024]{1,0:T(8,128)(2,1)} %bitcast.33, ...), custom_call_target="tpu_custom_call" | custom-call | tf_op jit(solution)/shard_map/block/pallas_call | solution.py:1169
  136.0 7.3 %finish.1 = (bf16[3136,1024]{1,0:T(8,128)(2,1)}, bf16[3136,1024]{1,0:T(8,128)(2,1)}, f32[1024,256]{1,0:T(8,128)}, f32[1,256]{1,0:T(1,128)}, f32[1,256]{1,0:T(1,1...) custom-call(bf16[3136,1024]{1,0:T(8,128)(2,1)S(1)} %get-tuple-elemen, ...), custom_call_target="tpu_custom_call" | custom-call | tf_op jit(solution)/shard_map/finish/pallas_call | solution.py:1256

commit v5 on v4

--- a/solution.py
+++ b/solution.py
@@ -76,6 +76,18 @@
 def split_bf16(cells):
     high = cells.astype(BF16)
     return high, (cells - high.astype(F32)).astype(BF16)
+
+
+def thirds(cells):
+    high = cells.astype(BF16)
+    rest = cells - high.astype(F32)
+    middle = rest.astype(BF16)
+    return jnp.concatenate([high, middle, (rest - middle.astype(F32)).astype(BF16)], axis=0)
+
+
+def add_thirds(cells):
+    rows = cells.shape[0] // 3
+    return cells[0:rows] + cells[rows : 2 * rows] + cells[2 * rows :]
 
 
 class Dims:
@@ -94,7 +106,8 @@
         self.sets = 5
         self.inside = n_img == 8 and n_ha == 4
         self.sums = dict(cnt=4, s1=4, s2=8, act=4, v0=8, s3=16, b3=16, b2=8, misc=8, b1=4)
-        self.paired = ("s3", "b3")
+        self.paired = ("s3",)
+        self.narrow = ("b3",)
         self.shared = dict(b1="s1", b2="s2")
 
 
@@ -103,7 +116,7 @@
     x_hbm, ct_hbm, mask_in, count_in, w1_hbm, g1, c1, w2_hbm, g2, c2, wsq, gs, cs, wex, bex, w3_hbm, g3, c3,
     dn_hbm, ost, xv, wg0, wg1, wg2, wg3, wg4, small,
     w1, w2, w3, mb, live, ctv, y1, a1p, y2, act2, slope2, mixed, dm, acc_c, acc_g, w3p, w2x, w2l, w2r,
-    mix_t, att, q2, q4, vecs, pools, v0, cols,
+    mix_t, rows16, att, q2, q4, vecs, pools, v0, cols,
     parts, rcs, rxys, rzs, mids, vres, sums, ga_src, ga_buf, pf_src, pf_buf, fc_src, fc_buf,
     sem_w, sem_x, sem_ct, sem_dn, sem_back, ssa, rsa, ssi, rsi, ssh, rsh, ssw, rsw,
 ):
@@ -447,17 +460,18 @@
 
     loads[0].wait()
     zeros = jnp.zeros((8, mid), F32)
-    totals, squares = lax.fori_loop(0, nh, first, (zeros, zeros))
+    sums0 = lax.fori_loop(0, nh // 2, first, (zeros, zeros))
     pl.semaphore_wait(barrier, len(peers))
     count = Everywhere("cnt")
     count.at[...] = jnp.zeros((4, LANES), F32)
     count.at[0:1, :] = total_row(pixels)
     count.at[1:2, :] = total_row(live[...]) * (1.0 / n_ha)
+    count.start()
+    totals, squares = lax.fori_loop(nh // 2, nh, first, sums0)
     norm1 = Everywhere("s1")
     put(norm1.at, 0, total_row(totals))
     put(norm1.at, 2, total_row(squares))
     norm1.start()
-    count.start()
     loads[1].wait()
     loads[2].wait()
     for r in range(d.radix):
@@ -581,9 +595,7 @@
         pools[:, own] = lax.fori_loop(0, rows // step2, act_group, zero)
 
     pool = pools[...]
-    squeeze = wsq[...].astype(F32)
-    excite = wex[...].astype(F32)
-    pf_src[:, 0 : d.inter] = dot(pool, squeeze, HIGH)
+    pf_src[:, 0 : d.inter] = add_thirds(dot(thirds(pool), wsq[...]))
     pf_src[:, d.inter :] = pixels
     pf_start, pf_finish = swap(pf_src, pf_buf, ssa.at[0], rsa.at[0], ha_peer, n_ha)
     pf_start()
@@ -622,7 +634,7 @@
     mean_s, scale_s = moments(got[0:1, :], got[1:2, :], images)
     centered = (squeezed - mean_s) * scale_s
     hidden, hidden_slope = gate(0.5 * (centered * gs[...] + cs[...]))
-    logits = dot(hidden, excite, HIGH) + bex[...]
+    logits = add_thirds(dot(thirds(hidden), wex[...])) + bex[...]
     gap = logits[:, 0:wd] - logits[:, wd:]
     att[:, 0:wd] = jax.nn.sigmoid(gap)
     att[:, wd:] = jax.nn.sigmoid(-gap)
@@ -647,12 +659,11 @@
     mix_sum = total_row(totals)
     gram_high, gram_low = split_bf16(gram)
     acc_g[0, :, 0:cin] = dot(gram_high, w3[...]) + dot(gram_low, w3[...])
-    mix_high, mix_low = split_bf16(mix_sum)
-    sum_last = dot(jnp.broadcast_to(mix_high, (16, wd)), w3[...]) + dot(
-        jnp.broadcast_to(mix_low, (16, wd)), w3[...]
-    )
+    mix_parts = [jnp.broadcast_to(part, (16, wd)) for part in split_bf16(mix_sum)]
+    sum_last = dot(jnp.concatenate(mix_parts, axis=0), w3[...])
+    sum_last = sum_last[0:1, :] + sum_last[16:17, :]
     norm3 = Everywhere("s3")
-    put(norm3.at, 0, sum_last[0:1, :])
+    put(norm3.at, 0, sum_last)
     put(norm3.at, 8, total_row(acc_g[0, :, 0:cin] * w3[...].astype(F32)))
     norm3.start()
 
@@ -721,8 +732,9 @@
     lax.fori_loop(0, nh, last, 0)
     sum_grad = total_row(vecs[...])
     back3 = Everywhere("b3")
-    put(back3.at, 0, sum_grad)
-    put(back3.at, 8, scale3 * (total_row(acc_c[...] * w3[...].astype(F32)) - mean3 * sum_grad))
+    put(rows16, 0, sum_grad)
+    put(rows16, 8, scale3 * (total_row(acc_c[...] * w3[...].astype(F32)) - mean3 * sum_grad))
+    back3.at[...] = rows16[...].astype(BF16)
     back3.start()
 
     w3p[...] = (w3[...].astype(F32) * grow3).astype(BF16)
@@ -741,12 +753,11 @@
     slant3 = scale3 * gain3 / all_wide
     level3 = bias3 / all_wide - mean3 * slant3
     fix = (w3[...].astype(F32) * slant3).astype(BF16)
-    fix = dot_nt(fix, w3p[...]).astype(BF16)
     level_high, level_low = split_bf16(level3)
-    shift = dot_nt(jnp.broadcast_to(level_high, (16, cin)), w3p[...]) + dot_nt(
-        jnp.broadcast_to(level_low, (16, cin)), w3p[...]
-    )
-    shift = shift[0:1, :]
+    levels = [jnp.broadcast_to(part, (16, cin)) for part in (level_high, level_low)]
+    stack = dot_nt(jnp.concatenate([fix, *levels], axis=0), w3p[...])
+    fix = stack[0:wd, :].astype(BF16)
+    shift = stack[wd : wd + 1, :] + stack[wd + 16 : wd + 17, :]
 
     def back_mix(t, carry):
         at = line_rows(t)
@@ -806,7 +817,7 @@
     weighed = weight * grad_att
     both = weighed[:, 0:wd] + weighed[:, wd:]
     grad_logits = weight * (grad_att - jnp.concatenate([both, both], axis=1))
-    grad_fc = dot_nt(grad_logits, excite, HIGH) * hidden_slope
+    grad_fc = add_thirds(dot_nt(thirds(grad_logits), wex[...])) * hidden_slope
     put(fc_src.at[1], 0, total_row(grad_fc))
     put(fc_src.at[1], 1, total_row(grad_fc * centered))
     pooled = pool / wide(floor, wd)
@@ -823,7 +834,7 @@
     grad_squeezed = (gs[...] * scale_s) * (
         grad_fc - live_now * (bias_s + centered * gain_s) / images
     )
-    grad_pool = dot_nt(grad_squeezed, squeeze, HIGH) / wide(floor, wd)
+    grad_pool = add_thirds(dot_nt(thirds(grad_squeezed), wsq[...])) / wide(floor, wd)
     pool2 = jnp.concatenate([grad_pool] * d.radix, axis=1)
     sum_grad = total_row(weight * q1 + pool2 * q2[...])
     sum_bend = total_row(weight * q3 + pool2 * q4[...])
@@ -836,6 +847,14 @@
     grow2 = g2[...] * scale2
     att[...] = weight * grow2
     q2[...] = pool2 * grow2
+    def first_slopes(t, carry):
+        at = pl.ds(pl.multiple_of(t * step1, step1), step1)
+        _, slope = gate(y1[at, :] * half_a1 + half_b1)
+        mixed[at, :] = (slope * mask_of(at, mid)).astype(BF16)
+        return carry
+
+    lax.fori_loop(0, rows // step1, first_slopes, 0)
+
     parts[4][0] = jnp.concatenate([grad_excite[:, 0:wd], grad_excite[:, wd:]], axis=0).astype(
         BF16
     ) * jnp.asarray(1.0 / n_ha, BF16)
@@ -938,12 +957,10 @@
         def cells(u, carry):
             sums, bends = carry
             at = block_rows(t, u, step1)
-            y = y1[at, :]
-            _, slope = gate(y * half_a1 + half_b1)
-            grad = dm[at, :] * (slope * mask_of(at, mid))
+            grad = dm[at, :] * mixed[at, :].astype(F32)
             dm[at, :] = grad
             mixed[at, :] = grad.astype(BF16)
-            return sums + fold(grad), bends + fold(grad * y)
+            return sums + fold(grad), bends + fold(grad * y1[at, :])
 
         return lax.fori_loop(0, line // step1, cells, (sums, bends))
 
@@ -1088,26 +1105,27 @@
     plane, zed = wd // 4, wd // 16
 
     def sums_of(name, count):
+        kind = bf16 if name in d.narrow else f32
         if not d.inside:
             return dict(
-                src=vmem((count, LANES), f32),
+                src=vmem((count, LANES), kind),
                 mid=vmem((count, LANES), f32),
-                buf_ha=vmem((d.n_ha, count, LANES), f32),
+                buf_ha=vmem((d.n_ha, count, LANES), kind),
                 buf_img=vmem((d.n_img, count, LANES), f32),
                 send_ha=dma((d.n_ha,)), recv_ha=dma((d.n_ha,)),
                 send=dma((d.n_img,)), recv=dma((d.n_img,)),
             )
         if name in d.paired:
             return dict(
-                src=vmem((count, LANES), f32),
+                src=vmem((count, LANES), kind),
                 mid=vmem((count, LANES), f32),
                 other=vmem((count, LANES), f32),
                 buf=vmem((16, count, LANES), f32),
                 send=dma((16,)), recv=dma((16,)),
             )
         return dict(
-            src=vmem((count, LANES), f32),
-            buf=vmem((32, count, LANES), f32),
+            src=vmem((count, LANES), kind),
+            buf=vmem((32, count, LANES), kind),
             send=dma((32,)), recv=dma((32,)),
         )
 
@@ -1132,6 +1150,7 @@
         vmem((d.radix, d.gin, 3 * wd), bf16),
         vmem((d.radix, d.gin, 3 * wd), bf16),
         vmem((nh, wd, d.line), bf16),
+        vmem((16, LANES), f32),
         vmem((nb, d.wide), f32),
         vmem((nb, d.wide), f32),
         vmem((nb, d.wide), f32),
@@ -1203,7 +1222,7 @@
     def weights(step):
         half = d.cin // 2
         if step < 2:
-            gw1[step * half : (step + 1) * half, :] = jnp.transpose(wg0[step].astype(F32))
+            gw1[step * half : (step + 1) * half, :] = jnp.transpose(wg0[step]).astype(F32)
             gw3[:, step * half : (step + 1) * half] = wg2[step].astype(F32)
         elif step < 4:
             r = step - 2
@@ -1215,7 +1234,7 @@
             for tap in range(9):
                 held, first = (wg1, 0) if tap < d.split else (wg3, d.split)
                 cells = held[r, :, (tap - first) * d.gin : (tap - first + 1) * d.gin]
-                gw2[r, tap] = jnp.transpose(cells.astype(F32)) + back
+                gw2[r, tap] = jnp.transpose(cells).astype(F32) + back
         elif step == 4:
             cells = wg4[0].astype(F32)
             gwex[:, 0:wd] = cells[0 : d.inter, :]

time: 144 us -> 140 us (0.972)
  Pallas kernels: 142 us -> 138 us
    pallas_call x1, Pallas kernels: 135 us -> 131 us  [call_block(): pl.pallas_call(functools.partial(block_kernel, d), out_shape=outs, in_spe...]
where the time goes in v5:
time: 140 us
  Pallas kernels  138 us (99%)
  between operations  1.47 us (1%)
    pallas_call x1, Pallas kernels, call_block(): pl.pallas_call(functools.partial(block_kernel, d), out_shape=outs, in_spe...  131 us
    pallas_call x1, Pallas kernels, call_finish(): pl.pallas_call(functools.partial(finish_kernel, d), out_shape=[shape((d.r...  7.09 us

profile of v5, /device:TPU:0, one launch (start us, length us, event | category | flops | bytes accessed | tf_op | source)
XLA Modules:
  0.0 139.7 jit_solution(2372570032849559830)
XLA Ops:
  1.3 131.2 %block.1 = (bf16[3136,1024]{1,0:T(8,128)(2,1)}, bf16[3136,1024]{1,0:T(8,128)(2,1)S(1)}, bf16[3136,1024]{1,0:T(8,128)(2,1)S(1)}, bf16[2,256,512]{2,1,0:T(8,128)(2...) custom-call(bf16[3136,1024]{1,0:T(8,128)(2,1)} %bitcast.33, ...), custom_call_target="tpu_custom_call" | custom-call | tf_op jit(solution)/shard_map/block/pallas_call | solution.py:1188
  132.5 7.1 %finish.1 = (bf16[3136,1024]{1,0:T(8,128)(2,1)}, bf16[3136,1024]{1,0:T(8,128)(2,1)}, f32[1024,256]{1,0:T(8,128)}, f32[1,256]{1,0:T(1,128)}, f32[1,256]{1,0:T(1,1...) custom-call(bf16[3136,1024]{1,0:T(8,128)(2,1)S(1)} %get-tuple-elemen, ...), custom_call_target="tpu_custom_call" | custom-call | tf_op jit(solution)/shard_map/finish/pallas_call | solution.py:1275

commit v6 on v5

--- a/solution.py
+++ b/solution.py
@@ -116,7 +116,7 @@
     x_hbm, ct_hbm, mask_in, count_in, w1_hbm, g1, c1, w2_hbm, g2, c2, wsq, gs, cs, wex, bex, w3_hbm, g3, c3,
     dn_hbm, ost, xv, wg0, wg1, wg2, wg3, wg4, small,
     w1, w2, w3, mb, live, ctv, y1, a1p, y2, act2, slope2, mixed, dm, acc_c, acc_g, w3p, w2x, w2l, w2r,
-    mix_t, rows16, att, q2, q4, vecs, pools, v0, cols,
+    mix_t, rows16, att, q2, q4, vecs, vecs2, pools, v0, cols,
     parts, rcs, rxys, rzs, mids, vres, sums, ga_src, ga_buf, pf_src, pf_buf, fc_src, fc_buf,
     sem_w, sem_x, sem_ct, sem_dn, sem_back, ssa, rsa, ssi, rsi, ssh, rsh, ssw, rsw,
 ):
@@ -506,7 +506,7 @@
             a1p[inner_rows(t + 1, nb + u * step1, step1), :] = value.astype(BF16)
             return carry + fold(value)
 
-        return lax.fori_loop(0, line // step1, cells, carry)
+        return lax.fori_loop(0, line // step1, cells, carry, unroll=True)
 
     def edges(body, carry):
         return lax.fori_loop(0, 2, lambda t, c: body(t * (nh - 1), c), carry)
@@ -650,31 +650,35 @@
             return carry
 
         lax.fori_loop(0, line // step3, cells, 0, unroll=7)
+        at = line_rows(t)
+        for c in range(2):
+            lanes = slice(c * half, (c + 1) * half)
+            y = dot(mixed[at, :], w3[:, lanes])
+            ost[at, lanes] = y.astype(BF16)
+            vecs[:, lanes] += fold(y)
+            vecs2[:, lanes] += fold(y * y)
+        return carry
+
+    vecs[...] = jnp.zeros((8, cin), F32)
+    vecs2[...] = jnp.zeros((8, cin), F32)
+    lax.fori_loop(0, nh, mix, 0)
+    norm3 = Everywhere("s3")
+    put(norm3.at, 0, total_row(vecs[...]))
+    put(norm3.at, 8, total_row(vecs2[...]))
+    norm3.start()
+
+    def mix_products(t, carry):
         gram, sums = carry
         cells = mixed[line_rows(t), :]
         mix_t[t] = jnp.transpose(cells)
+        ct_copy(t, 0).wait()
+        ct_copy(t, 1).wait()
         return gram + dot(mix_t[t], cells), sums + fold(cells.astype(F32))
 
-    gram, totals = lax.fori_loop(0, nh, mix, (jnp.zeros((wd, wd), F32), jnp.zeros((8, wd), F32)))
+    gram, totals = lax.fori_loop(0, nh, mix_products, (jnp.zeros((wd, wd), F32), jnp.zeros((8, wd), F32)))
     mix_sum = total_row(totals)
     gram_high, gram_low = split_bf16(gram)
     acc_g[0, :, 0:cin] = dot(gram_high, w3[...]) + dot(gram_low, w3[...])
-    mix_parts = [jnp.broadcast_to(part, (16, wd)) for part in split_bf16(mix_sum)]
-    sum_last = dot(jnp.concatenate(mix_parts, axis=0), w3[...])
-    sum_last = sum_last[0:1, :] + sum_last[16:17, :]
-    norm3 = Everywhere("s3")
-    put(norm3.at, 0, sum_last)
-    put(norm3.at, 8, total_row(acc_g[0, :, 0:cin] * w3[...].astype(F32)))
-    norm3.start()
-
-    def last_product(t, carry):
-        at = line_rows(t)
-        ost[at, :] = dot(mixed[at, :], w3[...]).astype(BF16)
-        ct_copy(t, 0).wait()
-        ct_copy(t, 1).wait()
-        return carry
-
-    lax.fori_loop(0, nh, last_product, 0)
     w_step(5, 1)
     got = norm3.finish()
     mean3, scale3 = moments(get(got, 0, cin), get(got, 8, cin), wide(total, cin))
@@ -698,8 +702,8 @@
     def grad_of(t):
         return jnp.concatenate([ctv[half_rows(t, 0), :], ctv[half_rows(t, 1), :]], axis=1)
 
-    acc_c[...] = jnp.zeros((wd, cin), F32)
     vecs[...] = jnp.zeros((8, cin), F32)
+    vecs2[...] = jnp.zeros((8, cin), F32)
 
     def last(t, carry):
         for j in range(cin // blocks4):
@@ -710,7 +714,8 @@
                 at = block_rows(t, u, step4)
                 mask = wide(mb[at, :], blocks4)
                 x = xv[at, lanes] * jnp.asarray(0.5, BF16)
-                arg = ost[at, lanes].astype(F32) * a3 + (b3 + x.astype(F32))
+                y = ost[at, lanes].astype(F32)
+                arg = y * a3 + (b3 + x.astype(F32))
                 bend = jnp.tanh(arg)
                 rise = 1.0 + bend
                 value = arg * rise
@@ -721,26 +726,32 @@
                 push = ctv[there, inner] * (mask * jnp.asarray(0.5, BF16))
                 grad = push.astype(F32) * (rise + value * (1.0 - bend))
                 ctv[there, inner] = grad.astype(BF16)
-                return carry + fold(grad)
-
-            vecs[:, lanes] = lax.fori_loop(0, line // step4, cells, vecs[:, lanes])
+                sums, bends = carry
+                return sums + fold(grad), bends + fold(grad * y)
+
+            vecs[:, lanes], vecs2[:, lanes] = lax.fori_loop(
+                0, line // step4, cells, (vecs[:, lanes], vecs2[:, lanes])
+            )
         dn_copy(t, 0).start()
         dn_copy(t, 1).start()
-        acc_c[...] += dot(mix_t[t], grad_of(t))
         return carry
 
     lax.fori_loop(0, nh, last, 0)
     sum_grad = total_row(vecs[...])
     back3 = Everywhere("b3")
     put(rows16, 0, sum_grad)
-    put(rows16, 8, scale3 * (total_row(acc_c[...] * w3[...].astype(F32)) - mean3 * sum_grad))
+    put(rows16, 8, scale3 * (total_row(vecs2[...]) - mean3 * sum_grad))
     back3.at[...] = rows16[...].astype(BF16)
     back3.start()
 
     w3p[...] = (w3[...].astype(F32) * grow3).astype(BF16)
 
+    acc_c[...] = jnp.zeros((wd, cin), F32)
+
     def plain_back(t, carry):
-        dm[line_rows(t), :] = dot_nt(grad_of(t), w3p[...])
+        grad = grad_of(t)
+        dm[line_rows(t), :] = dot_nt(grad, w3p[...])
+        acc_c[...] += dot(mix_t[t], grad)
         return carry
 
     lax.fori_loop(0, nh, plain_back, 0)
@@ -785,7 +796,7 @@
                 done.append((a, b, c))
             return tuple(done)
 
-        sums5.append(lax.fori_loop(0, rows // step5, image_sums, ((zero, zero, zero),) * d.radix))
+        sums5.append(lax.fori_loop(0, rows // step5, image_sums, ((zero, zero, zero),) * d.radix, unroll=7))
     pick = lambda which: jnp.concatenate(
         [sums5[j][r][which] for r in range(d.radix) for j in range(lane_blocks)], axis=1
     )
@@ -1154,6 +1165,7 @@
         vmem((nb, d.wide), f32),
         vmem((nb, d.wide), f32),
         vmem((nb, d.wide), f32),
+        vmem((8, cin), f32),
         vmem((8, cin), f32),
         vmem((nb, wd), f32),
         vmem((2, 8, cin // 2), f32),

time: 140 us -> 138 us (0.986)
  Pallas kernels: 138 us -> 136 us
    pallas_call x1, Pallas kernels: 131 us -> 129 us  [call_block(): pl.pallas_call(functools.partial(block_kernel, d), out_shape=outs, in_spe...]
where the time goes in v6:
time: 138 us; the launch traced here: 137 us
  Pallas kernels  136 us (99%)
  between operations  1.47 us (1%)
    pallas_call x1, Pallas kernels, call_block(): pl.pallas_call(functools.partial(block_kernel, d), out_shape=outs, in_spe...  129 us
    pallas_call x1, Pallas kernels, call_finish(): pl.pallas_call(functools.partial(finish_kernel, d), out_shape=[shape((d.r...  7.09 us

profile of v6, /device:TPU:0, one launch (start us, length us, event | category | flops | bytes accessed | tf_op | source)
XLA Modules:
  0.0 137.4 jit_solution(6482557307701054269)
XLA Ops:
  1.3 128.9 %block.1 = (bf16[3136,1024]{1,0:T(8,128)(2,1)}, bf16[3136,1024]{1,0:T(8,128)(2,1)S(1)}, bf16[3136,1024]{1,0:T(8,128)(2,1)S(1)}, bf16[2,256,512]{2,1,0:T(8,128)(2...) custom-call(bf16[3136,1024]{1,0:T(8,128)(2,1)} %bitcast.33, ...), custom_call_target="tpu_custom_call" | custom-call | tf_op jit(solution)/shard_map/block/pallas_call | solution.py:1200
  130.2 7.1 %finish.1 = (bf16[3136,1024]{1,0:T(8,128)(2,1)}, bf16[3136,1024]{1,0:T(8,128)(2,1)}, f32[1024,256]{1,0:T(8,128)}, f32[1,256]{1,0:T(1,128)}, f32[1,256]{1,0:T(1,1...) custom-call(bf16[3136,1024]{1,0:T(8,128)(2,1)S(1)} %get-tuple-elemen, ...), custom_call_target="tpu_custom_call" | custom-call | tf_op jit(solution)/shard_map/finish/pallas_call | solution.py:1287

commit v7 on v6

--- a/solution.py
+++ b/solution.py
@@ -661,7 +661,7 @@
 
     vecs[...] = jnp.zeros((8, cin), F32)
     vecs2[...] = jnp.zeros((8, cin), F32)
-    lax.fori_loop(0, nh, mix, 0)
+    lax.fori_loop(0, nh, mix, 0, unroll=True)
     norm3 = Everywhere("s3")
     put(norm3.at, 0, total_row(vecs[...]))
     put(norm3.at, 8, total_row(vecs2[...]))
@@ -775,7 +775,7 @@
         dm[at, :] = dm[at, :] - dot(mixed[at, :], fix) - mask_of(at, wd) * shift
         return carry
 
-    lax.fori_loop(0, nh, back_mix, 0)
+    lax.fori_loop(0, nh, back_mix, 0, unroll=True)
 
     step5 = 4 * nb
     sums5 = []
@@ -924,7 +924,7 @@
             acc_g[r] += dot(grad, taps(t, r))
         return carry
 
-    lax.fori_loop(0, nh, weights_group, 0)
+    lax.fori_loop(0, nh, weights_group, 0, unroll=True)
 
     def send_group(s, first, last):
         lanes = (last - first) * gin
@@ -1005,7 +1005,7 @@
         acc_c[...] += dot_tn(mixed[at, :], xv[at, :])
         return carry
 
-    lax.fori_loop(0, nh, first_weights, 0)
+    lax.fori_loop(0, nh, first_weights, 0, unroll=True)
     if d.inside:
         for c in range(2):
             parts[0][c] = acc_c[:, c * half : (c + 1) * half].astype(BF16)

time: 138 us -> 134 us (0.971)
  Pallas kernels: 136 us -> 133 us
    pallas_call x1, Pallas kernels: 129 us -> 126 us  [call_block(): pl.pallas_call(functools.partial(block_kernel, d), out_shape=outs, in_spe...]
where the time goes in v7:
time: 134 us
  Pallas kernels  133 us (99%)
  between operations  1.49 us (1%)
    pallas_call x1, Pallas kernels, call_block(): pl.pallas_call(functools.partial(block_kernel, d), out_shape=outs, in_spe...  126 us
    pallas_call x1, Pallas kernels, call_finish(): pl.pallas_call(functools.partial(finish_kernel, d), out_shape=[shape((d.r...  7.09 us

profile of v7, /device:TPU:0, one launch (start us, length us, event | category | flops | bytes accessed | tf_op | source)
XLA Modules:
  0.0 134.1 jit_solution(8052319690525287937)
XLA Ops:
  1.3 125.6 %block.1 = (bf16[3136,1024]{1,0:T(8,128)(2,1)}, bf16[3136,1024]{1,0:T(8,128)(2,1)S(1)}, bf16[3136,1024]{1,0:T(8,128)(2,1)S(1)}, bf16[2,256,512]{2,1,0:T(8,128)(2...) custom-call(bf16[3136,1024]{1,0:T(8,128)(2,1)} %bitcast.33, ...), custom_call_target="tpu_custom_call" | custom-call | tf_op jit(solution)/shard_map/block/pallas_call | solution.py:1200
  126.9 7.1 %finish.1 = (bf16[3136,1024]{1,0:T(8,128)(2,1)}, bf16[3136,1024]{1,0:T(8,128)(2,1)}, f32[1024,256]{1,0:T(8,128)}, f32[1,256]{1,0:T(1,128)}, f32[1,256]{1,0:T(1,1...) custom-call(bf16[3136,1024]{1,0:T(8,128)(2,1)S(1)} %get-tuple-elemen, ...), custom_call_target="tpu_custom_call" | custom-call | tf_op jit(solution)/shard_map/finish/pallas_call | solution.py:1287

commit v8 on v7

--- a/solution.py
+++ b/solution.py
@@ -542,7 +542,7 @@
         return tuple(done)
 
     zeros = jnp.zeros((8, wd), F32)
-    sums2 = lax.fori_loop(1, nh - 1, group, ((zeros, zeros),) * d.radix)
+    sums2 = lax.fori_loop(1, nh - 1, group, ((zeros, zeros),) * d.radix, unroll=True)
     halo1_recv()
     sums2 = edges(group, sums2)
     norm2 = Everywhere("s2")
@@ -881,7 +881,16 @@
     put(small.at[0], 20, bias2)
     put(small.at[0], 24, gain2)
     slant2 = grow2 * scale2 * gain2 / wide(total, wide2)
-    level2 = grow2 * bias2 / wide(total, wide2) - mean2 * slant2
+    lift2 = grow2 * bias2 / wide(total, wide2)
+    level2 = lift2 - mean2 * slant2
+    own_pixels = wide(total_row(pixels), wide2)
+    own_sum = jnp.concatenate([total_row(s) for s, _ in sums2], axis=1)
+    sum_dy2 = grow2 * sum_grad - lift2 * own_pixels - slant2 * (own_sum - mean2 * own_pixels)
+    misc = Everywhere("misc")
+    put(misc.at, 0, sum_dy2)
+    put(misc.at, 4, grad_bex)
+    misc.start()
+    sum_dy2 = [sum_dy2[:, r * wd : (r + 1) * wd] for r in range(d.radix)]
 
     step6 = 2 * nb
 
@@ -892,7 +901,6 @@
             again = step6 // nb
             grad = dm[at, :]
             mask = mask_of(at, wd)
-            sums = []
             for r in range(d.radix):
                 own = slice(r * wd, (r + 1) * wd)
                 grow = jnp.concatenate([att[:, own]] * again, axis=0)
@@ -900,21 +908,14 @@
                 push = (grow * grad + lift) * slope2[at, own].astype(F32)
                 pull = mask * (level2[:, own] + slant2[:, own] * y2[at, own].astype(F32))
                 dyp[to, own] = (push - pull).astype(BF16)
-                sums.append(carry[r] + fold(push - pull))
-            return tuple(sums)
+            return carry
 
         return lax.fori_loop(0, line // step6, cells, carry, unroll=7)
 
-    zeros = jnp.zeros((8, wd), F32)
-    sums2 = edges(back_group, (zeros,) * d.radix)
+    edges(back_group, 0)
     halo2_start, halo2_recv, halo2_sent = halo(dyp, 1)
     halo2_start()
-    sums2 = lax.fori_loop(1, nh - 1, back_group, sums2)
-    sum_dy2 = [total_row(s) for s in sums2]
-    misc = Everywhere("misc")
-    put(misc.at, 0, jnp.concatenate(sum_dy2, axis=1))
-    put(misc.at, 4, grad_bex)
-    misc.start()
+    lax.fori_loop(1, nh - 1, back_group, 0)
     w_step(2, 2)
     w_step(4, 1)
 

time: 134 us -> 133 us (level)
  no operation moved by 1% of the time
where the time goes in v8:
time: 133 us
  Pallas kernels  132 us (99%)
  between operations  1.49 us (1%)
    pallas_call x1, Pallas kernels, call_block(): pl.pallas_call(functools.partial(block_kernel, d), out_shape=outs, in_spe...  125 us
    pallas_call x1, Pallas kernels, call_finish(): pl.pallas_call(functools.partial(finish_kernel, d), out_shape=[shape((d.r...  7.09 us

profile of v8, /device:TPU:0, one launch (start us, length us, event | category | flops | bytes accessed | tf_op | source)
XLA Modules:
  0.0 133.3 jit_solution(4411522794080860643)
XLA Ops:
  1.3 124.7 %block.1 = (bf16[3136,1024]{1,0:T(8,128)(2,1)}, bf16[3136,1024]{1,0:T(8,128)(2,1)S(1)}, bf16[3136,1024]{1,0:T(8,128)(2,1)S(1)}, bf16[2,256,512]{2,1,0:T(8,128)(2...) custom-call(bf16[3136,1024]{1,0:T(8,128)(2,1)} %bitcast.33, ...), custom_call_target="tpu_custom_call" | custom-call | tf_op jit(solution)/shard_map/block/pallas_call | solution.py:1201
  126.0 7.1 %finish.1 = (bf16[3136,1024]{1,0:T(8,128)(2,1)}, bf16[3136,1024]{1,0:T(8,128)(2,1)}, f32[1024,256]{1,0:T(8,128)}, f32[1,256]{1,0:T(1,128)}, f32[1,256]{1,0:T(1,1...) custom-call(bf16[3136,1024]{1,0:T(8,128)(2,1)S(1)} %get-tuple-elemen, ...), custom_call_target="tpu_custom_call" | custom-call | tf_op jit(solution)/shard_map/finish/pallas_call | solution.py:1288
